TPU v7x, 256 devices: a whole 4x4x8 slice. The times are simulated.
256 devices in a mesh: expert: 64 (over x, z_lo, y, core), dp: 4 (over z_hi).
Axes of the slice: x: 4, y: 4, z: 8 (z_hi: 4, z_lo: 2; z = z_hi * 2 + z_lo), core: 2. Of those that a mesh axis runs over, the one named last changes fastest.
Arguments:
- tokens: bfloat16 [32768, 3584], P(('expert', 'dp')), may hold values from -6 to 6
- cotangent: bfloat16 [32768, 3584], P(('expert', 'dp')), may hold values from -0.29882812 to 0.29882812
- routes: int32 [32768, 2], P(('expert', 'dp')), may hold values from 0 to 63, as said below
- gates: float32 [32768, 2], P(('expert', 'dp')), may hold values from 0.1 to 1
- gate_weight: bfloat16 [64, 3584, 1024], P('expert'), may hold values from -0.09375 to 0.09375
Outputs:
- grad_down: float32 [64, 1024, 3584], P('expert', 'dp')
Inputs may be any that keep to these rules, and one draw needn't show every extreme that they name: `routes`: one expert, the same for all devices, is named exactly 12 times in the rows of each device; every other expert is named at most 6 times in the rows of one device, and some expert exactly 6 times; the 2 experts of a row differ.
All inputs are finite; a program needn't handle non-finite values.
Results may differ from a plain program's by a relative error of at most 0.004.
Values may be sent and summed in bfloat16 or wider, within the bound.
No kernel may reach another device: no remote copies, remote signals or barrier semaphores. Data moves between devices by JAX's collectives and lax.ppermute only.
A program may use at most 128 MiB of HBM per device.

v0:
```python
import jax
import jax.numpy as jnp
from jax import lax
from jax.sharding import PartitionSpec as P


def slot_sources(flat_experts, route_rank, keep, experts, depth):
    route_total = flat_experts.shape[0]
    target = jnp.where(keep, flat_experts * depth + route_rank, experts * depth)
    filler = jnp.full((experts * depth,), route_total, jnp.int32)
    return filler.at[target].set(jnp.arange(route_total, dtype=jnp.int32), mode="drop")


def expert_terms(send_tokens, send_scaled, weight):
    token_rows = lax.all_to_all(send_tokens, "expert", split_axis=0, concat_axis=0, tiled=True)
    scaled_rows = lax.all_to_all(send_scaled, "expert", split_axis=0, concat_axis=0, tiled=True)
    activate_hidden = jax.nn.silu(
        jnp.einsum("esd,dh->esh", token_rows, weight, preferred_element_type=jnp.float32)
    )
    hidden = activate_hidden.astype(jnp.bfloat16)
    arrived = scaled_rows
    hidden = hidden.reshape(-1, hidden.shape[-1])
    arrived = arrived.reshape(-1, arrived.shape[-1])
    return lax.psum_scatter(
        lax.dot_general(
            hidden, arrived, (((0,), (0,)), ((), ())), preferred_element_type=jnp.float32
        ),
        "dp",
        scatter_dimension=0,
        tiled=True,
    )


def local(tokens, cotangent, routes, gates, gate_weight):
    tok_rows, model_width = tokens.shape
    top_k = routes.shape[1]
    experts = lax.axis_size("expert")
    weight = gate_weight[0]
    flat_experts = routes.reshape(-1)
    route_total = flat_experts.shape[0]
    scaled = (gates[:, :, None] * cotangent[:, None, :].astype(jnp.float32)).astype(jnp.bfloat16)
    scaled = scaled.reshape(route_total, model_width)
    scaled_padded = jnp.concatenate([scaled, jnp.zeros((1, model_width), jnp.bfloat16)], 0)
    tokens_padded = jnp.concatenate([tokens, jnp.zeros((1, model_width), tokens.dtype)], 0)
    one_hot = (flat_experts[:, None] == jnp.arange(experts, dtype=jnp.int32)[None, :]).astype(
        jnp.int32
    )
    route_rank = jnp.sum((jnp.cumsum(one_hot, 0) - one_hot) * one_hot, 1)
    cold_slots = 3 * tok_rows * top_k // (2 * experts)
    crowded = 2 * cold_slots
    keep_all = flat_experts >= 0
    slot_source = slot_sources(flat_experts, route_rank, keep_all, experts, crowded)
    owner_token = jnp.where(slot_source < route_total, slot_source // top_k, tok_rows)
    send_tokens = tokens_padded[owner_token]
    send_scaled = scaled_padded[slot_source]
    result = expert_terms(
        send_tokens.reshape(experts, crowded, model_width),
        send_scaled.reshape(experts, crowded, model_width),
        weight,
    )
    return result[None]


def solution(mesh):
    placed = (
        P(("expert", "dp"), None),
        P(("expert", "dp"), None),
        P(("expert", "dp"), None),
        P(("expert", "dp"), None),
        P("expert", None, None),
    )
    return jax.shard_map(
        local, mesh=mesh, in_specs=placed, out_specs=P("expert", "dp", None), check_vma=False
    )
```

profile of v0, /device:TPU:64, one launch (start us, length us, event | category | flops | bytes accessed | tf_op | source)
XLA Modules:
  0.0 525.7 jit_solution(9089827678609480189)
XLA Ops:
  6.5 0.7 broadcast_compare_fusion
  7.2 0.7 broadcast_multiply_fusion
  7.9 0.8 copy.16
  8.7 0.1 eq.29
  8.8 0.1 eq.25
  9.0 0.1 copy.14
  9.1 0.2 ge.14
  9.3 0.1 copy.15
  9.4 0.1 mul.43
  9.5 0.6 reduce-window.6
  10.1 0.2 slice_reduce_fusion
  10.4 0.1 fusion.15
  10.5 1.4 scatter_custom_fusion
  11.9 0.8 copy.20
  12.7 0.1 mul.46
  12.9 4.0 mul.48
  16.8 5.6 %mul.49 = f32[256,3584]{1,0:T(8,128)} reshape(f32[128,2,3584]{2,1,0:T(2,128)} %mul.48) | data formatting | bytes 7340032 | tf_op jit(solution)/shard_map/mul | solution.py:41
  22.5 2.4 multiply_convert_fusion
  24.9 0.1 concatenate.7
  25.0 5.5 %gather_fusion.1 = bf16[768,3584]{1,0:T(8,128)(2,1)} fusion(bf16[257,3584]{1,0:T(8,128)(2,1)S(1)} %concatenate.7, s32[1024]{0:T(1024)S(1)} %get-tuple-element.7), kind=kCustom, calls=%fused_computation.1 | custom fusion | bytes 11013120 | tf_op jit(solution)/shard_map/gather | solution.py:55
  30.5 9.3 %reshape.77 = bf16[64,12,3584]{2,1,0:T(8,128)(2,1)} reshape(bf16[768,3584]{1,0:T(8,128)(2,1)} %gather_fusion.1) | data formatting | bytes 11010048 | tf_op jit(solution)/shard_map/reshape | solution.py:58
  39.7 0.0 copy-start
  39.7 9.7 %all-to-all-start.1 = ((bf16[64,12,3584]{2,1,0:T(8,128)(2,1)}), bf16[64,12,3584]{2,1,0:T(8,128)(2,1)}, u32[]{:S(2)}, u32[]{:S(2)}) async-start(bf16[64,12,3584]{2,1,0:T(8,128)(2,1)} %reshape.77), calls=%async_computation.1 | async-start | bytes 14680064 | tf_op jit(solution)/shard_map/all_to_all | solution.py:16
  49.4 0.0 reduce-scatter.2.cloned.1.call-start
  49.5 0.0 copy-done
  49.5 0.1 concatenate.6
  49.5 5.5 %gather_fusion = bf16[768,3584]{1,0:T(8,128)(2,1)} fusion(bf16[129,3584]{1,0:T(8,128)(2,1)S(1)} %concatenate.6, s32[1024]{0:T(1024)S(1)} %get-tuple-element.8), kind=kCustom, calls=%fused_computation | custom fusion | bytes 11013120 | tf_op jit(solution)/shard_map/gather | solution.py:54
  55.0 9.3 %reshape.76 = bf16[64,12,3584]{2,1,0:T(8,128)(2,1)} reshape(bf16[768,3584]{1,0:T(8,128)(2,1)} %gather_fusion) | data formatting | bytes 11010048 | tf_op jit(solution)/shard_map/reshape | solution.py:57
  64.3 79.6 %all-to-all-done.1 = bf16[64,12,3584]{2,1,0:T(8,128)(2,1)} async-done(((bf16[64,12,3584]{2,1,0:T(8,128)(2,1)}), bf16[64,12,3584]{2,1,0:T(8,128)(2,1)}, u32[]{:S(2)}, u32[]{:S(2)}) %all-to-all-start.1) | async-done | bytes 5505056 | tf_op jit(solution)/shard_map/all_to_all | solution.py:16
  143.9 91.3 %all_to_all.10 = bf16[64,12,3584]{2,1,0:T(8,128)(2,1)} all-to-all(bf16[64,12,3584]{2,1,0:T(8,128)(2,1)} %reshape.76), channel_id=1, replica_groups=mesh['expert'=64,'dp'=4] {'expert'}, dimensions={0} | all-to-all | bytes 11010048 | tf_op jit(solution)/shard_map/all_to_all | solution.py:15
  235.2 30.6 %convolution_bitcast_fusion = f32[1024,3584]{1,0:T(8,128)} fusion(bf16[64,12,3584]{2,1,0:T(8,128)(2,1)} %all-to-all-done.1, bf16[1,3584,1024]{2,1,0:T(8,128)(2,1)} %param.9, bf16[64,12,3584]{2,1,0:T(8,128)(2,1)} %all_to_all.10), kind=kOutput, calls=%fused_computation.3 | convolution fusion | flops 11278221312 | bytes 33030144 | tf_op jit(solution)/shard_map/dot_general | solution.py:25
  265.8 0.0 reduce-scatter.2.cloned.1.call-update
  265.8 253.0 %reduce-scatter.2.cloned.1.call-done = f32[256,3584]{1,0:T(8,128)} async-done(((f32[1024,3584]{1,0:T(8,128)}), f32[256,3584]{1,0:T(8,128)}) %reduce-scatter.2.cloned.1.call-update) | async-done | bytes 3670032 | tf_op jit(solution)/shard_map/reduce_scatter | solution.py:24
  (7 shorter events, 0.1 us)
Async XLA Ops:
  39.7 9.7 %copy-start = (bf16[128,3584]{1,0:T(8,128)(2,1)S(1)}, bf16[128,3584]{1,0:T(8,128)(2,1)}, u32[]{:S(2)}) copy-start(bf16[128,3584]{1,0:T(8,128)(2,1)} %param.5) | copy-start | bytes 2752516
  39.7 104.2 %all-to-all-start.1 = ((bf16[64,12,3584]{2,1,0:T(8,128)(2,1)}), bf16[64,12,3584]{2,1,0:T(8,128)(2,1)}, u32[]{:S(2)}, u32[]{:S(2)}) async-start(bf16[64,12,3584]{2,1,0:T(8,128)(2,1)} %reshape.77), calls=%async_computation.1 | async-start | bytes 14680064 | tf_op jit(solution)/shard_map/all_to_all | solution.py:16
  49.4 469.4 %reduce-scatter.2.cloned.1.call-start = ((), (), s32[]{:S(2)}) async-start(), calls=%async_computation.3 | async-start | bytes 18350080 | tf_op jit(solution)/shard_map/reduce_scatter | solution.py:24
Sparse Core Ops, SparseCore 0:
  265.9 252.8 reduce-scatter.1
where the time goes:
time: 529 us; the launch traced here: 526 us
  waiting for transfers between devices  333 us (63%)
  blocking collectives  91.3 us (17%)
  local copies, waits for them, and re-layouts  43.4 us (8%)
  matrix products  30.6 us (6%)
  between operations  13.5 us (3%)
  starting transfers between devices  9.7 us (2%)
    reduce_scatter x1, waiting for transfers between devices, expert_terms(): lax.psum_scatter(lax.dot_general(hidden, arrived, (((0,), (0,)), ((), ())...  253 us
    all_to_all x1, blocking collectives, expert_terms(): lax.all_to_all(send_tokens, 'expert', split_axis=0, concat_axis=0, tiled=...  91.3 us
    all_to_all x1, waiting for transfers between devices, expert_terms(): lax.all_to_all(send_scaled, 'expert', split_axis=0, concat_axis=0, tiled=...  79.6 us
    dot_general x1, matrix products, expert_terms(): lax.dot_general(hidden, arrived, (((0,), (0,)), ((), ())), preferred_elem...  30.6 us
  transfers between devices with their start and end apart: 2, of which 2 were waited for; matrix products, arithmetic and copies ran while one was open for 3% of the time, Pallas kernels for 0%

commit v1 on v0

v1 whole, which is shorter than its diff:
```python
import functools

import jax
import jax.numpy as jnp
from jax import lax
from jax.experimental import pallas as pl
from jax.experimental.pallas import tpu as pltpu
from jax.sharding import PartitionSpec as P

CAP = 6
F32 = jnp.float32
BF16 = jnp.bfloat16
VMEM_LIMIT = 56 * 1024 * 1024


def iota(shape, dim):
    return lax.broadcasted_iota(jnp.int32, shape, dim)


def floordiv(a, n):
    return jnp.floor((a.astype(F32) + 0.5) * (1.0 / n)).astype(jnp.int32)


def slot_keys(route, experts):
    tok = route.shape[1]
    column = route.T
    r0, r1 = route[0:1], route[1:2]
    c0, c1 = column[:, 0:1], column[:, 1:2]
    before = iota((tok, tok), 0) < iota((tok, tok), 1)

    def count(mask):
        return jnp.sum(jnp.where(mask, 1.0, 0.0), 0, keepdims=True)

    rank0 = count((c0 == r0) & before)
    rank1 = count(c0 == r1) + count((c1 == r1) & before)

    def key(r, rank):
        return jnp.where(rank < CAP, r * CAP + rank, experts * CAP + rank - CAP).astype(jnp.int32)

    return key(r0, rank0), key(r1, rank1)


def pack_tokens_kernel(experts, route_ref, head_ref, tail_ref, out_ref):
    k = pl.program_id(0)
    key0, key1 = slot_keys(route_ref[...], experts)
    rows = out_ref.shape[0]
    row = iota((rows, 1), 0)
    e, j = row >> 4, row & 15
    base = jnp.where(j < 8, e * CAP, experts * CAP)
    jj = j & 7
    head_slot = jnp.where(jj < CAP, base + jj, -1)
    tail_slot = jnp.where(jj >= CAP, base + 2 * k + jj - CAP, -1)

    def pick(slot):
        return jnp.where((slot == key0) | (slot == key1), 1.0, 0.0).astype(BF16)

    left = jnp.concatenate([pick(head_slot), pick(tail_slot)], 1)
    right = jnp.concatenate([head_ref[...], tail_ref[...]], 0)
    out_ref[...] = jnp.dot(left, right, preferred_element_type=F32).astype(BF16)


def pack_tokens(route, tokens, experts):
    tok, width = tokens.shape
    part = width // 4
    rows = experts * 16
    return pl.pallas_call(
        functools.partial(pack_tokens_kernel, experts),
        grid=(3,),
        in_specs=[
            pl.BlockSpec(route.shape, lambda k: (0, 0)),
            pl.BlockSpec((tok, part), lambda k: (0, k)),
            pl.BlockSpec((tok, part), lambda k: (0, 3)),
        ],
        out_specs=pl.BlockSpec((rows, part), lambda k: (0, k)),
        out_shape=jax.ShapeDtypeStruct((rows, 3 * part), BF16),
        compiler_params=pltpu.CompilerParams(vmem_limit_bytes=VMEM_LIMIT),
        name="pack_tokens",
    )(route, tokens, tokens)


def pack_scaled_kernel(experts, dests, raw_ref, out_ref):
    planes, _, part = raw_ref.shape
    tok = 128
    span = planes * CAP
    rows = dests * 2 * span
    row = iota((rows, 1), 0)
    e = floordiv(row, 2 * span)
    j = row - e * (2 * span)
    e = e + pl.program_id(0) * dests
    extra = j >= span
    j = jnp.where(extra, j - span, j)
    plane = floordiv(j, CAP)
    s = j - plane * CAP
    slot = jnp.where(extra, experts * CAP + s, e * CAP + s)
    lefts, rights = [], []
    gate = jnp.zeros((rows, 1), F32)
    for p in range(planes):
        meta = raw_ref[p, tok : tok + 16, 0:tok].astype(F32)
        key0, key1 = slot_keys(meta[0:8], experts)
        gate0 = (meta[2:3] + meta[3:4]) + meta[4:5]
        gate1 = (meta[5:6] + meta[6:7]) + meta[7:8]
        mine = jnp.where(plane == p, slot, -1)
        hit0, hit1 = mine == key0, mine == key1
        both = jnp.where(hit0, gate0, 0.0) + jnp.where(hit1, gate1, 0.0)
        gate = gate + jnp.sum(both, 1, keepdims=True)
        lefts.append(jnp.where(hit0 | hit1, 1.0, 0.0).astype(BF16))
        rights.append(raw_ref[p, 0:tok, :])
    left, right = jnp.concatenate(lefts, 1), jnp.concatenate(rights, 0)
    rows_out = jnp.dot(left, right, preferred_element_type=F32)
    out_ref[...] = (gate * rows_out).astype(BF16)


def pack_scaled(raw, experts):
    planes, _, part = raw.shape
    dests = 8
    rows = dests * 2 * planes * CAP
    return pl.pallas_call(
        functools.partial(pack_scaled_kernel, experts, dests),
        grid=(experts // dests,),
        in_specs=[pl.BlockSpec(raw.shape, lambda g: (0, 0, 0))],
        out_specs=pl.BlockSpec((rows, part), lambda g: (g, 0)),
        out_shape=jax.ShapeDtypeStruct((experts * 2 * planes * CAP, part), BF16),
        compiler_params=pltpu.CompilerParams(vmem_limit_bytes=VMEM_LIMIT),
        name="pack_scaled",
    )(raw)


def hidden_kernel(hot_ref, x_ref, w_ref, main_ref, extra_ref, rows_ref):
    sources, _, _, head = x_ref.shape
    part = head // 3
    half = sources // 2
    is_hot = hot_ref[0] > 0
    count = sources * CAP

    def unfold(which):
        r = iota((half * CAP, half * 8), 0)
        c = iota((half * CAP, half * 8), 1)
        src = floordiv(r, CAP)
        s = r - src * CAP

        def pick(mask):
            return jnp.where(mask, 1.0, 0.0).astype(BF16)

        for h in range(2):
            x = x_ref[h * half : (h + 1) * half, which].reshape(half * 8, head)
            rows = pl.ds(which * count + h * half * CAP, half * CAP)
            rows_ref[rows, 0:head] = jnp.dot(
                pick(c == src * 8 + s), x, preferred_element_type=F32
            ).astype(BF16)
            tail = jnp.zeros((half * CAP, part), F32)
            for k in range(3):
                mask = (c == src * 8 + CAP + s - 2 * k) & (s >= 2 * k) & (s < 2 * k + 2)
                tail = tail + jnp.dot(
                    pick(mask), x[:, k * part : (k + 1) * part], preferred_element_type=F32
                )
            rows_ref[rows, head:] = tail.astype(BF16)

    @pl.when(pl.program_id(0) == 0)
    def _():
        unfold(0)

        @pl.when(is_hot)
        def _():
            unfold(1)

    def hidden(first):
        v = jnp.dot(rows_ref[first : first + count, :], w_ref[...], preferred_element_type=F32)
        return (v / (1.0 + jnp.exp(-v))).astype(BF16)

    main_ref[...] = hidden(0)

    @pl.when(is_hot)
    def _():
        extra_ref[...] = hidden(count)

    @pl.when(jnp.logical_not(is_hot))
    def _():
        extra_ref[...] = jnp.zeros_like(extra_ref)


def hidden_of(hot, x, weight):
    sources, _, _, head = x.shape
    width, hid = weight.shape
    count = sources * CAP
    block = 256
    return pl.pallas_call(
        hidden_kernel,
        grid=(hid // block,),
        in_specs=[
            pl.BlockSpec(memory_space=pltpu.SMEM),
            pl.BlockSpec(x.shape, lambda n: (0, 0, 0, 0)),
            pl.BlockSpec((width, block), lambda n: (0, n)),
        ],
        out_specs=[pl.BlockSpec((count, block), lambda n: (0, n))] * 2,
        out_shape=[jax.ShapeDtypeStruct((count, hid), BF16)] * 2,
        scratch_shapes=[pltpu.VMEM((2 * count, width), BF16)],
        compiler_params=pltpu.CompilerParams(vmem_limit_bytes=VMEM_LIMIT),
        name="hidden_of",
    )(hot, x, weight)


def grad_kernel(group, hot_ref, main_ref, extra_ref, s_ref, out_ref, acc_ref):
    planes, _, hid = main_ref.shape
    part = s_ref.shape[-1]
    g = pl.program_id(0)
    n = group * CAP
    rows = planes * n

    o, i = iota((rows, rows), 0), iota((rows, rows), 1)
    plane = floordiv(o, n)
    rest = o - plane * n
    src = floordiv(rest, CAP)
    perm = jnp.where(i == src * planes * CAP + plane * CAP + rest - src * CAP, 1.0, 0.0).astype(BF16)

    def term(h_ref, which):
        s = s_ref[:, which].reshape(rows, part)
        s = jnp.dot(perm, s, preferred_element_type=F32).astype(BF16)
        h = h_ref[...].reshape(rows, hid)
        return lax.dot_general(h, s, (((0,), (0,)), ((), ())), preferred_element_type=F32)

    @pl.when(g == 0)
    def _():
        acc_ref[...] = term(main_ref, 0)

    @pl.when(g > 0)
    def _():
        acc_ref[...] += term(main_ref, 0)

    @pl.when(hot_ref[0] > 0)
    def _():
        acc_ref[...] += term(extra_ref, 1)

    @pl.when(g == pl.num_programs(0) - 1)
    def _():
        out_ref[...] = acc_ref[...].astype(out_ref.dtype)


def grad_of(hot, main, extra, s):
    planes, count, hid = main.shape
    sources, _, span, part = s.shape
    group = 16
    h_spec = pl.BlockSpec((planes, group * CAP, hid), lambda g: (0, g, 0))
    return pl.pallas_call(
        functools.partial(grad_kernel, group),
        grid=(sources // group,),
        in_specs=[
            pl.BlockSpec(memory_space=pltpu.SMEM),
            h_spec,
            h_spec,
            pl.BlockSpec((group, 2, span, part), lambda g: (g, 0, 0, 0)),
        ],
        out_specs=pl.BlockSpec((hid, part), lambda g: (0, 0)),
        out_shape=jax.ShapeDtypeStruct((hid, part), BF16),
        scratch_shapes=[pltpu.VMEM((hid, part), F32)],
        compiler_params=pltpu.CompilerParams(vmem_limit_bytes=VMEM_LIMIT),
        name="grad_of",
    )(hot, main, extra, s)


def bf16_parts(x):
    high = lax.reduce_precision(x, 8, 7)
    mid = lax.reduce_precision(x - high, 8, 7)
    return [high, mid, x - high - mid]


def gather_planes(x):
    planes = lax.axis_size("dp")
    me = lax.axis_index("dp")
    got = [x] + [
        lax.ppermute(x, "dp", [((i + d) % planes, i) for i in range(planes)]) for d in range(1, planes)
    ]
    stacked = jnp.stack(got)
    return jnp.roll(stacked, me, axis=0)


def local(tokens, cotangent, routes, gates, gate_weight):
    tok, width = tokens.shape
    experts = lax.axis_size("expert")
    planes = lax.axis_size("dp")
    part = width // planes

    route_rows = routes.T.astype(F32)
    gate_rows = gates.T
    meta = jnp.concatenate(
        [route_rows, jnp.stack(bf16_parts(gate_rows[0])), jnp.stack(bf16_parts(gate_rows[1]))], 0
    )
    counts = jnp.sum(
        (routes.reshape(-1)[:, None] == jnp.arange(experts, dtype=jnp.int32)[None, :]).astype(F32), 0
    )
    mine = lax.axis_index("expert")
    hot = (jnp.sum(jnp.where(jnp.arange(experts) == mine, counts, 0.0)) > CAP + 0.5).astype(jnp.int32)
    hot = hot.reshape(1)

    sent = pack_tokens(meta, tokens, experts)
    sent = sent.reshape(experts, 16, 3 * part)
    arrived = lax.all_to_all(sent, "expert", 0, 0, tiled=True)

    meta_block = jnp.pad(meta.astype(BF16), ((0, 8), (0, part - tok)))
    raw = cotangent.reshape(tok, planes, part).transpose(1, 0, 2)
    raw = jnp.concatenate([raw, jnp.broadcast_to(meta_block, (planes, 16, part))], 1)
    raw = lax.all_to_all(raw, "dp", 0, 0, tiled=True)

    scaled = pack_scaled(raw, experts).reshape(experts, 2 * planes * CAP, part)
    scaled = lax.all_to_all(scaled, "expert", 0, 0, tiled=True)

    main, extra = hidden_of(hot, arrived.reshape(experts, 2, 8, 3 * part), gate_weight[0])
    main = lax.all_gather(main, "dp")
    extra = lax.all_gather(extra, "dp")

    grad = grad_of(hot, main, extra, scaled.reshape(experts, 2, planes * CAP, part))
    hid = grad.shape[0] // planes
    grad = lax.all_to_all(grad.reshape(planes, hid, part), "dp", 0, 0, tiled=True)
    return grad.transpose(1, 0, 2).reshape(1, hid, width).astype(F32)


def solution(mesh):
    placed = (
        P(("expert", "dp"), None),
        P(("expert", "dp"), None),
        P(("expert", "dp"), None),
        P(("expert", "dp"), None),
        P("expert", None, None),
    )
    return jax.shard_map(
        local, mesh=mesh, in_specs=placed, out_specs=P("expert", "dp", None), check_vma=False
    )
```

time: 529 us -> 383 us (0.72)
  waiting for transfers between devices: 333 us -> 241 us
  blocking collectives: 91.3 us -> 47.6 us
  Pallas kernels: 0 us -> 37 us
  matrix products: 30.6 us -> 0 us
  local copies, waits for them, and re-layouts: 43.4 us -> 12.9 us
  starting transfers between devices: 9.7 us -> 24.6 us
    reduce_scatter x1 -> x0, waiting for transfers between devices: 253 us -> none  [expert_terms(): lax.psum_scatter(lax.dot_general(hidden, arrived, (((0,), (0,)), ((), ())...]
    all_to_all x1 -> x3, waiting for transfers between devices: 79.6 us -> 180 us  [the longest x1 103 us: local(): scaled = lax.all_to_all(scaled, 'expert', 0, 0, tiled=True)]
    all_gather x0 -> x2, waiting for transfers between devices: none -> 60.1 us  [the longest x1 60.1 us: local(): extra = lax.all_gather(extra, 'dp')]
    all_to_all x1, blocking collectives: 91.3 us -> 47.6 us  [local(): lax.all_to_all(grad.reshape(planes, hid, part), 'dp', 0, 0, tiled=True)]
    pallas_call x0 -> x4, Pallas kernels: none -> 37 us  [the longest x1 10.8 us: pack_scaled(): pl.pallas_call(functools.partial(pack_scaled_kernel, experts, dests), gri...]
    dot_general x1 -> x0, matrix products: 30.6 us -> none  [expert_terms(): lax.dot_general(hidden, arrived, (((0,), (0,)), ((), ())), preferred_elem...]
    reshape x2 -> x1, local copies, waits for them, and re-layouts: 18.5 us -> 0.6 us  [local(): raw = cotangent.reshape(tok, planes, part).transpose(1, 0, 2)]
    all_to_all x1 -> x3, starting transfers between devices: 9.66 us -> 24.3 us  [the longest x1 8.17 us: local(): arrived = lax.all_to_all(sent, 'expert', 0, 0, tiled=True)]
  transfers between devices with their start and end apart: 2 -> 5, of which waited for: 2 -> 4; matrix products, arithmetic and copies ran while one was open for 3% -> 0% of each run, Pallas kernels for 0% -> 7%
where the time goes in v1:
time: 383 us; the launch traced here: 380 us
  waiting for transfers between devices  241 us (63%)
  blocking collectives  47.6 us (12%)
  Pallas kernels  37 us (10%)
  starting transfers between devices  24.6 us (6%)
  between operations  14.2 us (4%)
  local copies, waits for them, and re-layouts  12.9 us (3%)
    all_to_all x1, waiting for transfers between devices, local(): scaled = lax.all_to_all(scaled, 'expert', 0, 0, tiled=True)  103 us
    all_gather x1, waiting for transfers between devices, local(): extra = lax.all_gather(extra, 'dp')  60.1 us
    all_to_all x1, waiting for transfers between devices, local(): arrived = lax.all_to_all(sent, 'expert', 0, 0, tiled=True)  56.9 us
    all_to_all x1, blocking collectives, local(): lax.all_to_all(grad.reshape(planes, hid, part), 'dp', 0, 0, tiled=True)  47.6 us
    all_to_all x1, waiting for transfers between devices, local(): raw = lax.all_to_all(raw, 'dp', 0, 0, tiled=True)  20.3 us
    pallas_call x1, Pallas kernels, pack_scaled(): pl.pallas_call(functools.partial(pack_scaled_kernel, experts, dests), gri...  10.8 us
    pallas_call x1, Pallas kernels, grad_of(): pl.pallas_call(functools.partial(grad_kernel, group), grid=(sources // gr...  10.6 us
    pallas_call x1, Pallas kernels, hidden_of(): pl.pallas_call(hidden_kernel, grid=(hid // block,), in_specs=[pl.BlockSpe...  9.85 us
  transfers between devices with their start and end apart: 5, of which 4 were waited for; matrix products, arithmetic and copies ran while one was open for 0% of the time, Pallas kernels for 7%

profile of v1, /device:TPU:64, one launch (start us, length us, event | category | flops | bytes accessed | tf_op | source)
XLA Modules:
  0.0 380.3 jit_solution(6359773867969673649)
XLA Ops:
  6.5 0.7 convert_bitcast_fusion.1
  7.2 0.8 reduce-precision_subtract_fusion
  8.0 0.0 copy-start.1
  8.0 1.6 copy.12
  9.6 0.6 copy.13
  10.2 1.0 pad_maximum_fusion
  11.3 0.0 copy-done.1
  11.3 8.1 %all-to-all-start.1 = ((bf16[4,144,896]{2,1,0:T(8,128)(2,1)}), bf16[4,144,896]{2,1,0:T(8,128)(2,1)S(1)}, u32[]{:S(2)}, u32[]{:S(2)}) async-start(bf16[4,144,896]{2,1,0:T(8,128)(2,1)} %pad_maximum_fusion), calls=%async_computation.1 | async-start | bytes 2064384 | tf_op jit(solution)/shard_map/all_to_all | solution.py:301
  19.4 5.7 %pack_tokens.1 = bf16[1024,2688]{1,0:T(8,128)(2,1)} custom-call(f32[8,128]{1,0:T(8,128)} %copy-done.1, bf16[128,3584]{1,0:T(8,128)(2,1)} %tail_ref.1, bf16[128,3584]{1,0:T(8,128)(2,1)} %tail_ref.1), custom_call_target="tpu_custom_call" | custom-call | tf_op jit(solution)/shard_map/pack_tokens/pallas_call | solution.py:66
  25.1 20.3 %all-to-all-done.1.raw_ref = bf16[4,144,896]{2,1,0:T(8,128)(2,1)S(1)} async-done(((bf16[4,144,896]{2,1,0:T(8,128)(2,1)}), bf16[4,144,896]{2,1,0:T(8,128)(2,1)S(1)}, u32[]{:S(2)}, u32[]{:S(2)}) %all-to-all-start.1) | async-done | bytes 1032224 | tf_op jit(solution)/shard_map/all_to_all | solution.py:301
  45.4 0.0 copy-start
  45.4 1.0 copy-done
  46.4 8.2 %all-to-all-start = ((bf16[64,16,2688]{2,1,0:T(8,128)(2,1)}), bf16[64,16,2688]{2,1,0:T(8,128)(2,1)}, u32[]{:S(2)}, u32[]{:S(2)}) async-start(bf16[64,16,2688]{2,1,0:T(8,128)(2,1)} %bitcast.17), calls=%async_computation | async-start | bytes 11010048 | tf_op jit(solution)/shard_map/all_to_all | solution.py:296
  54.5 10.8 %pack_scaled.1 = bf16[3072,896]{1,0:T(8,128)(2,1)} custom-call(bf16[4,144,896]{2,1,0:T(8,128)(2,1)} %copy-done), custom_call_target="tpu_custom_call" | custom-call | tf_op jit(solution)/shard_map/pack_scaled/pallas_call | solution.py:117
  65.4 56.9 %all-to-all-done = bf16[64,16,2688]{2,1,0:T(8,128)(2,1)} async-done(((bf16[64,16,2688]{2,1,0:T(8,128)(2,1)}), bf16[64,16,2688]{2,1,0:T(8,128)(2,1)}, u32[]{:S(2)}, u32[]{:S(2)}) %all-to-all-start) | async-done | bytes 5505056 | tf_op jit(solution)/shard_map/all_to_all | solution.py:296
  122.3 0.0 copy-start.2
  122.3 8.0 %all-to-all-start.2 = ((bf16[64,48,896]{2,1,0:T(8,128)(2,1)}), bf16[64,48,896]{2,1,0:T(8,128)(2,1)}, u32[]{:S(2)}, u32[]{:S(2)}) async-start(bf16[64,48,896]{2,1,0:T(8,128)(2,1)} %bitcast.16), calls=%async_computation.2 | async-start | bytes 11010048 | tf_op jit(solution)/shard_map/all_to_all | solution.py:304
  130.3 0.0 all-gather.5.cloned.1.call-start
  130.3 0.0 copy-done.2
  130.4 0.1 copy.11
  130.5 0.1 eq.23
  130.6 0.1 convert_reduce_fusion
  130.7 0.6 fusion
  132.0 9.8 %hidden_of.1 = (bf16[384,1024]{1,0:T(8,128)(2,1)}, bf16[384,1024]{1,0:T(8,128)(2,1)}) custom-call(s32[1]{0:T(128)} %bitcast.hot_ref, bf16[64,2,8,2688]{3,2,1,0:T(8,128)(2,1)} %bitcast.4.x_ref, bf16[3584,1024]{1,0:T(8,128)(2,1)} %bitcast.18), custom_call_target="tpu_custom_call" | custom-call | tf_op jit(solution)/shard_map/hidden_of/pallas_call | solution.py:186
  141.8 0.0 all-gather.5.cloned.1.call-update
  141.9 0.2 all-gather.7.cloned.1.call-start
  142.1 0.5 all-gather.7.cloned.1.call-update
  142.6 102.7 %all-to-all-done.2 = bf16[64,48,896]{2,1,0:T(8,128)(2,1)} async-done(((bf16[64,48,896]{2,1,0:T(8,128)(2,1)}), bf16[64,48,896]{2,1,0:T(8,128)(2,1)}, u32[]{:S(2)}, u32[]{:S(2)}) %all-to-all-start.2) | async-done | bytes 5505056 | tf_op jit(solution)/shard_map/all_to_all | solution.py:304
  245.3 0.0 all-gather.5.cloned.1.call-done
  245.3 60.1 %all-gather.7.cloned.1.call-done = bf16[1536,1024]{1,0:T(8,128)(2,1)} async-done(((bf16[384,1024]{1,0:T(8,128)(2,1)}), bf16[1536,1024]{1,0:T(8,128)(2,1)}) %all-gather.7.cloned.1.call-update) | async-done | bytes 3145744 | tf_op jit(solution)/shard_map/all_gather | solution.py:308
  305.5 10.6 %grad_of.1 = bf16[1024,896]{1,0:T(8,128)(2,1)} custom-call(s32[1]{0:T(128)} %bitcast.hot_ref, bf16[4,384,1024]{2,1,0:T(8,128)(2,1)} %bitcast.22, bf16[4,384,1024]{2,1,0:T(8,128)(2,1)} %bitcast.23, bf16[64,2,24,896]{3,2,1,0:T(8,128)(2,1)} %bitcast.11.s_ref), custom_call_target="tpu_custom_call" | custom-call | tf_op jit(solution)/shard_map/grad_of/pallas_call | solution.py:243
  316.0 47.6 %all_to_all.20 = bf16[4,256,896]{2,1,0:T(8,128)(2,1)S(1)} all-to-all(bf16[4,256,896]{2,1,0:T(8,128)(2,1)} %bitcast.19), channel_id=1, replica_groups=mesh['expert'=64,'dp'=4] {'dp'}, dimensions={0} | all-to-all | bytes 3670016 | tf_op jit(solution)/shard_map/all_to_all | solution.py:312
  363.6 0.2 convert_bitcast_fusion
  363.9 4.2 %copy.14 = f32[256,4,896]{2,1,0:T(4,128)} copy(f32[256,4,896]{2,0,1:T(8,128)S(1)} %convert_bitcast_fusion) | data formatting | bytes 7340032 | tf_op jit(solution)/shard_map/convert_element_type | solution.py:313
  368.1 5.4 %reshape.49 = f32[1,256,3584]{2,1,0:T(8,128)} reshape(f32[256,4,896]{2,1,0:T(4,128)} %copy.14) | data formatting | bytes 7340032 | tf_op jit(solution)/shard_map/convert_element_type | solution.py:313
  (4 shorter events, 0.0 us)
Async XLA Ops:
  8.0 3.3 copy-start.1
  11.3 34.1 %all-to-all-start.1 = ((bf16[4,144,896]{2,1,0:T(8,128)(2,1)}), bf16[4,144,896]{2,1,0:T(8,128)(2,1)S(1)}, u32[]{:S(2)}, u32[]{:S(2)}) async-start(bf16[4,144,896]{2,1,0:T(8,128)(2,1)} %pad_maximum_fusion), calls=%async_computation.1 | async-start | bytes 2064384 | tf_op jit(solution)/shard_map/all_to_all | solution.py:301
  45.4 1.0 copy-start
  46.4 75.9 %all-to-all-start = ((bf16[64,16,2688]{2,1,0:T(8,128)(2,1)}), bf16[64,16,2688]{2,1,0:T(8,128)(2,1)}, u32[]{:S(2)}, u32[]{:S(2)}) async-start(bf16[64,16,2688]{2,1,0:T(8,128)(2,1)} %bitcast.17), calls=%async_computation | async-start | bytes 11010048 | tf_op jit(solution)/shard_map/all_to_all | solution.py:296
  122.3 8.1 %copy-start.2 = (s32[128,2]{0,1:T(2,128)S(1)}, s32[128,2]{0,1:T(2,128)}, u32[]{:S(2)}) copy-start(s32[128,2]{0,1:T(2,128)} %param.7) | copy-start | bytes 3076
  122.3 123.0 %all-to-all-start.2 = ((bf16[64,48,896]{2,1,0:T(8,128)(2,1)}), bf16[64,48,896]{2,1,0:T(8,128)(2,1)}, u32[]{:S(2)}, u32[]{:S(2)}) async-start(bf16[64,48,896]{2,1,0:T(8,128)(2,1)} %bitcast.16), calls=%async_computation.2 | async-start | bytes 11010048 | tf_op jit(solution)/shard_map/all_to_all | solution.py:304
  130.3 115.0 %all-gather.5.cloned.1.call-start = ((), (), s32[]{:S(2)}) async-start(), calls=%async_computation.4 | async-start | bytes 3932160 | tf_op jit(solution)/shard_map/all_gather | solution.py:307
  141.9 163.6 %all-gather.7.cloned.1.call-start = ((), (), s32[]{:S(2)}) async-start(), calls=%async_computation.5 | async-start | bytes 3932160 | tf_op jit(solution)/shard_map/all_gather | solution.py:308
Sparse Core Ops, SparseCore 0:
  142.0 90.7 all-gather.4
  234.6 70.7 all-gather.6

commit v2 on v1

v2 whole, which is shorter than its diff:
```python
import functools

import jax
import jax.numpy as jnp
from jax import lax
from jax.experimental import pallas as pl
from jax.experimental.pallas import tpu as pltpu
from jax.sharding import PartitionSpec as P

CAP = 6
F32 = jnp.float32
BF16 = jnp.bfloat16
VMEM_LIMIT = 56 * 1024 * 1024


def iota(shape, dim):
    return lax.broadcasted_iota(jnp.int32, shape, dim)


def floordiv(a, n):
    return jnp.floor((a.astype(F32) + 0.5) * (1.0 / n)).astype(jnp.int32)


def slot_keys(route, experts):
    tok = route.shape[1]
    column = route.T
    r0, r1 = route[0:1], route[1:2]
    c0, c1 = column[:, 0:1], column[:, 1:2]
    before = iota((tok, tok), 0) < iota((tok, tok), 1)

    def count(mask):
        return jnp.sum(jnp.where(mask, 1.0, 0.0), 0, keepdims=True)

    rank0 = count((c0 == r0) & before)
    rank1 = count(c0 == r1) + count((c1 == r1) & before)

    def key(r, rank):
        return jnp.where(rank < CAP, r * CAP + rank, experts * CAP + rank - CAP).astype(jnp.int32)

    return key(r0, rank0), key(r1, rank1)


def split_raw_kernel(place_ref, q0_ref, q1_ref, q2_ref, q3_ref, meta_ref, *out_refs):
    tok = q0_ref.shape[0]
    note = jnp.concatenate([meta_ref[...], jnp.zeros_like(meta_ref)], 0).astype(BF16)
    for in_ref, out_ref in zip((q0_ref, q1_ref, q2_ref, q3_ref), out_refs):
        out_ref[0:tok, :] = in_ref[...]
        out_ref[tok:, :] = jnp.zeros((16, in_ref.shape[1]), BF16)
        out_ref[tok:, 0:tok] = note


def split_raw(place, cotangent, meta):
    tok, width = cotangent.shape
    part = width // 4
    quarter = [pl.BlockSpec((tok, part), lambda i, s, d=d: (0, lax.rem(s[1] + d, 4))) for d in range(4)]
    return pl.pallas_call(
        split_raw_kernel,
        grid_spec=pltpu.PrefetchScalarGridSpec(
            num_scalar_prefetch=1,
            grid=(1,),
            in_specs=quarter + [pl.BlockSpec(meta.shape, lambda i, s: (0, 0))],
            out_specs=[pl.BlockSpec((tok + 16, part), lambda i, s: (0, 0))] * 4,
        ),
        out_shape=[jax.ShapeDtypeStruct((tok + 16, part), BF16)] * 4,
        compiler_params=pltpu.CompilerParams(vmem_limit_bytes=VMEM_LIMIT),
        name="split_raw",
    )(place, cotangent, cotangent, cotangent, cotangent, meta)


def pick(mask):
    return jnp.where(mask, 1.0, 0.0).astype(BF16)


def expert_of(dest, z):
    return (dest >> 3) * 16 + z * 8 + (dest & 7)


def pack_tokens_kernel(experts, place_ref, a_meta, b_meta, a_head, b_head, a_tail, b_tail, out_ref):
    k = pl.program_id(0)
    dests, _, _, part = out_ref.shape
    keys = [slot_keys(m[...], experts) for m in (a_meta, b_meta)]
    right = jnp.concatenate([a_head[...], b_head[...], a_tail[...], b_tail[...]], 0)

    def rows_of(rows, base):
        row = iota((rows, 1), 0)
        source, jj = (row >> 3) & 1, row & 7
        parts = []
        for tail in (False, True):
            slot = base + (2 * k + jj - CAP if tail else jj)
            for i, (key0, key1) in enumerate(keys):
                fits = (source == i) & ((jj >= CAP) if tail else (jj < CAP))
                mine = jnp.where(fits, slot, -1)
                parts.append(pick((mine == key0) | (mine == key1)))
        left = jnp.concatenate(parts, 1)
        return jnp.dot(left, right, preferred_element_type=F32).astype(BF16)

    dest = iota((dests * 16, 1), 0) >> 4
    main = rows_of(dests * 16, expert_of(dest, place_ref[3]) * CAP)
    out_ref[:, 0] = main.reshape(dests, 16, part)
    extra = rows_of(16, experts * CAP)
    out_ref[:, 1] = jnp.broadcast_to(extra[None], (dests, 16, part))


def pack_tokens(place, metas, tokens, experts):
    tok, width = tokens[0].shape
    part = width // 4
    dests = experts // 2
    whole = pl.BlockSpec(metas[0].shape, lambda k, s: (0, 0))
    head = pl.BlockSpec((tok, part), lambda k, s: (0, k))
    tail = pl.BlockSpec((tok, part), lambda k, s: (0, 3))
    return pl.pallas_call(
        functools.partial(pack_tokens_kernel, experts),
        grid_spec=pltpu.PrefetchScalarGridSpec(
            num_scalar_prefetch=1,
            grid=(3,),
            in_specs=[whole, whole, head, head, tail, tail],
            out_specs=pl.BlockSpec((dests, 2, 16, part), lambda k, s: (0, 0, 0, k)),
        ),
        out_shape=jax.ShapeDtypeStruct((dests, 2, 16, 3 * part), BF16),
        compiler_params=pltpu.CompilerParams(vmem_limit_bytes=VMEM_LIMIT),
        name="pack_tokens",
    )(place, *metas, *tokens, *tokens)


def pack_scaled_kernel(experts, place_ref, a0, a1, a2, a3, b0, b1, b2, b3, out_ref):
    block, _, _, _, part = out_ref.shape
    tok = 128
    planes = 4
    span = planes * CAP
    first = pl.program_id(0) * block

    for source, raws in enumerate(((a0, a1, a2, a3), (b0, b1, b2, b3))):
        facts = []
        for raw in raws:
            meta = raw[tok : tok + 16, 0:tok].astype(F32)
            gate0 = (meta[2:3] + meta[3:4]) + meta[4:5]
            gate1 = (meta[5:6] + meta[6:7]) + meta[7:8]
            facts.append((*slot_keys(meta[0:8], experts), gate0, gate1))
        right = jnp.concatenate([raw[0:tok, :] for raw in raws], 0)

        def rows_of(slot, plane):
            lefts = []
            gate = jnp.zeros(slot.shape, F32)
            for p, (key0, key1, gate0, gate1) in enumerate(facts):
                mine = jnp.where(plane == p, slot, -1)
                hit0, hit1 = mine == key0, mine == key1
                both = jnp.where(hit0, gate0, 0.0) + jnp.where(hit1, gate1, 0.0)
                gate = gate + jnp.sum(both, 1, keepdims=True)
                lefts.append(pick(hit0 | hit1))
            rows = jnp.dot(jnp.concatenate(lefts, 1), right, preferred_element_type=F32)
            return (gate * rows).astype(BF16)

        row = iota((block * span, 1), 0)
        dest = floordiv(row, span)
        j = row - dest * span
        plane = floordiv(j, CAP)
        slot = expert_of(first + dest, place_ref[3]) * CAP + j - plane * CAP
        out_ref[:, 0, source] = rows_of(slot, plane).reshape(block, span, part)
        j = iota((span, 1), 0)
        plane = floordiv(j, CAP)
        extra = rows_of(experts * CAP + j - plane * CAP, plane)
        out_ref[:, 1, source] = jnp.broadcast_to(extra[None], (block, span, part))


def pack_scaled(place, raws, experts):
    part = raws[0].shape[1]
    dests = experts // 2
    block = 8
    span = 4 * CAP
    return pl.pallas_call(
        functools.partial(pack_scaled_kernel, experts),
        grid_spec=pltpu.PrefetchScalarGridSpec(
            num_scalar_prefetch=1,
            grid=(dests // block,),
            in_specs=[pl.BlockSpec(raws[0].shape, lambda g, s: (0, 0))] * 8,
            out_specs=pl.BlockSpec((block, 2, 2, span, part), lambda g, s: (g, 0, 0, 0, 0)),
        ),
        out_shape=jax.ShapeDtypeStruct((dests, 2, 2, span, part), BF16),
        compiler_params=pltpu.CompilerParams(vmem_limit_bytes=VMEM_LIMIT),
        name="pack_scaled",
    )(place, *raws)


def hidden_kernel(place_ref, x_ref, w_ref, main_ref, extra_ref, rows_ref):
    senders, _, _, head = x_ref.shape
    sources = 2 * senders
    part = head // 3
    half = sources // 2
    is_hot = place_ref[0] > 0
    count = sources * CAP

    def unfold(which):
        r = iota((half * CAP, half * 8), 0)
        c = iota((half * CAP, half * 8), 1)
        src = floordiv(r, CAP)
        s = r - src * CAP
        for h in range(2):
            x = x_ref[h * senders // 2 : (h + 1) * senders // 2, which].reshape(half * 8, head)
            rows = pl.ds(which * count + h * half * CAP, half * CAP)
            rows_ref[rows, 0:head] = jnp.dot(
                pick(c == src * 8 + s), x, preferred_element_type=F32
            ).astype(BF16)
            tail = jnp.zeros((half * CAP, part), F32)
            for k in range(3):
                mask = (c == src * 8 + CAP + s - 2 * k) & (s >= 2 * k) & (s < 2 * k + 2)
                tail = tail + jnp.dot(
                    pick(mask), x[:, k * part : (k + 1) * part], preferred_element_type=F32
                )
            rows_ref[rows, head:] = tail.astype(BF16)

    @pl.when(pl.program_id(0) == 0)
    def _():
        unfold(0)

        @pl.when(is_hot)
        def _():
            unfold(1)

    def hidden(first):
        v = jnp.dot(rows_ref[first : first + count, :], w_ref[...], preferred_element_type=F32)
        return (v / (1.0 + jnp.exp(-v))).astype(BF16)

    main_ref[...] = hidden(0)

    @pl.when(is_hot)
    def _():
        extra_ref[...] = hidden(count)

    @pl.when(jnp.logical_not(is_hot))
    def _():
        extra_ref[...] = jnp.zeros_like(extra_ref)


def hidden_of(place, x, weight):
    senders, _, _, head = x.shape
    width, hid = weight.shape
    count = 2 * senders * CAP
    block = 256
    return pl.pallas_call(
        hidden_kernel,
        grid_spec=pltpu.PrefetchScalarGridSpec(
            num_scalar_prefetch=1,
            grid=(hid // block,),
            in_specs=[
                pl.BlockSpec(x.shape, lambda n, s: (0, 0, 0, 0)),
                pl.BlockSpec((width, block), lambda n, s: (0, n)),
            ],
            out_specs=[pl.BlockSpec((count, block), lambda n, s: (0, n))] * 2,
            scratch_shapes=[pltpu.VMEM((2 * count, width), BF16)],
        ),
        out_shape=[jax.ShapeDtypeStruct((count, hid), BF16)] * 2,
        compiler_params=pltpu.CompilerParams(vmem_limit_bytes=VMEM_LIMIT),
        name="hidden_of",
    )(place, x, weight)


def grad_kernel(place_ref, main_ref, near_ref, far_ref, s_ref, out_ref, acc_ref):
    planes, n, hid = main_ref.shape
    part = s_ref.shape[-1]
    g = pl.program_id(0)
    rows = planes * n

    o, i = iota((rows, rows), 0), iota((rows, rows), 1)
    plane = floordiv(o, n)
    rest = o - plane * n
    src = floordiv(rest, CAP)
    perm = pick(i == src * planes * CAP + plane * CAP + rest - src * CAP)

    def term(h_ref, which):
        s = s_ref[:, which].reshape(rows, part)
        s = jnp.dot(perm, s, preferred_element_type=F32).astype(BF16)
        h = [h_ref[lax.rem(place_ref[1] + planes - d, planes)] for d in range(planes)]
        h = jnp.concatenate(h, 0)
        return lax.dot_general(h, s, (((0,), (0,)), ((), ())), preferred_element_type=F32)

    @pl.when(g == 0)
    def _():
        acc_ref[...] = term(main_ref, 0)

    @pl.when(g > 0)
    def _():
        acc_ref[...] += term(main_ref, 0)

    is_hot = place_ref[0] > 0
    is_near = g // 2 == place_ref[2]

    @pl.when(is_hot & is_near)
    def _():
        acc_ref[...] += term(near_ref, 1)

    @pl.when(is_hot & jnp.logical_not(is_near))
    def _():
        acc_ref[...] += term(far_ref, 1)

    @pl.when(g == pl.num_programs(0) - 1)
    def _():
        out_ref[...] = acc_ref[...].astype(out_ref.dtype)


def grad_of(place, hidden, far, s):
    planes, _, hid = hidden.shape
    senders, _, span, part = s.shape
    group = 8
    block = (planes, 2 * group * CAP, hid)
    return pl.pallas_call(
        grad_kernel,
        grid_spec=pltpu.PrefetchScalarGridSpec(
            num_scalar_prefetch=1,
            grid=(senders // group,),
            in_specs=[
                pl.BlockSpec(block, lambda g, s: (0, g, 0)),
                pl.BlockSpec(block, lambda g, s: (0, 4 + lax.rem(g, 2), 0)),
                pl.BlockSpec(block, lambda g, s: (0, lax.rem(g, 2), 0)),
                pl.BlockSpec((group, 2, span, part), lambda g, s: (g, 0, 0, 0)),
            ],
            out_specs=pl.BlockSpec((hid, part), lambda g, s: (0, 0)),
            scratch_shapes=[pltpu.VMEM((hid, part), F32)],
        ),
        out_shape=jax.ShapeDtypeStruct((hid, part), BF16),
        compiler_params=pltpu.CompilerParams(vmem_limit_bytes=VMEM_LIMIT),
        name="grad_of",
    )(place, hidden, hidden, far, s)


def join_kernel(in_ref, out_ref):
    out_ref[...] = in_ref[...].astype(F32)


def join(parts):
    planes, rows, part = parts.shape
    return pl.pallas_call(
        join_kernel,
        grid=(planes,),
        in_specs=[pl.BlockSpec((1, rows, part), lambda n: (n, 0, 0))],
        out_specs=pl.BlockSpec((1, rows, part), lambda n: (0, 0, n)),
        out_shape=jax.ShapeDtypeStruct((1, rows, planes * part), F32),
        compiler_params=pltpu.CompilerParams(vmem_limit_bytes=VMEM_LIMIT),
        name="join",
    )(parts)


def bf16_parts(x):
    high = lax.reduce_precision(x, 8, 7)
    mid = lax.reduce_precision(x - high, 8, 7)
    return [high, mid, x - high - mid]


def local(tokens, cotangent, routes, gates, gate_weight):
    experts = lax.axis_size("expert")
    planes = lax.axis_size("dp")
    me = lax.axis_index("expert")
    dp = lax.axis_index("dp")
    core = me & 1
    other_z = [(i, i ^ 8) for i in range(experts)]
    other_core = [(i, i ^ 1) for i in range(experts)]
    same_z = [[i for i in range(experts) if (i >> 3) & 1 == z] for z in range(2)]

    route_rows = routes.T.astype(F32)
    gate_rows = gates.T
    meta = jnp.concatenate(
        [route_rows, jnp.stack(bf16_parts(gate_rows[0])), jnp.stack(bf16_parts(gate_rows[1]))], 0
    )
    own = jnp.sum((routes == me).astype(jnp.int32))
    hot = (own > CAP).astype(jnp.int32)
    place = jnp.stack([hot, dp, core, (me >> 3) & 1]).astype(jnp.int32)

    far_tokens = lax.ppermute(tokens, "expert", other_z)
    far_meta = lax.ppermute(meta, "expert", other_z)

    blocks = split_raw(place, cotangent, meta)
    far_tokens, blocks = lax.optimization_barrier((far_tokens, blocks))
    raws = [blocks[0]]
    for d in range(1, planes):
        raws.append(lax.ppermute(blocks[d], "dp", [(i, (i + d) % planes) for i in range(planes)]))
    raws = raws + [lax.ppermute(raw, "expert", other_z) for raw in raws]

    sent = pack_tokens(place, (meta, far_meta), (tokens, far_tokens), experts)
    sent = sent.reshape(experts // 2, 32, sent.shape[-1])
    arrived = lax.all_to_all(sent, "expert", 0, 0, tiled=True, axis_index_groups=same_z)
    arrived = arrived.reshape(experts // 2, 2, 16, arrived.shape[-1])

    scaled = pack_scaled(place, raws, experts)
    span = scaled.shape[-2]
    scaled = scaled.reshape(experts // 2, 4 * span, scaled.shape[-1])
    scaled = lax.all_to_all(scaled, "expert", 0, 0, tiled=True, axis_index_groups=same_z)
    scaled = scaled.reshape(experts // 2, 2, 2 * span, scaled.shape[-1])

    main, extra = hidden_of(place, arrived, gate_weight[0])
    half = extra.shape[0] // 2
    kept = lax.dynamic_slice_in_dim(extra, core * half, half, 0)
    given = lax.dynamic_slice_in_dim(extra, (1 - core) * half, half, 0)
    kept = kept + lax.ppermute(given, "expert", other_core)
    hidden = lax.all_gather(jnp.concatenate([main, kept], 0), "dp")
    far = lax.ppermute(hidden[:, main.shape[0] :], "expert", other_core)

    grad = grad_of(place, hidden, far, scaled)
    hid = grad.shape[0] // planes
    grad = lax.all_to_all(grad.reshape(planes, hid, grad.shape[-1]), "dp", 0, 0, tiled=True)
    return join(grad)


def solution(mesh):
    placed = (
        P(("expert", "dp"), None),
        P(("expert", "dp"), None),
        P(("expert", "dp"), None),
        P(("expert", "dp"), None),
        P("expert", None, None),
    )
    return jax.shard_map(
        local, mesh=mesh, in_specs=placed, out_specs=P("expert", "dp", None), check_vma=False
    )
```

time: 383 us -> 416 us (1.086)
  the two profiles are of different devices: /device:TPU:64 before, /device:TPU:41 now
where the time goes in v2:
time: 416 us; the launch traced here: 415 us
  waiting for transfers between devices  268 us (64%)
  blocking collectives  48.5 us (12%)
  Pallas kernels  45.8 us (11%)
  starting transfers between devices  28 us (7%)
  between operations  14.2 us (3%)
  local copies, waits for them, and re-layouts  5.98 us (1%)
  other arithmetic  5.03 us (1%)
    all_to_all x1, waiting for transfers between devices, local(): lax.all_to_all(sent, 'expert', 0, 0, tiled=True, axis_index_groups=same_z)  74.6 us
    all_to_all x1, waiting for transfers between devices, local(): lax.all_to_all(scaled, 'expert', 0, 0, tiled=True, axis_index_groups=same_z)  71.5 us
    ppermute x4, waiting for transfers between devices, local(): raws = raws + [lax.ppermute(raw, 'expert', other_z) for raw in raws]  63.7 us
    all_to_all x1, blocking collectives, local(): lax.all_to_all(grad.reshape(planes, hid, grad.shape[-1]), 'dp', 0, 0, til...  48.5 us
    ppermute x3, waiting for transfers between devices, local(): lax.ppermute(blocks[d], 'dp', [(i, (i + d) % planes) for i in range(plane...  43.2 us
    ppermute x1, waiting for transfers between devices, local(): far_tokens = lax.ppermute(tokens, 'expert', other_z)  13.4 us
    pallas_call x1, Pallas kernels, grad_of(): pl.pallas_call(grad_kernel, grid_spec=pltpu.PrefetchScalarGridSpec(num_sc...  11.8 us
    pallas_call x1, Pallas kernels, hidden_of(): pl.pallas_call(hidden_kernel, grid_spec=pltpu.PrefetchScalarGridSpec(num_...  10.5 us
  transfers between devices with their start and end apart: 14, of which 12 were waited for; matrix products, arithmetic and copies ran while one was open for 1% of the time, Pallas kernels for 3%

profile of v2, /device:TPU:41, one launch (start us, length us, event | category | flops | bytes accessed | tf_op | source)
XLA Modules:
  0.0 415.4 jit_solution(478613514452903004)
XLA Ops:
  6.5 0.0 collective-permute-start.1
  6.5 1.4 convert_bitcast_fusion
  7.9 0.8 reduce-precision_subtract_fusion
  8.7 1.6 collective-permute-start
  10.9 0.7 pad_add_fusion.place_ref
  11.6 0.0 copy-done.11
  11.6 2.9 split_raw.1
  14.5 13.4 %collective-permute-done.1.b_head.b_tail = bf16[128,3584]{1,0:T(8,128)(2,1)S(1)} collective-permute-done((bf16[128,3584]{1,0:T(8,128)(2,1)}, bf16[128,3584]{1,0:T(8,128)(2,1)S(1)}, u32[]{:S(2)}, u32[]{:S(2)}) %collective-permute-start.1) | collective-permute-done | bytes 917536 | tf_op jit(solution)/shard_map/ppermute | solution.py:367
  28.0 0.1 collective-permute-done.b_meta
  28.1 0.8 copy-done
  28.9 0.6 copy-done.12
  29.5 7.3 %pack_tokens.1 = bf16[32,2,16,2688]{3,2,1,0:T(8,128)(2,1)} custom-call(s32[4]{0:T(128)} %pad_add_fusion.place_ref, f32[8,128]{1,0:T(8,128)} %copy-done.11, f32[8,128]{1,0:T(8,128)} %copy-done.12, bf16[128,3584]{1,0:T(8,128)(2,1)} %a_tail.1, bf16[128,3584]{1,0:T(8,128)(2,1)} %copy-done, bf16[128,3584]{1,0:T(8,128)(2,1)} %a_tail.1, bf16[128,3584]{1,0:T(8,128)(2,1)} %copy-done), custom_call_target="tpu_custom_call" | custom-call | tf_op jit(solution)/shard_map/pack_tokens/pallas_call | solution.py:111
  36.8 8.8 %all-to-all-start = ((bf16[32,32,2688]{2,1,0:T(8,128)(2,1)}), bf16[32,32,2688]{2,1,0:T(8,128)(2,1)}, u32[]{:S(2)}, u32[]{:S(2)}) async-start(bf16[32,32,2688]{2,1,0:T(8,128)(2,1)} %bitcast.18), calls=%async_computation | async-start | bytes 11010048 | tf_op jit(solution)/shard_map/all_to_all | solution.py:379
  45.6 0.0 all-gather.3.cloned.1.call-start
  45.7 74.6 %all-to-all-done = bf16[32,32,2688]{2,1,0:T(8,128)(2,1)} async-done(((bf16[32,32,2688]{2,1,0:T(8,128)(2,1)}), bf16[32,32,2688]{2,1,0:T(8,128)(2,1)}, u32[]{:S(2)}, u32[]{:S(2)}) %all-to-all-start) | async-done | bytes 5505056 | tf_op jit(solution)/shard_map/all_to_all | solution.py:379
  120.3 10.5 %hidden_of.1 = (bf16[384,1024]{1,0:T(8,128)(2,1)}, bf16[384,1024]{1,0:T(8,128)(2,1)}) custom-call(s32[4]{0:T(128)} %pad_add_fusion.place_ref, bf16[32,2,16,2688]{3,2,1,0:T(8,128)(2,1)} %bitcast.7.x_ref, bf16[3584,1024]{1,0:T(8,128)(2,1)} %bitcast.19), custom_call_target="tpu_custom_call" | custom-call | tf_op jit(solution)/shard_map/hidden_of/pallas_call | solution.py:239
  130.8 1.1 constant_dynamic-slice_fusion
  131.9 1.0 collective-permute-start.2
  132.9 1.3 collective-permute-done.2
  134.2 1.1 dynamic-slice_add_fusion
  135.4 1.1 pad_maximum_fusion
  136.5 0.0 all-gather.3.cloned.1.call-update
  136.5 5.2 %collective-permute-start.6 = (bf16[144,896]{1,0:T(8,128)(2,1)S(1)}, bf16[144,896]{1,0:T(8,128)(2,1)S(1)}, u32[]{:S(2)}, u32[]{:S(2)}) collective-permute-start(bf16[144,896]{1,0:T(8,128)(2,1)S(1)} %copy-done.15), channel_id=1, source_target_pairs={{0,3},{1,0},{2,1},{3,2},{4,7},{5,4},{6,5},{7,6},{8,11},{9,8},{10,9... | collective-permute-start | bytes 774152 | tf_op jit(solution)/shard_map/ppermute | solution.py:374
  141.7 0.0 collective-permute-start.4
  141.7 3.2 collective-permute-start.5
  144.9 0.7 collective-permute-start.7
  145.7 13.2 %collective-permute-done.6.a3 = bf16[144,896]{1,0:T(8,128)(2,1)S(1)} collective-permute-done((bf16[144,896]{1,0:T(8,128)(2,1)S(1)}, bf16[144,896]{1,0:T(8,128)(2,1)S(1)}, u32[]{:S(2)}, u32[]{:S(2)}) %collective-permute-start.6) | collective-permute-done | bytes 258080 | tf_op jit(solution)/shard_map/ppermute | solution.py:374
  158.8 0.0 collective-permute-start.10
  158.8 16.6 %collective-permute-done.4.a1 = bf16[144,896]{1,0:T(8,128)(2,1)S(1)} collective-permute-done((bf16[144,896]{1,0:T(8,128)(2,1)S(1)}, bf16[144,896]{1,0:T(8,128)(2,1)S(1)}, u32[]{:S(2)}, u32[]{:S(2)}) %collective-permute-start.4) | collective-permute-done | bytes 258080 | tf_op jit(solution)/shard_map/ppermute | solution.py:374
  175.4 0.0 collective-permute-start.8
  175.5 13.4 %collective-permute-done.5.a2 = bf16[144,896]{1,0:T(8,128)(2,1)S(1)} collective-permute-done((bf16[144,896]{1,0:T(8,128)(2,1)S(1)}, bf16[144,896]{1,0:T(8,128)(2,1)S(1)}, u32[]{:S(2)}, u32[]{:S(2)}) %collective-permute-start.5) | collective-permute-done | bytes 258080 | tf_op jit(solution)/shard_map/ppermute | solution.py:374
  188.9 0.0 collective-permute-start.9
  188.9 20.2 %collective-permute-done.7.b0 = bf16[144,896]{1,0:T(8,128)(2,1)S(1)} collective-permute-done((bf16[144,896]{1,0:T(8,128)(2,1)S(1)}, bf16[144,896]{1,0:T(8,128)(2,1)S(1)}, u32[]{:S(2)}, u32[]{:S(2)}) %collective-permute-start.7) | collective-permute-done | bytes 258080 | tf_op jit(solution)/shard_map/ppermute | solution.py:375
  209.1 18.2 %collective-permute-done.10.b3 = bf16[144,896]{1,0:T(8,128)(2,1)S(1)} collective-permute-done((bf16[144,896]{1,0:T(8,128)(2,1)S(1)}, bf16[144,896]{1,0:T(8,128)(2,1)S(1)}, u32[]{:S(2)}, u32[]{:S(2)}) %collective-permute-start.10) | collective-permute-done | bytes 258080 | tf_op jit(solution)/shard_map/ppermute | solution.py:375
  227.3 14.2 %collective-permute-done.8.b1 = bf16[144,896]{1,0:T(8,128)(2,1)S(1)} collective-permute-done((bf16[144,896]{1,0:T(8,128)(2,1)S(1)}, bf16[144,896]{1,0:T(8,128)(2,1)S(1)}, u32[]{:S(2)}, u32[]{:S(2)}) %collective-permute-start.8) | collective-permute-done | bytes 258080 | tf_op jit(solution)/shard_map/ppermute | solution.py:375
  241.5 11.1 %collective-permute-done.9.b2 = bf16[144,896]{1,0:T(8,128)(2,1)S(1)} collective-permute-done((bf16[144,896]{1,0:T(8,128)(2,1)S(1)}, bf16[144,896]{1,0:T(8,128)(2,1)S(1)}, u32[]{:S(2)}, u32[]{:S(2)}) %collective-permute-start.9) | collective-permute-done | bytes 258080 | tf_op jit(solution)/shard_map/ppermute | solution.py:375
  252.7 0.7 copy-done.10
  253.3 9.1 %pack_scaled.1 = bf16[32,2,2,24,896]{4,3,2,1,0:T(8,128)(2,1)} custom-call(s32[4]{0:T(128)} %pad_add_fusion.place_ref, bf16[144,896]{1,0:T(8,128)(2,1)} %get-tuple-element.23.a0, bf16[144,896]{1,0:T(8,128)(2,1)} %copy-done.5, bf16[144,896]{1,0:T(8,128)(2,1)} %copy-done.6, bf16[144,896]{1,0:T(8,128)(2,1)} %copy-done.4, bf16[144,896]{1,0:T(8,128)(2,1)} %copy-done.7, ...), custom_call_target="tpu_custom_call" | custom-call | tf_op jit(solution)/shard_map/pack_scaled/pallas_call | solution.py:170
  262.5 5.8 %all-to-all-start.1 = ((bf16[32,96,896]{2,1,0:T(8,128)(2,1)}), bf16[32,96,896]{2,1,0:T(8,128)(2,1)}, u32[]{:S(2)}, u32[]{:S(2)}) async-start(bf16[32,96,896]{2,1,0:T(8,128)(2,1)} %bitcast.17), calls=%async_computation.1 | async-start | bytes 11010048 | tf_op jit(solution)/shard_map/all_to_all | solution.py:385
  268.3 0.0 all-gather.3.cloned.1.call-done
  268.4 1.5 slice.12
  269.9 1.6 collective-permute-start.3
  271.5 71.5 %all-to-all-done.1 = bf16[32,96,896]{2,1,0:T(8,128)(2,1)} async-done(((bf16[32,96,896]{2,1,0:T(8,128)(2,1)}), bf16[32,96,896]{2,1,0:T(8,128)(2,1)}, u32[]{:S(2)}, u32[]{:S(2)}) %all-to-all-start.1) | async-done | bytes 5505056 | tf_op jit(solution)/shard_map/all_to_all | solution.py:385
  343.0 0.0 collective-permute-done.3.far_ref
  343.0 1.2 copy-done.1
  344.2 11.8 %grad_of.1 = bf16[1024,896]{1,0:T(8,128)(2,1)} custom-call(s32[4]{0:T(128)} %pad_add_fusion.place_ref, bf16[4,576,1024]{2,1,0:T(8,128)(2,1)} %bitcast.15, bf16[4,576,1024]{2,1,0:T(8,128)(2,1)} %bitcast.16, bf16[4,192,1024]{2,1,0:T(8,128)(2,1)} %copy-done.1, bf16[32,2,48,896]{3,2,1,0:T(8,128)(2,1)} %bitcast.11.s_ref), custom_call_target="tpu_custom_call" | custom-call | tf_op jit(solution)/shard_map/grad_of/pallas_call | solution.py:305
  356.0 48.5 %all_to_all.15.in_ref = bf16[4,256,896]{2,1,0:T(8,128)(2,1)} all-to-all(bf16[4,256,896]{2,1,0:T(8,128)(2,1)} %bitcast.20), channel_id=1, replica_groups=mesh['expert'=64,'dp'=4] {'dp'}, dimensions={0} | all-to-all | bytes 3670016 | tf_op jit(solution)/shard_map/all_to_all | solution.py:398
  404.5 4.0 join.1
  (28 shorter events, 0.1 us)
Async XLA Ops:
  6.5 21.4 %collective-permute-start.1 = (bf16[128,3584]{1,0:T(8,128)(2,1)}, bf16[128,3584]{1,0:T(8,128)(2,1)S(1)}, u32[]{:S(2)}, u32[]{:S(2)}) collective-permute-start(bf16[128,3584]{1,0:T(8,128)(2,1)} %a_tail.1), channel_id=1, source_target_pairs={{0,32},{4,36},{8,40},{12,44},{16,48},{20,52},{24,56},{28,60},{32,0... | collective-permute-start | bytes 2752520 | tf_op jit(solution)/shard_map/ppermute | solution.py:367
  8.7 2.9 copy-start.11
  8.7 19.3 %collective-permute-start = (f32[8,128]{1,0:T(8,128)S(1)}, f32[8,128]{1,0:T(8,128)S(1)}, u32[]{:S(2)}, u32[]{:S(2)}) collective-permute-start(f32[8,128]{1,0:T(8,128)S(1)} %concatenate.6.meta_ref.a_meta), channel_id=1, source_target_pairs={{0,32},{4,36},{8,40},{12,44},{16,48},{20,52},{24,56},{28,60},{32,0... | collective-permute-start | bytes 12296 | tf_op jit(solution)/shard_map/ppermute | solution.py:368
  28.0 0.9 copy-start
  28.9 0.6 copy-start.12
  36.8 83.5 %all-to-all-start = ((bf16[32,32,2688]{2,1,0:T(8,128)(2,1)}), bf16[32,32,2688]{2,1,0:T(8,128)(2,1)}, u32[]{:S(2)}, u32[]{:S(2)}) async-start(bf16[32,32,2688]{2,1,0:T(8,128)(2,1)} %bitcast.18), calls=%async_computation | async-start | bytes 11010048 | tf_op jit(solution)/shard_map/all_to_all | solution.py:379
  45.6 222.7 %all-gather.3.cloned.1.call-start = ((), (), s32[]{:S(2)}) async-start(), calls=%async_computation.3 | async-start | bytes 5898240 | tf_op jit(solution)/shard_map/all_gather | solution.py:393
  130.8 4.5 %copy-start.2 = (bf16[384,1024]{1,0:T(8,128)(2,1)S(1)}, bf16[384,1024]{1,0:T(8,128)(2,1)}, u32[]{:S(2)}) copy-start(bf16[384,1024]{1,0:T(8,128)(2,1)} %get-tuple-element.21) | copy-start | bytes 2359300
  131.9 2.3 collective-permute-start.2
  132.9 3.6 copy-start.15
  132.9 8.8 %copy-start.14 = (bf16[144,896]{1,0:T(8,128)(2,1)S(1)}, bf16[144,896]{1,0:T(8,128)(2,1)}, u32[]{:S(2)}) copy-start(bf16[144,896]{1,0:T(8,128)(2,1)} %get-tuple-element.24) | copy-start | bytes 774148
  132.9 8.8 %copy-start.13 = (bf16[144,896]{1,0:T(8,128)(2,1)S(1)}, bf16[144,896]{1,0:T(8,128)(2,1)}, u32[]{:S(2)}) copy-start(bf16[144,896]{1,0:T(8,128)(2,1)} %get-tuple-element.25) | copy-start | bytes 774148
  132.9 12.1 %copy-start.3 = (bf16[144,896]{1,0:T(8,128)(2,1)S(1)}, bf16[144,896]{1,0:T(8,128)(2,1)}, u32[]{:S(2)}) copy-start(bf16[144,896]{1,0:T(8,128)(2,1)} %get-tuple-element.23.a0) | copy-start | bytes 774148
  136.5 22.3 %collective-permute-start.6 = (bf16[144,896]{1,0:T(8,128)(2,1)S(1)}, bf16[144,896]{1,0:T(8,128)(2,1)S(1)}, u32[]{:S(2)}, u32[]{:S(2)}) collective-permute-start(bf16[144,896]{1,0:T(8,128)(2,1)S(1)} %copy-done.15), channel_id=1, source_target_pairs={{0,3},{1,0},{2,1},{3,2},{4,7},{5,4},{6,5},{7,6},{8,11},{9,8},{10,9... | collective-permute-start | bytes 774152 | tf_op jit(solution)/shard_map/ppermute | solution.py:374
  141.7 33.8 %collective-permute-start.4 = (bf16[144,896]{1,0:T(8,128)(2,1)S(1)}, bf16[144,896]{1,0:T(8,128)(2,1)S(1)}, u32[]{:S(2)}, u32[]{:S(2)}) collective-permute-start(bf16[144,896]{1,0:T(8,128)(2,1)S(1)} %copy-done.14), channel_id=1, source_target_pairs={{0,1},{1,2},{2,3},{3,0},{4,5},{5,6},{6,7},{7,4},{8,9},{9,10},{10,1... | collective-permute-start | bytes 774152 | tf_op jit(solution)/shard_map/ppermute | solution.py:374
  141.7 47.2 %collective-permute-start.5 = (bf16[144,896]{1,0:T(8,128)(2,1)S(1)}, bf16[144,896]{1,0:T(8,128)(2,1)S(1)}, u32[]{:S(2)}, u32[]{:S(2)}) collective-permute-start(bf16[144,896]{1,0:T(8,128)(2,1)S(1)} %copy-done.13), channel_id=1, source_target_pairs={{0,2},{1,3},{2,0},{3,1},{4,6},{5,7},{6,4},{7,5},{8,10},{9,11},{10,... | collective-permute-start | bytes 774152 | tf_op jit(solution)/shard_map/ppermute | solution.py:374
  144.9 64.2 %collective-permute-start.7 = (bf16[144,896]{1,0:T(8,128)(2,1)S(1)}, bf16[144,896]{1,0:T(8,128)(2,1)S(1)}, u32[]{:S(2)}, u32[]{:S(2)}) collective-permute-start(bf16[144,896]{1,0:T(8,128)(2,1)S(1)} %copy-done.3), channel_id=1, source_target_pairs={{0,32},{4,36},{8,40},{12,44},{16,48},{20,52},{24,56},{28,60},{32,0... | collective-permute-start | bytes 774152 | tf_op jit(solution)/shard_map/ppermute | solution.py:375
  158.8 93.8 %copy-start.4 = (bf16[144,896]{1,0:T(8,128)(2,1)}, bf16[144,896]{1,0:T(8,128)(2,1)S(1)}, u32[]{:S(2)}) copy-start(bf16[144,896]{1,0:T(8,128)(2,1)S(1)} %collective-permute-done.6.a3) | copy-start | bytes 774148
  158.8 68.5 %collective-permute-start.10 = (bf16[144,896]{1,0:T(8,128)(2,1)S(1)}, bf16[144,896]{1,0:T(8,128)(2,1)S(1)}, u32[]{:S(2)}, u32[]{:S(2)}) collective-permute-start(bf16[144,896]{1,0:T(8,128)(2,1)S(1)} %collective-permute-done.6.a3), channel_id=1, source_target_pairs={{0,32},{4,36},{8,40},{12,44},{16,48},{20,52},{24,56},{28,60},{32,0... | collective-permute-start | bytes 774152 | tf_op jit(solution)/shard_map/ppermute | solution.py:375
  175.4 77.2 %copy-start.5 = (bf16[144,896]{1,0:T(8,128)(2,1)}, bf16[144,896]{1,0:T(8,128)(2,1)S(1)}, u32[]{:S(2)}) copy-start(bf16[144,896]{1,0:T(8,128)(2,1)S(1)} %collective-permute-done.4.a1) | copy-start | bytes 774148
  175.4 66.1 %collective-permute-start.8 = (bf16[144,896]{1,0:T(8,128)(2,1)S(1)}, bf16[144,896]{1,0:T(8,128)(2,1)S(1)}, u32[]{:S(2)}, u32[]{:S(2)}) collective-permute-start(bf16[144,896]{1,0:T(8,128)(2,1)S(1)} %collective-permute-done.4.a1), channel_id=1, source_target_pairs={{0,32},{4,36},{8,40},{12,44},{16,48},{20,52},{24,56},{28,60},{32,0... | collective-permute-start | bytes 774152 | tf_op jit(solution)/shard_map/ppermute | solution.py:375
  188.9 63.7 %copy-start.6 = (bf16[144,896]{1,0:T(8,128)(2,1)}, bf16[144,896]{1,0:T(8,128)(2,1)S(1)}, u32[]{:S(2)}) copy-start(bf16[144,896]{1,0:T(8,128)(2,1)S(1)} %collective-permute-done.5.a2) | copy-start | bytes 774148
  188.9 63.7 %collective-permute-start.9 = (bf16[144,896]{1,0:T(8,128)(2,1)S(1)}, bf16[144,896]{1,0:T(8,128)(2,1)S(1)}, u32[]{:S(2)}, u32[]{:S(2)}) collective-permute-start(bf16[144,896]{1,0:T(8,128)(2,1)S(1)} %collective-permute-done.5.a2), channel_id=1, source_target_pairs={{0,32},{4,36},{8,40},{12,44},{16,48},{20,52},{24,56},{28,60},{32,0... | collective-permute-start | bytes 774152 | tf_op jit(solution)/shard_map/ppermute | solution.py:375
  209.1 43.5 %copy-start.7 = (bf16[144,896]{1,0:T(8,128)(2,1)}, bf16[144,896]{1,0:T(8,128)(2,1)S(1)}, u32[]{:S(2)}) copy-start(bf16[144,896]{1,0:T(8,128)(2,1)S(1)} %collective-permute-done.7.b0) | copy-start | bytes 774148
  227.3 25.3 %copy-start.8 = (bf16[144,896]{1,0:T(8,128)(2,1)}, bf16[144,896]{1,0:T(8,128)(2,1)S(1)}, u32[]{:S(2)}) copy-start(bf16[144,896]{1,0:T(8,128)(2,1)S(1)} %collective-permute-done.10.b3) | copy-start | bytes 774148
  241.5 11.1 %copy-start.9 = (bf16[144,896]{1,0:T(8,128)(2,1)}, bf16[144,896]{1,0:T(8,128)(2,1)S(1)}, u32[]{:S(2)}) copy-start(bf16[144,896]{1,0:T(8,128)(2,1)S(1)} %collective-permute-done.8.b1) | copy-start | bytes 774148
  252.6 0.7 copy-start.10
  262.5 80.5 %all-to-all-start.1 = ((bf16[32,96,896]{2,1,0:T(8,128)(2,1)}), bf16[32,96,896]{2,1,0:T(8,128)(2,1)}, u32[]{:S(2)}, u32[]{:S(2)}) async-start(bf16[32,96,896]{2,1,0:T(8,128)(2,1)} %bitcast.17), calls=%async_computation.1 | async-start | bytes 11010048 | tf_op jit(solution)/shard_map/all_to_all | solution.py:385
  269.9 73.1 %collective-permute-start.3 = (bf16[4,192,1024]{2,1,0:T(8,128)(2,1)S(1)}, bf16[4,192,1024]{2,1,0:T(8,128)(2,1)S(1)}, u32[]{:S(2)}, u32[]{:S(2)}) collective-permute-start(bf16[4,192,1024]{2,1,0:T(8,128)(2,1)S(1)} %slice.12), channel_id=1, source_target_pairs={{0,4},{4,0},{8,12},{12,8},{16,20},{20,16},{24,28},{28,24},{32,36},... | collective-permute-start | bytes 4718600 | tf_op jit(solution)/shard_map/ppermute | solution.py:394
  343.0 1.2 copy-start.1
Sparse Core Ops, SparseCore 0:
  136.6 124.3 all-gather.2

commit v3 on v2

v3 whole, which is shorter than its diff:
```python
import functools

import jax
import jax.numpy as jnp
from jax import lax
from jax.experimental import pallas as pl
from jax.experimental.pallas import tpu as pltpu
from jax.sharding import PartitionSpec as P

CAP = 6
F32 = jnp.float32
BF16 = jnp.bfloat16
VMEM_LIMIT = 56 * 1024 * 1024


def iota(shape, dim):
    return lax.broadcasted_iota(jnp.int32, shape, dim)


def floordiv(a, n):
    return jnp.floor((a.astype(F32) + 0.5) * (1.0 / n)).astype(jnp.int32)


def slot_keys(route, experts):
    tok = route.shape[1]
    column = route.T
    r0, r1 = route[0:1], route[1:2]
    c0, c1 = column[:, 0:1], column[:, 1:2]
    before = iota((tok, tok), 0) < iota((tok, tok), 1)

    def count(mask):
        return jnp.sum(jnp.where(mask, 1.0, 0.0), 0, keepdims=True)

    rank0 = count((c0 == r0) & before)
    rank1 = count(c0 == r1) + count((c1 == r1) & before)

    def key(r, rank):
        return jnp.where(rank < CAP, r * CAP + rank, experts * CAP + rank - CAP).astype(jnp.int32)

    return key(r0, rank0), key(r1, rank1)


def split_raw_kernel(place_ref, q0_ref, q1_ref, q2_ref, q3_ref, meta_ref, *out_refs):
    tok, part = q0_ref.shape
    note = jnp.concatenate([meta_ref[...], jnp.zeros_like(meta_ref)], 0).astype(BF16)
    note = jnp.concatenate([note, jnp.zeros((16, part - tok), BF16)], 1)
    for in_ref, out_ref in zip((q0_ref, q1_ref, q2_ref, q3_ref), out_refs):
        out_ref[0:tok, :] = in_ref[...]
        out_ref[tok:, :] = note


def split_raw(place, cotangent, meta):
    tok, width = cotangent.shape
    part = width // 4
    quarter = [pl.BlockSpec((tok, part), lambda i, s, d=d: (0, lax.rem(s[1] + d, 4))) for d in range(4)]
    return pl.pallas_call(
        split_raw_kernel,
        grid_spec=pltpu.PrefetchScalarGridSpec(
            num_scalar_prefetch=1,
            grid=(1,),
            in_specs=quarter + [pl.BlockSpec(meta.shape, lambda i, s: (0, 0))],
            out_specs=[pl.BlockSpec((tok + 16, part), lambda i, s: (0, 0))] * 4,
        ),
        out_shape=[jax.ShapeDtypeStruct((tok + 16, part), BF16)] * 4,
        compiler_params=pltpu.CompilerParams(vmem_limit_bytes=VMEM_LIMIT),
        name="split_raw",
    )(place, cotangent, cotangent, cotangent, cotangent, meta)


def pick(mask):
    return jnp.where(mask, 1.0, 0.0).astype(BF16)


def expert_of(dest, z):
    return (dest >> 3) * 16 + z * 8 + (dest & 7)


def fold_rows(place_ref, meta_ref, tokens_ref, out_ref, experts, begin):
    dests = out_ref.shape[0]
    part = tokens_ref.shape[1] // 4
    key0, key1 = slot_keys(meta_ref[...], experts)
    row = iota((dests * 8, 1), 0)
    jj = row & 7
    first = expert_of(row >> 3, place_ref[3]) * CAP

    def choose(slot):
        return pick((slot == key0) | (slot == key1))

    head = choose(jnp.where(jj < CAP, first + jj, -1))
    for k in range(3):
        tail = choose(jnp.where(jj >= CAP, first + 2 * k + jj - CAP, -1))
        right = [tokens_ref[:, i * part : (i + 1) * part] for i in (k, 3)]
        left, right = jnp.concatenate([head, tail], 1), jnp.concatenate(right, 0)
        rows = jnp.dot(left, right, preferred_element_type=F32).astype(BF16)
        out_ref[:, :, begin + k * part : begin + (k + 1) * part] = rows.reshape(dests, 8, part)


def pack_tokens_kernel(experts, place_ref, a_meta, b_meta, a_ref, b_ref, out_ref):
    dests = out_ref.shape[0]
    width = a_ref.shape[1]
    half, head = width // 2, 3 * width // 4
    slot = experts * CAP + iota((8, 1), 0)
    odd = (iota((dests, 1, 1), 0) & 1) == 1
    for source, (meta, in_ref) in enumerate(((a_meta, a_ref), (b_meta, b_ref))):
        fold_rows(place_ref, meta, in_ref, out_ref, experts, source * head)
        key0, key1 = slot_keys(meta[...], experts)
        left = pick((slot == key0) | (slot == key1))
        rows = jnp.dot(left, in_ref[...], preferred_element_type=F32)[None]
        first = 2 * head + source * half
        out_ref[:, :, first : first + half] = jnp.where(odd, rows[..., half:], rows[..., :half]).astype(BF16)


def pack_tokens(place, metas, tokens, experts):
    return pl.pallas_call(
        functools.partial(pack_tokens_kernel, experts),
        in_specs=[pl.BlockSpec(memory_space=pltpu.SMEM)] + [pl.BlockSpec(memory_space=pltpu.VMEM)] * 4,
        out_shape=jax.ShapeDtypeStruct((experts // 2, 8, 10 * tokens[0].shape[1] // 4), BF16),
        compiler_params=pltpu.CompilerParams(vmem_limit_bytes=VMEM_LIMIT),
        name="pack_tokens",
    )(place, *metas, *tokens)


def pack_scaled_kernel(experts, place_ref, near_ref, far_ref, out_ref):
    block, part = 2 * out_ref.shape[0], out_ref.shape[-1]
    extras = []
    tok = 128
    planes = 4
    span = planes * CAP
    first = pl.program_id(0) * block

    for source, raw in enumerate((near_ref, far_ref)):
        facts = []
        for p in range(planes):
            meta = raw[p, tok : tok + 16, 0:tok].astype(F32)
            gate0 = (meta[2:3] + meta[3:4]) + meta[4:5]
            gate1 = (meta[5:6] + meta[6:7]) + meta[7:8]
            facts.append((*slot_keys(meta[0:8], experts), gate0, gate1))
        right = jnp.concatenate([raw[p, 0:tok, :] for p in range(planes)], 0)

        def rows_of(slot, plane):
            lefts = []
            gate = jnp.zeros(slot.shape, F32)
            for p, (key0, key1, gate0, gate1) in enumerate(facts):
                mine = jnp.where(plane == p, slot, -1)
                hit0, hit1 = mine == key0, mine == key1
                both = jnp.where(hit0, gate0, 0.0) + jnp.where(hit1, gate1, 0.0)
                gate = gate + jnp.sum(both, 1, keepdims=True)
                lefts.append(pick(hit0 | hit1))
            rows = jnp.dot(jnp.concatenate(lefts, 1), right, preferred_element_type=F32)
            return (gate * rows).astype(BF16)

        row = iota((block * span, 1), 0)
        dest = floordiv(row, span)
        j = row - dest * span
        plane = floordiv(j, CAP)
        slot = expert_of(first + dest, place_ref[3]) * CAP + j - plane * CAP
        main = rows_of(slot, plane).reshape(block, span, part)
        out_ref[:, :, source * span : (source + 1) * span] = main.reshape(block // 2, 2, span, part)
        j = iota((span, 1), 0)
        plane = floordiv(j, CAP)
        extras.append(rows_of(experts * CAP + j - plane * CAP, plane))
    half = span // 2
    for core in range(2):
        extra = jnp.concatenate([e[core * half : (core + 1) * half] for e in extras], 0)
        out_ref[:, core, 2 * span :] = jnp.broadcast_to(extra[None], (block // 2, span, part))


def pack_scaled(place, near, far, experts):
    part = near.shape[-1]
    dests = experts // 2
    block = 8
    span = 4 * CAP
    return pl.pallas_call(
        functools.partial(pack_scaled_kernel, experts),
        grid_spec=pltpu.PrefetchScalarGridSpec(
            num_scalar_prefetch=1,
            grid=(dests // block,),
            in_specs=[pl.BlockSpec(near.shape, lambda g, s: (0, 0, 0))] * 2,
            out_specs=pl.BlockSpec((block // 2, 2, 3 * span, part), lambda g, s: (g, 0, 0, 0)),
        ),
        out_shape=jax.ShapeDtypeStruct((dests // 2, 2, 3 * span, part), BF16),
        compiler_params=pltpu.CompilerParams(vmem_limit_bytes=VMEM_LIMIT),
        name="pack_scaled",
    )(place, near, far)


def silu(v):
    return v / (1.0 + jnp.exp(-v))


def compact(senders):
    r, c = iota((senders * CAP, senders * 8), 0), iota((senders * CAP, senders * 8), 1)
    src = floordiv(r, CAP)
    s = r - src * CAP
    return src, s, c, pick(c == src * 8 + s)


def hidden_main_kernel(x_ref, w_ref, out_ref, rows_ref):
    senders = x_ref.shape[0]
    width = w_ref.shape[0]
    part = width // 4
    head = 3 * part

    @pl.when(pl.program_id(0) == 0)
    def _():
        src, s, c, choose = compact(senders)
        for source in range(2):
            x = x_ref[:, :, source * head : (source + 1) * head].reshape(senders * 8, head)
            first = source * senders * CAP
            into = slice(first, first + senders * CAP)
            rows_ref[into, 0:head] = jnp.dot(choose, x, preferred_element_type=F32).astype(BF16)
            tail = jnp.zeros((senders * CAP, part), F32)
            for k in range(3):
                mask = (c == src * 8 + CAP + s - 2 * k) & (s >= 2 * k) & (s < 2 * k + 2)
                tail = tail + jnp.dot(
                    pick(mask), x[:, k * part : (k + 1) * part], preferred_element_type=F32
                )
            rows_ref[into, head:] = tail.astype(BF16)

    v = jnp.dot(rows_ref[...], w_ref[...], preferred_element_type=F32)
    out_ref[...] = silu(v).astype(BF16)


def hidden_main(x, weight):
    senders = x.shape[0]
    width, hid = weight.shape
    count = 2 * senders * CAP
    block = 256
    return pl.pallas_call(
        hidden_main_kernel,
        grid=(hid // block,),
        in_specs=[
            pl.BlockSpec((senders, 8, 6 * width // 4), lambda n: (0, 0, 0)),
            pl.BlockSpec((width, block), lambda n: (0, n)),
        ],
        out_specs=pl.BlockSpec((count, block), lambda n: (0, n)),
        out_shape=jax.ShapeDtypeStruct((count, hid), BF16),
        scratch_shapes=[pltpu.VMEM((count, width), BF16)],
        compiler_params=pltpu.CompilerParams(vmem_limit_bytes=VMEM_LIMIT),
        name="hidden_main",
    )(x, weight)


def hidden_extra_kernel(place_ref, near_ref, far_ref, w_ref, out_ref, rows_ref):
    senders, _, width = near_ref.shape
    half = width // 2
    count = senders * CAP
    is_hot = place_ref[0] > 0

    @pl.when(is_hot & (pl.program_id(0) == 0))
    def _():
        choose = compact(senders)[-1]

        def put(x_ref, first):
            for source in range(2):
                x = x_ref[:, :, source * half : (source + 1) * half].reshape(senders * 8, half)
                rows = jnp.dot(choose, x, preferred_element_type=F32).astype(BF16)
                rows_ref[source * count : (source + 1) * count, first : first + half] = rows

        for core in range(2):

            @pl.when(place_ref[2] == core)
            def _():
                put(near_ref, core * half)
                put(far_ref, (1 - core) * half)

    @pl.when(is_hot)
    def _():
        v = jnp.dot(rows_ref[...], w_ref[...], preferred_element_type=F32)
        out_ref[...] = silu(v).astype(BF16)

    @pl.when(jnp.logical_not(is_hot))
    def _():
        out_ref[...] = jnp.zeros_like(out_ref)


def hidden_extra(place, near, far, weight):
    senders = near.shape[0]
    width, hid = weight.shape
    count = 2 * senders * CAP
    block = 256
    x_spec = pl.BlockSpec(near.shape, lambda n, s: (0, 0, 0))
    return pl.pallas_call(
        hidden_extra_kernel,
        grid_spec=pltpu.PrefetchScalarGridSpec(
            num_scalar_prefetch=1,
            grid=(hid // block,),
            in_specs=[x_spec, x_spec, pl.BlockSpec((width, block), lambda n, s: (0, n))],
            out_specs=pl.BlockSpec((count, block), lambda n, s: (0, n)),
            scratch_shapes=[pltpu.VMEM((count, width), BF16)],
        ),
        out_shape=jax.ShapeDtypeStruct((count, hid), BF16),
        compiler_params=pltpu.CompilerParams(vmem_limit_bytes=VMEM_LIMIT),
        name="hidden_extra",
    )(place, near, far, weight)


GROUP = 16


def by_plane(planes):
    n = GROUP * CAP
    rows = planes * 2 * n
    o, i = iota((rows, rows), 0), iota((rows, rows), 1)
    pair = floordiv(o, n)
    rest = o - pair * n
    plane, source = pair >> 1, pair & 1
    sender = floordiv(rest, CAP)
    return pick(i == ((sender * 2 + source) * planes + plane) * CAP + rest - sender * CAP)


def grad_kernel(place_ref, near_ref, far_ref, x0, x1, x2, x3, s_ref, here_ref, there_ref, out_ref, acc_ref):
    planes, _, _, hid = near_ref.shape
    part = s_ref.shape[-1]
    g = pl.program_id(0)

    def ordered(s, count):
        s = s.reshape(count * 2 * GROUP * CAP, part)
        return jnp.dot(by_plane(count), s, preferred_element_type=F32).astype(BF16)

    def total(hs, s):
        h = jnp.concatenate(hs, 0)
        return lax.dot_general(h, s, (((0,), (0,)), ((), ())), preferred_element_type=F32)

    sender = floordiv(iota((near_ref.shape[2], 1), 0), CAP)
    is_z = place_ref[3]
    even, odd = pick((sender & 1) == 0), pick((sender & 1) == 1)
    odd_z = [pick(((sender & 1) == 1) & (is_z == z)) for z in range(2)]

    def main():
        hs = []
        for d in range(planes):
            plane = place_ref[1] + planes - d
            other = lax.rem(plane + 1 - 2 * is_z, planes)
            plane = lax.rem(plane, planes)
            hs += [near_ref[plane, 0], far_ref[plane, 0] * even + far_ref[other, 0] * odd]
        return total(hs, ordered(s_ref[...], planes))

    @pl.when(g == 0)
    def _():
        acc_ref[...] = main()

    @pl.when(g > 0)
    def _():
        acc_ref[...] += main()

    for core in range(2):

        @pl.when((place_ref[0] > 0) & (place_ref[2] == core))
        def _():
            here, there = ordered(here_ref[...], planes // 2), ordered(there_ref[...], planes // 2)
            s = jnp.concatenate([there, here] if core else [here, there], 0)
            xs = (x0, x1, x2, x3)
            hs = []
            for d in range(planes):
                other = xs[d - 1][1] * odd_z[0] + xs[(d + 1) % planes][1] * odd_z[1]
                hs += [xs[d][0], xs[d][1] * even + other]
            acc_ref[...] += total(hs, s)

    @pl.when(g == pl.num_programs(0) - 1)
    def _():
        out_ref[...] = acc_ref[...].astype(out_ref.dtype)


def grad_of(place, hidden, extras, s, here, there):
    planes, _, hid = hidden.shape
    senders, span, part = here.shape
    n = GROUP * CAP
    hidden = hidden.reshape(planes, 2, -1, hid)
    h_specs = [pl.BlockSpec((planes, 1, n, hid), lambda g, s, i=i: (0, i, g, 0)) for i in range(2)]
    x_spec = pl.BlockSpec((2, n, hid), lambda g, s: (0, g, 0))
    half = pl.BlockSpec((GROUP, span, part), lambda g, s: (g, 0, 0))
    return pl.pallas_call(
        grad_kernel,
        grid_spec=pltpu.PrefetchScalarGridSpec(
            num_scalar_prefetch=1,
            grid=(senders // GROUP,),
            in_specs=h_specs
            + [x_spec] * 4
            + [pl.BlockSpec((GROUP, 2 * span, part), lambda g, s: (g, 0, 0)), half, half],
            out_specs=pl.BlockSpec((hid, part), lambda g, s: (0, 0)),
            scratch_shapes=[pltpu.VMEM((hid, part), F32)],
        ),
        out_shape=jax.ShapeDtypeStruct((hid, part), BF16),
        compiler_params=pltpu.CompilerParams(vmem_limit_bytes=VMEM_LIMIT),
        name="grad_of",
    )(place, hidden, hidden, *[x.reshape(2, -1, hid) for x in extras], s, here, there)


def join_kernel(in_ref, out_ref):
    out_ref[...] = in_ref[...].astype(F32)


def join(parts):
    planes, rows, part = parts.shape
    return pl.pallas_call(
        join_kernel,
        grid=(planes,),
        in_specs=[pl.BlockSpec((1, rows, part), lambda n: (n, 0, 0))],
        out_specs=pl.BlockSpec((1, rows, part), lambda n: (0, 0, n)),
        out_shape=jax.ShapeDtypeStruct((1, rows, planes * part), F32),
        compiler_params=pltpu.CompilerParams(vmem_limit_bytes=VMEM_LIMIT),
        name="join",
    )(parts)


def bf16_parts(x):
    high = lax.reduce_precision(x, 8, 7)
    mid = lax.reduce_precision(x - high, 8, 7)
    return [high, mid, x - high - mid]


def z_neighbours(experts, planes):
    pairs = []
    for e in range(experts):
        step = 0 if e & 1 == 0 else (1 if (e >> 3) & 1 else -1)
        pairs += [(e * planes + p, (e ^ 8) * planes + (p + step) % planes) for p in range(planes)]
    return pairs


def local(tokens, cotangent, routes, gates, gate_weight):
    experts = lax.axis_size("expert")
    planes = lax.axis_size("dp")
    me = lax.axis_index("expert")
    dp = lax.axis_index("dp")
    core = me & 1
    other_z = [(i, i ^ 8) for i in range(experts)]
    other_core = [(i, i ^ 1) for i in range(experts)]
    same_z = [[i for i in range(experts) if (i >> 3) & 1 == z] for z in range(2)]

    route_rows = routes.T.astype(F32)
    gate_rows = gates.T
    meta = jnp.concatenate(
        [route_rows, jnp.stack(bf16_parts(gate_rows[0])), jnp.stack(bf16_parts(gate_rows[1]))], 0
    )
    named = (routes.reshape(-1)[:, None] == jnp.arange(experts, dtype=jnp.int32)[None, :]).astype(F32)
    hot_expert = jnp.argmax(jnp.sum(named, 0)).astype(jnp.int32)
    hot = (hot_expert == me).astype(jnp.int32)
    place = jnp.stack([hot, dp, core, (me >> 3) & 1]).astype(jnp.int32)

    def dispatch(x):
        return lax.all_to_all(x, "expert", 0, 0, tiled=True, axis_index_groups=same_z)

    weight = gate_weight[0]

    either_z = z_neighbours(experts, planes)
    far_tokens = lax.ppermute(tokens, ("expert", "dp"), either_z)
    far_meta = lax.ppermute(meta, ("expert", "dp"), either_z)
    blocks = split_raw(place, cotangent, meta)
    far_tokens, far_meta, blocks = lax.optimization_barrier((far_tokens, far_meta, blocks))
    sent = pack_tokens(place, (meta, far_meta), (tokens, far_tokens), experts)
    arrived = dispatch(sent)

    raw = [blocks[0]]
    for d in range(1, planes):
        raw.append(lax.ppermute(blocks[d], "dp", [(i, (i + d) % planes) for i in range(planes)]))
    raw = jnp.stack(raw)
    far_raw = lax.ppermute(raw, "expert", other_z)
    scaled = pack_scaled(place, raw, far_raw, experts)
    arrived, scaled = lax.optimization_barrier((arrived, scaled))

    span = scaled.shape[-2] // 3
    scaled = dispatch(scaled.reshape(experts // 2, 3 * span, scaled.shape[-1]))

    hidden = hidden_main(arrived, weight)
    arrived, _ = lax.optimization_barrier((arrived, hidden))
    hidden = lax.all_gather(hidden, "dp")
    extra = arrived[:, :, 6 * arrived.shape[-1] // 10 :]
    far_extra = lax.ppermute(extra, "expert", other_core)
    own_extra = hidden_extra(place, extra, far_extra, weight)

    def share(z, c):
        def permutes(x):
            def shift(y, d):
                pairs = [
                    (e * planes + i, e * planes + (i + d) % planes)
                    for e in range(experts)
                    if (e >> 3) & 1 == z and e & 1 == c
                    for i in range(planes)
                ]
                return lax.ppermute(y, ("expert", "dp"), pairs)

            half = x.shape[0] // 2
            before, after = shift(x, 1), shift(x, -1)
            opposite = jnp.concatenate([shift(before[:half], 1), shift(after[half:], -1)], 0)
            return before, opposite, after

        return permutes

    table = [share(z, c) for z in range(2) for c in range(2)]
    extras = lax.switch(((hot_expert >> 3) & 1) * 2 + (hot_expert & 1), table, own_extra)

    scaled, own_extra, extras = lax.optimization_barrier((scaled, own_extra, extras))
    near_scaled = scaled[:, 2 * span :]
    far_scaled = lax.ppermute(near_scaled, "expert", other_core)
    extras = (own_extra, *extras)
    grad = grad_of(place, hidden, extras, scaled, near_scaled, far_scaled)
    hid = grad.shape[0] // planes
    grad = lax.all_to_all(grad.reshape(planes, hid, -1), "dp", 0, 0, tiled=True)
    return join(grad)


def solution(mesh):
    placed = (
        P(("expert", "dp"), None),
        P(("expert", "dp"), None),
        P(("expert", "dp"), None),
        P(("expert", "dp"), None),
        P("expert", None, None),
    )
    return jax.shard_map(
        local, mesh=mesh, in_specs=placed, out_specs=P("expert", "dp", None), check_vma=False
    )
```

time: 416 us -> 271 us (0.65)
  the two profiles are of different devices: /device:TPU:41 before, /device:TPU:64 now
where the time goes in v3:
time: 271 us; the launch traced here: 268 us
  waiting for transfers between devices  116 us (43%)
  blocking collectives  48.5 us (18%)
  Pallas kernels  46.6 us (17%)
  starting transfers between devices  30.6 us (11%)
  between operations  15.6 us (6%)
  local copies, waits for them, and re-layouts  8.04 us (3%)
  other arithmetic  3.1 us (1%)
    all_to_all x1, blocking collectives, local(): grad = lax.all_to_all(grad.reshape(planes, hid, -1), 'dp', 0, 0, tiled=True)  48.5 us
    all_gather x1, waiting for transfers between devices, local(): hidden = lax.all_gather(hidden, 'dp')  37.6 us
    all_to_all x2, waiting for transfers between devices, dispatch(): lax.all_to_all(x, 'expert', 0, 0, tiled=True, axis_index_groups=same_z)  24.9 us
    ppermute x1, waiting for transfers between devices, local(): far_raw = lax.ppermute(raw, 'expert', other_z)  24.6 us
    ppermute x3, waiting for transfers between devices, local(): lax.ppermute(blocks[d], 'dp', [(i, (i + d) % planes) for i in range(plane...  22.1 us
    all_to_all x2, starting transfers between devices, dispatch(): lax.all_to_all(x, 'expert', 0, 0, tiled=True, axis_index_groups=same_z)  14.9 us
    pallas_call x1, Pallas kernels, grad_of(): pl.pallas_call(grad_kernel, grid_spec=pltpu.PrefetchScalarGridSpec(num_sc...  11.1 us
    pallas_call x1, Pallas kernels, pack_scaled(): pl.pallas_call(functools.partial(pack_scaled_kernel, experts), grid_spec=...  8.85 us
  transfers between devices with their start and end apart: 15, of which 8 were waited for; matrix products, arithmetic and copies ran while one was open for 3% of the time, Pallas kernels for 10%

profile of v3, /device:TPU:64, one launch (start us, length us, event | category | flops | bytes accessed | tf_op | source)
XLA Modules:
  0.0 268.1 jit_solution(6922628480299743295)
XLA Ops:
  6.5 1.9 collective-permute-start.16
  8.5 0.7 convert_bitcast_fusion
  9.1 0.8 reduce-precision_subtract_fusion
  9.9 0.2 collective-permute-start.17
  10.1 0.8 copy.7
  10.9 0.1 eq.20
  11.0 0.1 convert_reduce_fusion
  11.2 0.7 iota_reduce_fusion
  12.6 0.6 pad_add_fusion.place_ref
  13.2 3.0 %split_raw.1 = (bf16[144,896]{1,0:T(8,128)(2,1)}, bf16[144,896]{1,0:T(8,128)(2,1)}, bf16[144,896]{1,0:T(8,128)(2,1)}, bf16[144,896]{1,0:T(8,128)(2,1)}) custom-call(s32[4]{0:T(128)} %pad_add_fusion.place_ref, bf16[128,3584]{1,0:T(8,128)(2,1)} %q3_ref.1, bf16[128,3584]{1,0:T(8,128)(2,1)} %q3_ref.1, bf16[128,3584]{1,0:T(8,128)(2,1)} %q3_ref.1, ...), custom_call_target="tpu_custom_call" | custom-call | tf_op jit(solution)/shard_map/split_raw/pallas_call | solution.py:56
  16.2 4.0 %collective-permute-done.17.b_meta = f32[8,128]{1,0:T(8,128)S(1)} collective-permute-done((f32[8,128]{1,0:T(8,128)S(1)}, f32[8,128]{1,0:T(8,128)S(1)}, u32[]{:S(2)}, u32[]{:S(2)}) %collective-permute-start.17) | collective-permute-done | bytes 4128 | tf_op jit(solution)/shard_map/ppermute | solution.py:448
  20.2 0.6 copy-done.7
  20.8 0.3 copy-done.4
  21.1 5.2 %pack_tokens.1 = bf16[32,8,8960]{2,1,0:T(8,128)(2,1)} custom-call(s32[4]{0:T(128)} %pad_add_fusion.place_ref, f32[8,128]{1,0:T(8,128)} %copy-done.6, f32[8,128]{1,0:T(8,128)} %copy-done.7, bf16[128,3584]{1,0:T(8,128)(2,1)} %a_ref.1, bf16[128,3584]{1,0:T(8,128)(2,1)} %copy-done.4), custom_call_target="tpu_custom_call" | custom-call | tf_op jit(solution)/shard_map/pack_tokens/pallas_call | solution.py:114
  26.3 7.6 %all-to-all-start = ((bf16[32,8,8960]{2,1,0:T(8,128)(2,1)}), bf16[32,8,8960]{2,1,0:T(8,128)(2,1)}, u32[]{:S(2)}, u32[]{:S(2)}) async-start(bf16[32,8,8960]{2,1,0:T(8,128)(2,1)} %pack_tokens.1), calls=%async_computation | async-start | bytes 9175040 | tf_op jit(solution)/shard_map/all_to_all | solution.py:442
  33.9 4.6 %collective-permute-start.18 = (bf16[144,896]{1,0:T(8,128)(2,1)S(1)}, bf16[144,896]{1,0:T(8,128)(2,1)S(1)}, u32[]{:S(2)}, u32[]{:S(2)}) collective-permute-start(bf16[144,896]{1,0:T(8,128)(2,1)S(1)} %copy-done.10), channel_id=1, source_target_pairs={{0,1},{1,2},{2,3},{3,0},{4,5},{5,6},{6,7},{7,4},{8,9},{9,10},{10,1... | collective-permute-start | bytes 774152 | tf_op jit(solution)/shard_map/ppermute | solution.py:456
  38.5 1.2 collective-permute-start.19
  39.6 2.7 %collective-permute-start.20 = (bf16[144,896]{1,0:T(8,128)(2,1)S(1)}, bf16[144,896]{1,0:T(8,128)(2,1)S(1)}, u32[]{:S(2)}, u32[]{:S(2)}) collective-permute-start(bf16[144,896]{1,0:T(8,128)(2,1)S(1)} %copy-done.8), channel_id=1, source_target_pairs={{0,3},{1,0},{2,1},{3,2},{4,7},{5,4},{6,5},{7,6},{8,11},{9,8},{10,9... | collective-permute-start | bytes 774152 | tf_op jit(solution)/shard_map/ppermute | solution.py:456
  42.3 13.4 %collective-permute-done.18 = bf16[144,896]{1,0:T(8,128)(2,1)S(1)} collective-permute-done((bf16[144,896]{1,0:T(8,128)(2,1)S(1)}, bf16[144,896]{1,0:T(8,128)(2,1)S(1)}, u32[]{:S(2)}, u32[]{:S(2)}) %collective-permute-start.18) | collective-permute-done | bytes 258080 | tf_op jit(solution)/shard_map/ppermute | solution.py:456
  55.7 6.9 %collective-permute-done.19 = bf16[144,896]{1,0:T(8,128)(2,1)S(1)} collective-permute-done((bf16[144,896]{1,0:T(8,128)(2,1)S(1)}, bf16[144,896]{1,0:T(8,128)(2,1)S(1)}, u32[]{:S(2)}, u32[]{:S(2)}) %collective-permute-start.19) | collective-permute-done | bytes 258080 | tf_op jit(solution)/shard_map/ppermute | solution.py:456
  62.6 1.8 collective-permute-done.20
  64.5 0.2 pad_maximum_fusion.4.near_ref
  64.6 0.1 collective-permute-start.21
  64.7 24.6 %collective-permute-done.21.far_ref = bf16[4,144,896]{2,1,0:T(8,128)(2,1)S(1)} collective-permute-done((bf16[4,144,896]{2,1,0:T(8,128)(2,1)S(1)}, bf16[4,144,896]{2,1,0:T(8,128)(2,1)S(1)}, u32[]{:S(2)}, u32[]{:S(2)}) %collective-permute-start.21) | collective-permute-done | bytes 1032224 | tf_op jit(solution)/shard_map/ppermute | solution.py:458
  89.4 1.0 copy-done.3
  90.4 8.9 %pack_scaled.1 = bf16[16,2,72,896]{3,2,1,0:T(8,128)(2,1)} custom-call(s32[4]{0:T(128)} %pad_add_fusion.place_ref, bf16[4,144,896]{2,1,0:T(8,128)(2,1)} %copy-done.2, bf16[4,144,896]{2,1,0:T(8,128)(2,1)} %copy-done.3), custom_call_target="tpu_custom_call" | custom-call | tf_op jit(solution)/shard_map/pack_scaled/pallas_call | solution.py:173
  99.2 7.3 %all-to-all-start.1 = ((bf16[32,72,896]{2,1,0:T(8,128)(2,1)}), bf16[32,72,896]{2,1,0:T(8,128)(2,1)}, u32[]{:S(2)}, u32[]{:S(2)}) async-start(bf16[32,72,896]{2,1,0:T(8,128)(2,1)} %bitcast.21), calls=%async_computation.1 | async-start | bytes 8257536 | tf_op jit(solution)/shard_map/all_to_all | solution.py:442
  106.5 0.0 all-gather.3.cloned.1.call-start
  106.5 8.8 %hidden_main.1 = bf16[384,1024]{1,0:T(8,128)(2,1)} custom-call(bf16[32,8,8960]{2,1,0:T(8,128)(2,1)} %all-to-all-done.x_ref, bf16[3584,1024]{1,0:T(8,128)(2,1)} %bitcast.19), custom_call_target="tpu_custom_call" | custom-call | tf_op jit(solution)/shard_map/hidden_main/pallas_call | solution.py:229
  115.4 1.6 slice.38.near_ref
  117.0 0.5 collective-permute-start.22
  118.9 2.3 collective-permute-done.22.far_ref
  121.2 5.6 %hidden_extra.1 = bf16[384,1024]{1,0:T(8,128)(2,1)S(1)} custom-call(s32[4]{0:T(128)} %pad_add_fusion.place_ref, bf16[32,8,3584]{2,1,0:T(8,128)(2,1)} %copy-done, bf16[32,8,3584]{2,1,0:T(8,128)(2,1)} %collective-permute-done.22.far_ref, bf16[3584,1024]{1,0:T(8,128)(2,1)} %bitcast.20), custom_call_target="tpu_custom_call" | custom-call | tf_op jit(solution)/shard_map/hidden_extra/pallas_call | solution.py:283
  126.8 6.8 %conditional.1 = (bf16[384,1024]{1,0:T(8,128)(2,1)}, bf16[384,1024]{1,0:T(8,128)(2,1)S(1)}, bf16[384,1024]{1,0:T(8,128)(2,1)}) conditional(s32[]{:T(128)} %clamp.3, bf16[384,1024]{1,0:T(8,128)(2,1)S(1)} %hidden_extra.1, bf16[384,1024]{1,0:T(8,128)(2,1)S(1)} %hidden_extra.1, ...), branch_computations={%region_2.3_spmd, %region_3.4_spmd, %region_4.5_spmd, %region_5.6_... | conditional | flops 1572864 | bytes 12583096 | solution.py:491
  126.8 1.6 collective-permute-start.10
  128.5 1.5 collective-permute-start.8
  130.0 1.1 slice.45
  131.1 0.7 collective-permute-start.11
  131.8 1.0 slice.44
  132.8 0.7 collective-permute-start.9
  133.5 0.1 pad_maximum_fusion.2
  133.6 24.9 %all-to-all-done.1.s_ref = bf16[32,72,896]{2,1,0:T(8,128)(2,1)} async-done(((bf16[32,72,896]{2,1,0:T(8,128)(2,1)}), bf16[32,72,896]{2,1,0:T(8,128)(2,1)}, u32[]{:S(2)}, u32[]{:S(2)}) %all-to-all-start.1) | async-done | bytes 4128800 | tf_op jit(solution)/shard_map/all_to_all | solution.py:442
  158.5 1.5 slice.39.here_ref
  160.0 0.1 collective-permute-start.23
  160.1 37.6 %all-gather.3.cloned.1.call-done = bf16[1536,1024]{1,0:T(8,128)(2,1)} async-done(((bf16[384,1024]{1,0:T(8,128)(2,1)}), bf16[1536,1024]{1,0:T(8,128)(2,1)}) %all-gather.3.cloned.1.call-update) | async-done | bytes 3145744 | tf_op jit(solution)/shard_map/all_gather | solution.py:467
  197.7 11.1 %grad_of.1 = bf16[1024,896]{1,0:T(8,128)(2,1)} custom-call(s32[4]{0:T(128)} %pad_add_fusion.place_ref, bf16[4,2,192,1024]{3,2,1,0:T(8,128)(2,1)} %bitcast.22, bf16[4,2,192,1024]{3,2,1,0:T(8,128)(2,1)} %bitcast.23, bf16[2,192,1024]{2,1,0:T(8,128)(2,1)S(1)} %bitcast.25, bf16[2,192,1024]{2,1,0:T(8,128)(2,1)} %bitcast.14.x1, bf16[2,192,1024]{2,1,0:T(8,128)(2,1)S(1)} %bitcast.26, ...), custom_call_target="tpu_custom_call" | custom-call | tf_op jit(solution)/shard_map/grad_of/pallas_call | solution.py:373
  208.8 48.5 %all_to_all.15.in_ref = bf16[4,256,896]{2,1,0:T(8,128)(2,1)} all-to-all(bf16[4,256,896]{2,1,0:T(8,128)(2,1)} %bitcast.24), channel_id=1, replica_groups=mesh['expert'=64,'dp'=4] {'dp'}, dimensions={0} | all-to-all | bytes 3670016 | tf_op jit(solution)/shard_map/all_to_all | solution.py:499
  257.2 4.0 %join.1 = f32[1,256,3584]{2,1,0:T(8,128)} custom-call(bf16[4,256,896]{2,1,0:T(8,128)(2,1)} %all_to_all.15.in_ref), custom_call_target="tpu_custom_call" | custom-call | tf_op jit(solution)/shard_map/join/pallas_call | solution.py:396
  (28 shorter events, 0.1 us)
Async XLA Ops:
  6.5 13.7 %collective-permute-start.16 = (bf16[128,3584]{1,0:T(8,128)(2,1)}, bf16[128,3584]{1,0:T(8,128)(2,1)S(1)}, u32[]{:S(2)}, u32[]{:S(2)}) collective-permute-start(bf16[128,3584]{1,0:T(8,128)(2,1)} %a_ref.1), channel_id=1, source_target_pairs={{0,32},{1,33},{2,34},{3,35},{4,39},{5,36},{6,37},{7,38},{8,40},{9,... | collective-permute-start | bytes 2752520 | tf_op jit(solution)/shard_map/ppermute | solution.py:447
  9.9 3.3 %copy-start.6 = (f32[8,128]{1,0:T(8,128)}, f32[8,128]{1,0:T(8,128)S(1)}, u32[]{:S(2)}) copy-start(f32[8,128]{1,0:T(8,128)S(1)} %concatenate.15.meta_ref.a_meta) | copy-start | bytes 12292
  9.9 10.3 %collective-permute-start.17 = (f32[8,128]{1,0:T(8,128)S(1)}, f32[8,128]{1,0:T(8,128)S(1)}, u32[]{:S(2)}, u32[]{:S(2)}) collective-permute-start(f32[8,128]{1,0:T(8,128)S(1)} %concatenate.15.meta_ref.a_meta), channel_id=1, source_target_pairs={{0,32},{1,33},{2,34},{3,35},{4,39},{5,36},{6,37},{7,38},{8,40},{9,... | collective-permute-start | bytes 12296 | tf_op jit(solution)/shard_map/ppermute | solution.py:448
  20.2 0.6 copy-start.7
  20.2 0.9 copy-start.4
  26.3 7.6 %copy-start.10 = (bf16[144,896]{1,0:T(8,128)(2,1)S(1)}, bf16[144,896]{1,0:T(8,128)(2,1)}, u32[]{:S(2)}) copy-start(bf16[144,896]{1,0:T(8,128)(2,1)} %get-tuple-element.39) | copy-start | bytes 774148
  26.3 12.2 %copy-start.9 = (bf16[144,896]{1,0:T(8,128)(2,1)S(1)}, bf16[144,896]{1,0:T(8,128)(2,1)}, u32[]{:S(2)}) copy-start(bf16[144,896]{1,0:T(8,128)(2,1)} %get-tuple-element.40) | copy-start | bytes 774148
  26.3 13.3 %copy-start.8 = (bf16[144,896]{1,0:T(8,128)(2,1)S(1)}, bf16[144,896]{1,0:T(8,128)(2,1)}, u32[]{:S(2)}) copy-start(bf16[144,896]{1,0:T(8,128)(2,1)} %get-tuple-element.41) | copy-start | bytes 774148
  26.3 38.2 %copy-start.5 = (bf16[144,896]{1,0:T(8,128)(2,1)S(1)}, bf16[144,896]{1,0:T(8,128)(2,1)}, u32[]{:S(2)}) copy-start(bf16[144,896]{1,0:T(8,128)(2,1)} %get-tuple-element.38) | copy-start | bytes 774148
  26.3 72.9 %all-to-all-start = ((bf16[32,8,8960]{2,1,0:T(8,128)(2,1)}), bf16[32,8,8960]{2,1,0:T(8,128)(2,1)}, u32[]{:S(2)}, u32[]{:S(2)}) async-start(bf16[32,8,8960]{2,1,0:T(8,128)(2,1)} %pack_tokens.1), calls=%async_computation | async-start | bytes 9175040 | tf_op jit(solution)/shard_map/all_to_all | solution.py:442
  33.9 21.8 %collective-permute-start.18 = (bf16[144,896]{1,0:T(8,128)(2,1)S(1)}, bf16[144,896]{1,0:T(8,128)(2,1)S(1)}, u32[]{:S(2)}, u32[]{:S(2)}) collective-permute-start(bf16[144,896]{1,0:T(8,128)(2,1)S(1)} %copy-done.10), channel_id=1, source_target_pairs={{0,1},{1,2},{2,3},{3,0},{4,5},{5,6},{6,7},{7,4},{8,9},{9,10},{10,1... | collective-permute-start | bytes 774152 | tf_op jit(solution)/shard_map/ppermute | solution.py:456
  38.5 24.1 %collective-permute-start.19 = (bf16[144,896]{1,0:T(8,128)(2,1)S(1)}, bf16[144,896]{1,0:T(8,128)(2,1)S(1)}, u32[]{:S(2)}, u32[]{:S(2)}) collective-permute-start(bf16[144,896]{1,0:T(8,128)(2,1)S(1)} %copy-done.9), channel_id=1, source_target_pairs={{0,2},{1,3},{2,0},{3,1},{4,6},{5,7},{6,4},{7,5},{8,10},{9,11},{10,... | collective-permute-start | bytes 774152 | tf_op jit(solution)/shard_map/ppermute | solution.py:456
  39.6 24.8 %collective-permute-start.20 = (bf16[144,896]{1,0:T(8,128)(2,1)S(1)}, bf16[144,896]{1,0:T(8,128)(2,1)S(1)}, u32[]{:S(2)}, u32[]{:S(2)}) collective-permute-start(bf16[144,896]{1,0:T(8,128)(2,1)S(1)} %copy-done.8), channel_id=1, source_target_pairs={{0,3},{1,0},{2,1},{3,2},{4,7},{5,4},{6,5},{7,6},{8,11},{9,8},{10,9... | collective-permute-start | bytes 774152 | tf_op jit(solution)/shard_map/ppermute | solution.py:456
  64.6 24.7 %copy-start.2 = (bf16[4,144,896]{2,1,0:T(8,128)(2,1)}, bf16[4,144,896]{2,1,0:T(8,128)(2,1)S(1)}, u32[]{:S(2)}) copy-start(bf16[4,144,896]{2,1,0:T(8,128)(2,1)S(1)} %pad_maximum_fusion.4.near_ref) | copy-start | bytes 3096580
  64.6 24.7 %collective-permute-start.21 = (bf16[4,144,896]{2,1,0:T(8,128)(2,1)S(1)}, bf16[4,144,896]{2,1,0:T(8,128)(2,1)S(1)}, u32[]{:S(2)}, u32[]{:S(2)}) collective-permute-start(bf16[4,144,896]{2,1,0:T(8,128)(2,1)S(1)} %pad_maximum_fusion.4.near_ref), channel_id=1, source_target_pairs={{0,32},{4,36},{8,40},{12,44},{16,48},{20,52},{24,56},{28,60},{32,0... | collective-permute-start | bytes 3096584 | tf_op jit(solution)/shard_map/ppermute | solution.py:458
  89.4 1.0 copy-start.3
  99.2 59.3 %all-to-all-start.1 = ((bf16[32,72,896]{2,1,0:T(8,128)(2,1)}), bf16[32,72,896]{2,1,0:T(8,128)(2,1)}, u32[]{:S(2)}, u32[]{:S(2)}) async-start(bf16[32,72,896]{2,1,0:T(8,128)(2,1)} %bitcast.21), calls=%async_computation.1 | async-start | bytes 8257536 | tf_op jit(solution)/shard_map/all_to_all | solution.py:442
  106.5 91.2 %all-gather.3.cloned.1.call-start = ((), (), s32[]{:S(2)}) async-start(), calls=%async_computation.3 | async-start | bytes 3932160 | tf_op jit(solution)/shard_map/all_gather | solution.py:467
  117.0 4.2 %copy-start = (bf16[32,8,3584]{2,1,0:T(8,128)(2,1)}, bf16[32,8,3584]{2,1,0:T(8,128)(2,1)S(1)}, u32[]{:S(2)}) copy-start(bf16[32,8,3584]{2,1,0:T(8,128)(2,1)S(1)} %slice.38.near_ref) | copy-start | bytes 5505028
  117.0 4.2 %collective-permute-start.22 = (bf16[32,8,3584]{2,1,0:T(8,128)(2,1)S(1)}, bf16[32,8,3584]{2,1,0:T(8,128)(2,1)}, u32[]{:S(2)}, u32[]{:S(2)}) collective-permute-start(bf16[32,8,3584]{2,1,0:T(8,128)(2,1)S(1)} %slice.38.near_ref), channel_id=1, source_target_pairs={{0,4},{4,0},{8,12},{12,8},{16,20},{20,16},{24,28},{28,24},{32,36},... | collective-permute-start | bytes 5505032 | tf_op jit(solution)/shard_map/ppermute | solution.py:469
  126.8 3.2 %collective-permute-start.10 = (bf16[384,1024]{1,0:T(8,128)(2,1)S(1)}, bf16[384,1024]{1,0:T(8,128)(2,1)}, u32[]{:S(2)}, u32[]{:S(2)}) collective-permute-start(bf16[384,1024]{1,0:T(8,128)(2,1)S(1)} %param.2), channel_id=1, source_target_pairs={{32,35},{33,32},{34,33},{35,34},{40,43},{41,40},{42,41},{43,42},{4... | collective-permute-start | bytes 2359304 | tf_op jit(solution)/shard_map/cond/branch_2_fun/ppermute | solution.py:481
  128.5 3.3 %collective-permute-start.8 = (bf16[384,1024]{1,0:T(8,128)(2,1)S(1)}, bf16[384,1024]{1,0:T(8,128)(2,1)}, u32[]{:S(2)}, u32[]{:S(2)}) collective-permute-start(bf16[384,1024]{1,0:T(8,128)(2,1)S(1)} %param.2), channel_id=1, source_target_pairs={{32,33},{33,34},{34,35},{35,32},{40,41},{41,42},{42,43},{43,40},{4... | collective-permute-start | bytes 2359304 | tf_op jit(solution)/shard_map/cond/branch_2_fun/ppermute | solution.py:481
  131.1 2.4 collective-permute-start.11
  132.8 0.7 collective-permute-start.9
  160.0 37.7 %copy-start.1 = (bf16[32,24,896]{2,1,0:T(8,128)(2,1)}, bf16[32,24,896]{2,1,0:T(8,128)(2,1)S(1)}, u32[]{:S(2)}) copy-start(bf16[32,24,896]{2,1,0:T(8,128)(2,1)S(1)} %slice.39.here_ref) | copy-start | bytes 4128772
  160.0 37.7 %collective-permute-start.23 = (bf16[32,24,896]{2,1,0:T(8,128)(2,1)S(1)}, bf16[32,24,896]{2,1,0:T(8,128)(2,1)}, u32[]{:S(2)}, u32[]{:S(2)}) collective-permute-start(bf16[32,24,896]{2,1,0:T(8,128)(2,1)S(1)} %slice.39.here_ref), channel_id=1, source_target_pairs={{0,4},{4,0},{8,12},{12,8},{16,20},{20,16},{24,28},{28,24},{32,36},... | collective-permute-start | bytes 4128776 | tf_op jit(solution)/shard_map/ppermute | solution.py:495
Sparse Core Ops, SparseCore 0:
  115.5 82.0 all-gather.2

commit v4 on v3

--- a/solution.py
+++ b/solution.py
@@ -21,7 +21,7 @@
     return jnp.floor((a.astype(F32) + 0.5) * (1.0 / n)).astype(jnp.int32)
 
 
-def slot_keys(route, experts):
+def slot_ranks(route):
     tok = route.shape[1]
     column = route.T
     r0, r1 = route[0:1], route[1:2]
@@ -31,18 +31,22 @@
     def count(mask):
         return jnp.sum(jnp.where(mask, 1.0, 0.0), 0, keepdims=True)
 
-    rank0 = count((c0 == r0) & before)
-    rank1 = count(c0 == r1) + count((c1 == r1) & before)
-
-    def key(r, rank):
-        return jnp.where(rank < CAP, r * CAP + rank, experts * CAP + rank - CAP).astype(jnp.int32)
-
-    return key(r0, rank0), key(r1, rank1)
+    return count((c0 == r0) & before), count(c0 == r1) + count((c1 == r1) & before)
+
+
+def slot_key(r, rank, experts):
+    return jnp.where(rank < CAP, r * CAP + rank, experts * CAP + rank - CAP).astype(jnp.int32)
+
+
+def slot_keys(route, experts):
+    rank0, rank1 = slot_ranks(route)
+    return slot_key(route[0:1], rank0, experts), slot_key(route[1:2], rank1, experts)
 
 
 def split_raw_kernel(place_ref, q0_ref, q1_ref, q2_ref, q3_ref, meta_ref, *out_refs):
     tok, part = q0_ref.shape
-    note = jnp.concatenate([meta_ref[...], jnp.zeros_like(meta_ref)], 0).astype(BF16)
+    ranks = jnp.concatenate([*slot_ranks(meta_ref[...]), jnp.zeros((6, tok), F32)], 0)
+    note = jnp.concatenate([meta_ref[...], ranks], 0).astype(BF16)
     note = jnp.concatenate([note, jnp.zeros((16, part - tok), BF16)], 1)
     for in_ref, out_ref in zip((q0_ref, q1_ref, q2_ref, q3_ref), out_refs):
         out_ref[0:tok, :] = in_ref[...]
@@ -120,7 +124,7 @@
     )(place, *metas, *tokens)
 
 
-def pack_scaled_kernel(experts, place_ref, near_ref, far_ref, out_ref):
+def pack_scaled_kernel(experts, place_ref, own_ref, moved_ref, far_own_ref, far_moved_ref, out_ref):
     block, part = 2 * out_ref.shape[0], out_ref.shape[-1]
     extras = []
     tok = 128
@@ -128,14 +132,16 @@
     span = planes * CAP
     first = pl.program_id(0) * block
 
-    for source, raw in enumerate((near_ref, far_ref)):
+    for source, (first_ref, others_ref) in enumerate(((own_ref, moved_ref), (far_own_ref, far_moved_ref))):
+        raws = [first_ref[...]] + [others_ref[p] for p in range(planes - 1)]
         facts = []
         for p in range(planes):
-            meta = raw[p, tok : tok + 16, 0:tok].astype(F32)
+            meta = raws[p][tok : tok + 16, 0:tok].astype(F32)
             gate0 = (meta[2:3] + meta[3:4]) + meta[4:5]
             gate1 = (meta[5:6] + meta[6:7]) + meta[7:8]
-            facts.append((*slot_keys(meta[0:8], experts), gate0, gate1))
-        right = jnp.concatenate([raw[p, 0:tok, :] for p in range(planes)], 0)
+            keys = [slot_key(meta[i : i + 1], meta[8 + i : 9 + i], experts) for i in range(2)]
+            facts.append((*keys, gate0, gate1))
+        right = jnp.concatenate([raw[0:tok, :] for raw in raws], 0)
 
         def rows_of(slot, plane):
             lefts = []
@@ -165,8 +171,8 @@
         out_ref[:, core, 2 * span :] = jnp.broadcast_to(extra[None], (block // 2, span, part))
 
 
-def pack_scaled(place, near, far, experts):
-    part = near.shape[-1]
+def pack_scaled(place, raws, experts):
+    part = raws[0].shape[-1]
     dests = experts // 2
     block = 8
     span = 4 * CAP
@@ -175,13 +181,13 @@
         grid_spec=pltpu.PrefetchScalarGridSpec(
             num_scalar_prefetch=1,
             grid=(dests // block,),
-            in_specs=[pl.BlockSpec(near.shape, lambda g, s: (0, 0, 0))] * 2,
+            in_specs=[pl.BlockSpec(r.shape, lambda g, s, n=r.ndim: (0,) * n) for r in raws],
             out_specs=pl.BlockSpec((block // 2, 2, 3 * span, part), lambda g, s: (g, 0, 0, 0)),
         ),
         out_shape=jax.ShapeDtypeStruct((dests // 2, 2, 3 * span, part), BF16),
         compiler_params=pltpu.CompilerParams(vmem_limit_bytes=VMEM_LIMIT),
         name="pack_scaled",
-    )(place, near, far)
+    )(place, *raws)
 
 
 def silu(v):
@@ -189,7 +195,7 @@
 
 
 def compact(senders):
-    r, c = iota((senders * CAP, senders * 8), 0), iota((senders * CAP, senders * 8), 1)
+    r, c = iota((senders * CAP, 1), 0), iota((senders * CAP, senders * 8), 1)
     src = floordiv(r, CAP)
     s = r - src * CAP
     return src, s, c, pick(c == src * 8 + s)
@@ -211,7 +217,8 @@
             rows_ref[into, 0:head] = jnp.dot(choose, x, preferred_element_type=F32).astype(BF16)
             tail = jnp.zeros((senders * CAP, part), F32)
             for k in range(3):
-                mask = (c == src * 8 + CAP + s - 2 * k) & (s >= 2 * k) & (s < 2 * k + 2)
+                held = (s >= 2 * k) & (s < 2 * k + 2)
+                mask = c == jnp.where(held, src * 8 + CAP + s - 2 * k, -1)
                 tail = tail + jnp.dot(
                     pick(mask), x[:, k * part : (k + 1) * part], preferred_element_type=F32
                 )
@@ -301,12 +308,13 @@
 def by_plane(planes):
     n = GROUP * CAP
     rows = planes * 2 * n
-    o, i = iota((rows, rows), 0), iota((rows, rows), 1)
+    o = iota((rows, 1), 0)
     pair = floordiv(o, n)
     rest = o - pair * n
     plane, source = pair >> 1, pair & 1
     sender = floordiv(rest, CAP)
-    return pick(i == ((sender * 2 + source) * planes + plane) * CAP + rest - sender * CAP)
+    origin = ((sender * 2 + source) * planes + plane) * CAP + rest - sender * CAP
+    return pick(iota((rows, rows), 1) == origin)
 
 
 def grad_kernel(place_ref, near_ref, far_ref, x0, x1, x2, x3, s_ref, here_ref, there_ref, out_ref, acc_ref):
@@ -454,9 +462,11 @@
     raw = [blocks[0]]
     for d in range(1, planes):
         raw.append(lax.ppermute(blocks[d], "dp", [(i, (i + d) % planes) for i in range(planes)]))
-    raw = jnp.stack(raw)
-    far_raw = lax.ppermute(raw, "expert", other_z)
-    scaled = pack_scaled(place, raw, far_raw, experts)
+    far_own = lax.ppermute(blocks[0], "expert", other_z)
+    far_own, raw = lax.optimization_barrier((far_own, raw))
+    moved = jnp.stack(raw[1:])
+    far_moved = lax.ppermute(moved, "expert", other_z)
+    scaled = pack_scaled(place, (blocks[0], moved, far_own, far_moved), experts)
     arrived, scaled = lax.optimization_barrier((arrived, scaled))
 
     span = scaled.shape[-2] // 3

time: 271 us -> 267 us (0.985)
  waiting for transfers between devices: 116 us -> 113 us
    ppermute x1 -> x2, waiting for transfers between devices: 24.6 us -> 23.1 us  [the longest x1 18.7 us: local(): far_moved = lax.ppermute(moved, 'expert', other_z)]
  transfers between devices with their start and end apart: 15 -> 16, of which waited for: 8 -> 9; matrix products, arithmetic and copies ran while one was open for 3% -> 3% of each run, Pallas kernels for 10% -> 9%
where the time goes in v4:
time: 267 us; the launch traced here: 264 us
  waiting for transfers between devices  113 us (42%)
  blocking collectives  48.3 us (18%)
  Pallas kernels  45.2 us (17%)
  starting transfers between devices  31.6 us (12%)
  between operations  15.6 us (6%)
  local copies, waits for them, and re-layouts  7.94 us (3%)
  other arithmetic  3.01 us (1%)
    all_to_all x1, blocking collectives, local(): grad = lax.all_to_all(grad.reshape(planes, hid, -1), 'dp', 0, 0, tiled=True)  48.3 us
    all_gather x1, waiting for transfers between devices, local(): hidden = lax.all_gather(hidden, 'dp')  37.3 us
    all_to_all x2, waiting for transfers between devices, dispatch(): lax.all_to_all(x, 'expert', 0, 0, tiled=True, axis_index_groups=same_z)  25 us
    ppermute x3, waiting for transfers between devices, local(): lax.ppermute(blocks[d], 'dp', [(i, (i + d) % planes) for i in range(plane...  21.2 us
    ppermute x1, waiting for transfers between devices, local(): far_moved = lax.ppermute(moved, 'expert', other_z)  18.7 us
    all_to_all x2, starting transfers between devices, dispatch(): lax.all_to_all(x, 'expert', 0, 0, tiled=True, axis_index_groups=same_z)  14.9 us
    pallas_call x1, Pallas kernels, grad_of(): pl.pallas_call(grad_kernel, grid_spec=pltpu.PrefetchScalarGridSpec(num_sc...  11.1 us
    pallas_call x1, Pallas kernels, hidden_main(): pl.pallas_call(hidden_main_kernel, grid=(hid // block,), in_specs=[pl.Blo...  8.85 us
  transfers between devices with their start and end apart: 16, of which 9 were waited for; matrix products, arithmetic and copies ran while one was open for 3% of the time, Pallas kernels for 9%

profile of v4, /device:TPU:64, one launch (start us, length us, event | category | flops | bytes accessed | tf_op | source)
XLA Modules:
  0.0 264.5 jit_solution(6288362304425263616)
XLA Ops:
  6.5 1.9 collective-permute-start.16
  8.5 0.7 convert_bitcast_fusion
  9.1 0.8 reduce-precision_subtract_fusion
  9.9 0.2 collective-permute-start.17
  10.1 0.8 copy.7
  10.9 0.1 eq.20
  11.0 0.1 convert_reduce_fusion
  11.2 0.7 iota_reduce_fusion
  12.6 0.6 pad_add_fusion.place_ref
  13.2 3.2 %split_raw.1 = (bf16[144,896]{1,0:T(8,128)(2,1)}, bf16[144,896]{1,0:T(8,128)(2,1)}, bf16[144,896]{1,0:T(8,128)(2,1)}, bf16[144,896]{1,0:T(8,128)(2,1)}) custom-call(s32[4]{0:T(128)} %pad_add_fusion.place_ref, bf16[128,3584]{1,0:T(8,128)(2,1)} %q3_ref.1, bf16[128,3584]{1,0:T(8,128)(2,1)} %q3_ref.1, bf16[128,3584]{1,0:T(8,128)(2,1)} %q3_ref.1, ...), custom_call_target="tpu_custom_call" | custom-call | tf_op jit(solution)/shard_map/split_raw/pallas_call | solution.py:60
  16.3 3.8 %collective-permute-done.17.b_meta = f32[8,128]{1,0:T(8,128)S(1)} collective-permute-done((f32[8,128]{1,0:T(8,128)S(1)}, f32[8,128]{1,0:T(8,128)S(1)}, u32[]{:S(2)}, u32[]{:S(2)}) %collective-permute-start.17) | collective-permute-done | bytes 4128 | tf_op jit(solution)/shard_map/ppermute | solution.py:456
  20.2 0.6 copy-done.8
  20.8 0.3 copy-done.3
  21.1 5.2 %pack_tokens.1 = bf16[32,8,8960]{2,1,0:T(8,128)(2,1)} custom-call(s32[4]{0:T(128)} %pad_add_fusion.place_ref, f32[8,128]{1,0:T(8,128)} %copy-done.7, f32[8,128]{1,0:T(8,128)} %copy-done.8, bf16[128,3584]{1,0:T(8,128)(2,1)} %a_ref.1, bf16[128,3584]{1,0:T(8,128)(2,1)} %copy-done.3), custom_call_target="tpu_custom_call" | custom-call | tf_op jit(solution)/shard_map/pack_tokens/pallas_call | solution.py:118
  26.4 7.6 %all-to-all-start = ((bf16[32,8,8960]{2,1,0:T(8,128)(2,1)}), bf16[32,8,8960]{2,1,0:T(8,128)(2,1)}, u32[]{:S(2)}, u32[]{:S(2)}) async-start(bf16[32,8,8960]{2,1,0:T(8,128)(2,1)} %pack_tokens.1), calls=%async_computation | async-start | bytes 9175040 | tf_op jit(solution)/shard_map/all_to_all | solution.py:450
  34.0 4.6 %collective-permute-start.19 = (bf16[144,896]{1,0:T(8,128)(2,1)S(1)}, bf16[144,896]{1,0:T(8,128)(2,1)S(1)}, u32[]{:S(2)}, u32[]{:S(2)}) collective-permute-start(bf16[144,896]{1,0:T(8,128)(2,1)S(1)} %copy-done.11), channel_id=1, source_target_pairs={{0,1},{1,2},{2,3},{3,0},{4,5},{5,6},{6,7},{7,4},{8,9},{9,10},{10,1... | collective-permute-start | bytes 774152 | tf_op jit(solution)/shard_map/ppermute | solution.py:464
  38.5 1.2 collective-permute-start.20
  39.7 2.7 %collective-permute-start.21 = (bf16[144,896]{1,0:T(8,128)(2,1)S(1)}, bf16[144,896]{1,0:T(8,128)(2,1)S(1)}, u32[]{:S(2)}, u32[]{:S(2)}) collective-permute-start(bf16[144,896]{1,0:T(8,128)(2,1)S(1)} %copy-done.9), channel_id=1, source_target_pairs={{0,3},{1,0},{2,1},{3,2},{4,7},{5,4},{6,5},{7,6},{8,11},{9,8},{10,9... | collective-permute-start | bytes 774152 | tf_op jit(solution)/shard_map/ppermute | solution.py:464
  42.4 1.0 collective-permute-start.18
  43.4 12.2 %collective-permute-done.19 = bf16[144,896]{1,0:T(8,128)(2,1)S(1)} collective-permute-done((bf16[144,896]{1,0:T(8,128)(2,1)S(1)}, bf16[144,896]{1,0:T(8,128)(2,1)S(1)}, u32[]{:S(2)}, u32[]{:S(2)}) %collective-permute-start.19) | collective-permute-done | bytes 258080 | tf_op jit(solution)/shard_map/ppermute | solution.py:464
  55.6 7.7 %collective-permute-done.20 = bf16[144,896]{1,0:T(8,128)(2,1)S(1)} collective-permute-done((bf16[144,896]{1,0:T(8,128)(2,1)S(1)}, bf16[144,896]{1,0:T(8,128)(2,1)S(1)}, u32[]{:S(2)}, u32[]{:S(2)}) %collective-permute-start.20) | collective-permute-done | bytes 258080 | tf_op jit(solution)/shard_map/ppermute | solution.py:464
  63.3 1.2 collective-permute-done.21
  64.6 4.5 %collective-permute-done.18.far_own_ref = bf16[144,896]{1,0:T(8,128)(2,1)S(1)} collective-permute-done((bf16[144,896]{1,0:T(8,128)(2,1)S(1)}, bf16[144,896]{1,0:T(8,128)(2,1)S(1)}, u32[]{:S(2)}, u32[]{:S(2)}) %collective-permute-start.18) | collective-permute-done | bytes 258080 | tf_op jit(solution)/shard_map/ppermute | solution.py:465
  69.0 0.1 pad_maximum_fusion.4.moved_ref
  69.2 0.1 collective-permute-start.22
  69.3 18.7 %collective-permute-done.22.far_moved_ref = bf16[3,144,896]{2,1,0:T(8,128)(2,1)S(1)} collective-permute-done((bf16[3,144,896]{2,1,0:T(8,128)(2,1)S(1)}, bf16[3,144,896]{2,1,0:T(8,128)(2,1)S(1)}, u32[]{:S(2)}, u32[]{:S(2)}) %collective-permute-start.22) | collective-permute-done | bytes 774176 | tf_op jit(solution)/shard_map/ppermute | solution.py:468
  87.9 0.9 copy-done.4
  88.8 7.2 %pack_scaled.1 = bf16[16,2,72,896]{3,2,1,0:T(8,128)(2,1)} custom-call(s32[4]{0:T(128)} %pad_add_fusion.place_ref, bf16[144,896]{1,0:T(8,128)(2,1)} %get-tuple-element.42.own_ref, bf16[3,144,896]{2,1,0:T(8,128)(2,1)} %copy-done.2, bf16[144,896]{1,0:T(8,128)(2,1)} %copy-done.6, bf16[3,144,896]{2,1,0:T(8,128)(2,1)} %copy-done.4), custom_call_target="tpu_custom_call" | custom-call | tf_op jit(solution)/shard_map/pack_scaled/pallas_call | solution.py:179
  96.0 7.3 %all-to-all-start.1 = ((bf16[32,72,896]{2,1,0:T(8,128)(2,1)}), bf16[32,72,896]{2,1,0:T(8,128)(2,1)}, u32[]{:S(2)}, u32[]{:S(2)}) async-start(bf16[32,72,896]{2,1,0:T(8,128)(2,1)} %bitcast.20), calls=%async_computation.1 | async-start | bytes 8257536 | tf_op jit(solution)/shard_map/all_to_all | solution.py:450
  103.4 8.8 %hidden_main.1 = bf16[384,1024]{1,0:T(8,128)(2,1)} custom-call(bf16[32,8,8960]{2,1,0:T(8,128)(2,1)} %all-to-all-done.x_ref, bf16[3584,1024]{1,0:T(8,128)(2,1)} %bitcast.18), custom_call_target="tpu_custom_call" | custom-call | tf_op jit(solution)/shard_map/hidden_main/pallas_call | solution.py:236
  112.3 1.6 slice.38.near_ref
  113.9 0.5 collective-permute-start.23
  115.8 2.3 collective-permute-done.23.far_ref
  118.1 5.6 %hidden_extra.1 = bf16[384,1024]{1,0:T(8,128)(2,1)S(1)} custom-call(s32[4]{0:T(128)} %pad_add_fusion.place_ref, bf16[32,8,3584]{2,1,0:T(8,128)(2,1)} %copy-done, bf16[32,8,3584]{2,1,0:T(8,128)(2,1)} %collective-permute-done.23.far_ref, bf16[3584,1024]{1,0:T(8,128)(2,1)} %bitcast.19), custom_call_target="tpu_custom_call" | custom-call | tf_op jit(solution)/shard_map/hidden_extra/pallas_call | solution.py:290
  123.7 6.7 %conditional.1 = (bf16[384,1024]{1,0:T(8,128)(2,1)}, bf16[384,1024]{1,0:T(8,128)(2,1)S(1)}, bf16[384,1024]{1,0:T(8,128)(2,1)}) conditional(s32[]{:T(128)} %clamp.3, bf16[384,1024]{1,0:T(8,128)(2,1)S(1)} %hidden_extra.1, bf16[384,1024]{1,0:T(8,128)(2,1)S(1)} %hidden_extra.1, ...), branch_computations={%region_2.3_spmd, %region_3.4_spmd, %region_4.5_spmd, %region_5.6_... | conditional | flops 1572864 | bytes 12583096 | solution.py:501
  123.7 1.6 collective-permute-start.10
  125.3 1.5 collective-permute-start.8
  126.8 1.1 slice.45
  127.9 0.7 collective-permute-start.11
  128.6 1.0 slice.44
  129.6 0.7 collective-permute-start.9
  130.4 25.0 %all-to-all-done.1.s_ref = bf16[32,72,896]{2,1,0:T(8,128)(2,1)} async-done(((bf16[32,72,896]{2,1,0:T(8,128)(2,1)}), bf16[32,72,896]{2,1,0:T(8,128)(2,1)}, u32[]{:S(2)}, u32[]{:S(2)}) %all-to-all-start.1) | async-done | bytes 4128800 | tf_op jit(solution)/shard_map/all_to_all | solution.py:450
  155.4 1.5 slice.39.here_ref
  156.8 0.1 collective-permute-start.24
  156.9 37.3 %all-gather.3.cloned.1.call-done = bf16[1536,1024]{1,0:T(8,128)(2,1)} async-done(((bf16[384,1024]{1,0:T(8,128)(2,1)}), bf16[1536,1024]{1,0:T(8,128)(2,1)}) %all-gather.3.cloned.1.call-update) | async-done | bytes 3145744 | tf_op jit(solution)/shard_map/all_gather | solution.py:477
  194.3 11.1 %grad_of.1 = bf16[1024,896]{1,0:T(8,128)(2,1)} custom-call(s32[4]{0:T(128)} %pad_add_fusion.place_ref, bf16[4,2,192,1024]{3,2,1,0:T(8,128)(2,1)} %bitcast.21, bf16[4,2,192,1024]{3,2,1,0:T(8,128)(2,1)} %bitcast.22, bf16[2,192,1024]{2,1,0:T(8,128)(2,1)S(1)} %bitcast.24, bf16[2,192,1024]{2,1,0:T(8,128)(2,1)} %bitcast.13.x1, bf16[2,192,1024]{2,1,0:T(8,128)(2,1)S(1)} %bitcast.25, ...), custom_call_target="tpu_custom_call" | custom-call | tf_op jit(solution)/shard_map/grad_of/pallas_call | solution.py:381
  205.3 48.3 %all_to_all.15.in_ref = bf16[4,256,896]{2,1,0:T(8,128)(2,1)} all-to-all(bf16[4,256,896]{2,1,0:T(8,128)(2,1)} %bitcast.23), channel_id=1, replica_groups=mesh['expert'=64,'dp'=4] {'dp'}, dimensions={0} | all-to-all | bytes 3670016 | tf_op jit(solution)/shard_map/all_to_all | solution.py:509
  253.6 4.0 %join.1 = f32[1,256,3584]{2,1,0:T(8,128)} custom-call(bf16[4,256,896]{2,1,0:T(8,128)(2,1)} %all_to_all.15.in_ref), custom_call_target="tpu_custom_call" | custom-call | tf_op jit(solution)/shard_map/join/pallas_call | solution.py:404
  (32 shorter events, 0.2 us)
Async XLA Ops:
  6.5 13.7 %collective-permute-start.16 = (bf16[128,3584]{1,0:T(8,128)(2,1)}, bf16[128,3584]{1,0:T(8,128)(2,1)S(1)}, u32[]{:S(2)}, u32[]{:S(2)}) collective-permute-start(bf16[128,3584]{1,0:T(8,128)(2,1)} %a_ref.1), channel_id=1, source_target_pairs={{0,32},{1,33},{2,34},{3,35},{4,39},{5,36},{6,37},{7,38},{8,40},{9,... | collective-permute-start | bytes 2752520 | tf_op jit(solution)/shard_map/ppermute | solution.py:455
  9.9 3.2 %copy-start.7 = (f32[8,128]{1,0:T(8,128)}, f32[8,128]{1,0:T(8,128)S(1)}, u32[]{:S(2)}) copy-start(f32[8,128]{1,0:T(8,128)S(1)} %concatenate.15.meta_ref.a_meta) | copy-start | bytes 12292
  9.9 10.3 %collective-permute-start.17 = (f32[8,128]{1,0:T(8,128)S(1)}, f32[8,128]{1,0:T(8,128)S(1)}, u32[]{:S(2)}, u32[]{:S(2)}) collective-permute-start(f32[8,128]{1,0:T(8,128)S(1)} %concatenate.15.meta_ref.a_meta), channel_id=1, source_target_pairs={{0,32},{1,33},{2,34},{3,35},{4,39},{5,36},{6,37},{7,38},{8,40},{9,... | collective-permute-start | bytes 12296 | tf_op jit(solution)/shard_map/ppermute | solution.py:456
  20.2 0.6 copy-start.8
  20.2 0.9 copy-start.3
  26.3 7.6 %copy-start.11 = (bf16[144,896]{1,0:T(8,128)(2,1)S(1)}, bf16[144,896]{1,0:T(8,128)(2,1)}, u32[]{:S(2)}) copy-start(bf16[144,896]{1,0:T(8,128)(2,1)} %get-tuple-element.43) | copy-start | bytes 774148
  26.3 12.2 %copy-start.10 = (bf16[144,896]{1,0:T(8,128)(2,1)S(1)}, bf16[144,896]{1,0:T(8,128)(2,1)}, u32[]{:S(2)}) copy-start(bf16[144,896]{1,0:T(8,128)(2,1)} %get-tuple-element.44) | copy-start | bytes 774148
  26.3 13.3 %copy-start.9 = (bf16[144,896]{1,0:T(8,128)(2,1)S(1)}, bf16[144,896]{1,0:T(8,128)(2,1)}, u32[]{:S(2)}) copy-start(bf16[144,896]{1,0:T(8,128)(2,1)} %get-tuple-element.45) | copy-start | bytes 774148
  26.3 16.0 %copy-start.5 = (bf16[144,896]{1,0:T(8,128)(2,1)S(1)}, bf16[144,896]{1,0:T(8,128)(2,1)}, u32[]{:S(2)}) copy-start(bf16[144,896]{1,0:T(8,128)(2,1)} %get-tuple-element.42.own_ref) | copy-start | bytes 774148
  26.4 69.7 %all-to-all-start = ((bf16[32,8,8960]{2,1,0:T(8,128)(2,1)}), bf16[32,8,8960]{2,1,0:T(8,128)(2,1)}, u32[]{:S(2)}, u32[]{:S(2)}) async-start(bf16[32,8,8960]{2,1,0:T(8,128)(2,1)} %pack_tokens.1), calls=%async_computation | async-start | bytes 9175040 | tf_op jit(solution)/shard_map/all_to_all | solution.py:450
  34.0 21.6 %collective-permute-start.19 = (bf16[144,896]{1,0:T(8,128)(2,1)S(1)}, bf16[144,896]{1,0:T(8,128)(2,1)S(1)}, u32[]{:S(2)}, u32[]{:S(2)}) collective-permute-start(bf16[144,896]{1,0:T(8,128)(2,1)S(1)} %copy-done.11), channel_id=1, source_target_pairs={{0,1},{1,2},{2,3},{3,0},{4,5},{5,6},{6,7},{7,4},{8,9},{9,10},{10,1... | collective-permute-start | bytes 774152 | tf_op jit(solution)/shard_map/ppermute | solution.py:464
  38.5 24.8 %collective-permute-start.20 = (bf16[144,896]{1,0:T(8,128)(2,1)S(1)}, bf16[144,896]{1,0:T(8,128)(2,1)S(1)}, u32[]{:S(2)}, u32[]{:S(2)}) collective-permute-start(bf16[144,896]{1,0:T(8,128)(2,1)S(1)} %copy-done.10), channel_id=1, source_target_pairs={{0,2},{1,3},{2,0},{3,1},{4,6},{5,7},{6,4},{7,5},{8,10},{9,11},{10,... | collective-permute-start | bytes 774152 | tf_op jit(solution)/shard_map/ppermute | solution.py:464
  39.7 24.9 %collective-permute-start.21 = (bf16[144,896]{1,0:T(8,128)(2,1)S(1)}, bf16[144,896]{1,0:T(8,128)(2,1)S(1)}, u32[]{:S(2)}, u32[]{:S(2)}) collective-permute-start(bf16[144,896]{1,0:T(8,128)(2,1)S(1)} %copy-done.9), channel_id=1, source_target_pairs={{0,3},{1,0},{2,1},{3,2},{4,7},{5,4},{6,5},{7,6},{8,11},{9,8},{10,9... | collective-permute-start | bytes 774152 | tf_op jit(solution)/shard_map/ppermute | solution.py:464
  42.4 26.7 %collective-permute-start.18 = (bf16[144,896]{1,0:T(8,128)(2,1)S(1)}, bf16[144,896]{1,0:T(8,128)(2,1)S(1)}, u32[]{:S(2)}, u32[]{:S(2)}) collective-permute-start(bf16[144,896]{1,0:T(8,128)(2,1)S(1)} %copy-done.5), channel_id=1, source_target_pairs={{0,32},{4,36},{8,40},{12,44},{16,48},{20,52},{24,56},{28,60},{32,0... | collective-permute-start | bytes 774152 | tf_op jit(solution)/shard_map/ppermute | solution.py:465
  69.0 18.9 %copy-start.6 = (bf16[144,896]{1,0:T(8,128)(2,1)}, bf16[144,896]{1,0:T(8,128)(2,1)S(1)}, u32[]{:S(2)}) copy-start(bf16[144,896]{1,0:T(8,128)(2,1)S(1)} %collective-permute-done.18.far_own_ref) | copy-start | bytes 774148
  69.1 18.8 %copy-start.2 = (bf16[3,144,896]{2,1,0:T(8,128)(2,1)}, bf16[3,144,896]{2,1,0:T(8,128)(2,1)S(1)}, u32[]{:S(2)}) copy-start(bf16[3,144,896]{2,1,0:T(8,128)(2,1)S(1)} %pad_maximum_fusion.4.moved_ref) | copy-start | bytes 2322436
  69.2 18.8 %collective-permute-start.22 = (bf16[3,144,896]{2,1,0:T(8,128)(2,1)S(1)}, bf16[3,144,896]{2,1,0:T(8,128)(2,1)S(1)}, u32[]{:S(2)}, u32[]{:S(2)}) collective-permute-start(bf16[3,144,896]{2,1,0:T(8,128)(2,1)S(1)} %pad_maximum_fusion.4.moved_ref), channel_id=1, source_target_pairs={{0,32},{4,36},{8,40},{12,44},{16,48},{20,52},{24,56},{28,60},{32,0... | collective-permute-start | bytes 2322440 | tf_op jit(solution)/shard_map/ppermute | solution.py:468
  87.9 0.9 copy-start.4
  96.0 59.3 %all-to-all-start.1 = ((bf16[32,72,896]{2,1,0:T(8,128)(2,1)}), bf16[32,72,896]{2,1,0:T(8,128)(2,1)}, u32[]{:S(2)}, u32[]{:S(2)}) async-start(bf16[32,72,896]{2,1,0:T(8,128)(2,1)} %bitcast.20), calls=%async_computation.1 | async-start | bytes 8257536 | tf_op jit(solution)/shard_map/all_to_all | solution.py:450
  103.3 90.9 %all-gather.3.cloned.1.call-start = ((), (), s32[]{:S(2)}) async-start(), calls=%async_computation.3 | async-start | bytes 3932160 | tf_op jit(solution)/shard_map/all_gather | solution.py:477
  113.9 4.2 %copy-start = (bf16[32,8,3584]{2,1,0:T(8,128)(2,1)}, bf16[32,8,3584]{2,1,0:T(8,128)(2,1)S(1)}, u32[]{:S(2)}) copy-start(bf16[32,8,3584]{2,1,0:T(8,128)(2,1)S(1)} %slice.38.near_ref) | copy-start | bytes 5505028
  113.9 4.2 %collective-permute-start.23 = (bf16[32,8,3584]{2,1,0:T(8,128)(2,1)S(1)}, bf16[32,8,3584]{2,1,0:T(8,128)(2,1)}, u32[]{:S(2)}, u32[]{:S(2)}) collective-permute-start(bf16[32,8,3584]{2,1,0:T(8,128)(2,1)S(1)} %slice.38.near_ref), channel_id=1, source_target_pairs={{0,4},{4,0},{8,12},{12,8},{16,20},{20,16},{24,28},{28,24},{32,36},... | collective-permute-start | bytes 5505032 | tf_op jit(solution)/shard_map/ppermute | solution.py:479
  123.7 3.1 %collective-permute-start.10 = (bf16[384,1024]{1,0:T(8,128)(2,1)S(1)}, bf16[384,1024]{1,0:T(8,128)(2,1)}, u32[]{:S(2)}, u32[]{:S(2)}) collective-permute-start(bf16[384,1024]{1,0:T(8,128)(2,1)S(1)} %param.2), channel_id=1, source_target_pairs={{32,35},{33,32},{34,33},{35,34},{40,43},{41,40},{42,41},{43,42},{4... | collective-permute-start | bytes 2359304 | tf_op jit(solution)/shard_map/cond/branch_2_fun/ppermute | solution.py:491
  125.3 3.3 %collective-permute-start.8 = (bf16[384,1024]{1,0:T(8,128)(2,1)S(1)}, bf16[384,1024]{1,0:T(8,128)(2,1)}, u32[]{:S(2)}, u32[]{:S(2)}) collective-permute-start(bf16[384,1024]{1,0:T(8,128)(2,1)S(1)} %param.2), channel_id=1, source_target_pairs={{32,33},{33,34},{34,35},{35,32},{40,41},{41,42},{42,43},{43,40},{4... | collective-permute-start | bytes 2359304 | tf_op jit(solution)/shard_map/cond/branch_2_fun/ppermute | solution.py:491
  127.9 2.4 collective-permute-start.11
  129.6 0.7 collective-permute-start.9
  156.8 37.5 %copy-start.1 = (bf16[32,24,896]{2,1,0:T(8,128)(2,1)}, bf16[32,24,896]{2,1,0:T(8,128)(2,1)S(1)}, u32[]{:S(2)}) copy-start(bf16[32,24,896]{2,1,0:T(8,128)(2,1)S(1)} %slice.39.here_ref) | copy-start | bytes 4128772
  156.8 37.4 %collective-permute-start.24 = (bf16[32,24,896]{2,1,0:T(8,128)(2,1)S(1)}, bf16[32,24,896]{2,1,0:T(8,128)(2,1)}, u32[]{:S(2)}, u32[]{:S(2)}) collective-permute-start(bf16[32,24,896]{2,1,0:T(8,128)(2,1)S(1)} %slice.39.here_ref), channel_id=1, source_target_pairs={{0,4},{4,0},{8,12},{12,8},{16,20},{20,16},{24,28},{28,24},{32,36},... | collective-permute-start | bytes 4128776 | tf_op jit(solution)/shard_map/ppermute | solution.py:505
Sparse Core Ops, SparseCore 0:
  112.4 81.8 all-gather.2

commit v5 on v4

--- a/solution.py
+++ b/solution.py
@@ -125,7 +125,7 @@
 
 
 def pack_scaled_kernel(experts, place_ref, own_ref, moved_ref, far_own_ref, far_moved_ref, out_ref):
-    block, part = 2 * out_ref.shape[0], out_ref.shape[-1]
+    block, _, part = out_ref.shape
     extras = []
     tok = 128
     planes = 4
@@ -161,14 +161,12 @@
         plane = floordiv(j, CAP)
         slot = expert_of(first + dest, place_ref[3]) * CAP + j - plane * CAP
         main = rows_of(slot, plane).reshape(block, span, part)
-        out_ref[:, :, source * span : (source + 1) * span] = main.reshape(block // 2, 2, span, part)
+        out_ref[:, source * span : (source + 1) * span] = main
         j = iota((span, 1), 0)
         plane = floordiv(j, CAP)
         extras.append(rows_of(experts * CAP + j - plane * CAP, plane))
-    half = span // 2
-    for core in range(2):
-        extra = jnp.concatenate([e[core * half : (core + 1) * half] for e in extras], 0)
-        out_ref[:, core, 2 * span :] = jnp.broadcast_to(extra[None], (block // 2, span, part))
+    extra = jnp.concatenate(extras, 0)
+    out_ref[:, 2 * span :] = jnp.broadcast_to(extra[None], (block, 2 * span, part))
 
 
 def pack_scaled(place, raws, experts):
@@ -182,9 +180,9 @@
             num_scalar_prefetch=1,
             grid=(dests // block,),
             in_specs=[pl.BlockSpec(r.shape, lambda g, s, n=r.ndim: (0,) * n) for r in raws],
-            out_specs=pl.BlockSpec((block // 2, 2, 3 * span, part), lambda g, s: (g, 0, 0, 0)),
+            out_specs=pl.BlockSpec((block, 4 * span, part), lambda g, s: (g, 0, 0)),
         ),
-        out_shape=jax.ShapeDtypeStruct((dests // 2, 2, 3 * span, part), BF16),
+        out_shape=jax.ShapeDtypeStruct((dests, 4 * span, part), BF16),
         compiler_params=pltpu.CompilerParams(vmem_limit_bytes=VMEM_LIMIT),
         name="pack_scaled",
     )(place, *raws)
@@ -302,7 +300,7 @@
     )(place, near, far, weight)
 
 
-GROUP = 16
+GROUP = 8
 
 
 def by_plane(planes):
@@ -317,14 +315,16 @@
     return pick(iota((rows, rows), 1) == origin)
 
 
-def grad_kernel(place_ref, near_ref, far_ref, x0, x1, x2, x3, s_ref, here_ref, there_ref, out_ref, acc_ref):
+def grad_kernel(place_ref, near_ref, far_ref, x0, x1, x2, x3, s_ref, sx_ref, out_ref, acc_ref):
     planes, _, _, hid = near_ref.shape
     part = s_ref.shape[-1]
     g = pl.program_id(0)
 
-    def ordered(s, count):
-        s = s.reshape(count * 2 * GROUP * CAP, part)
-        return jnp.dot(by_plane(count), s, preferred_element_type=F32).astype(BF16)
+    choose = by_plane(planes)
+
+    def ordered(s):
+        s = s.reshape(planes * 2 * GROUP * CAP, part)
+        return jnp.dot(choose, s, preferred_element_type=F32).astype(BF16)
 
     def total(hs, s):
         h = jnp.concatenate(hs, 0)
@@ -342,7 +342,7 @@
             other = lax.rem(plane + 1 - 2 * is_z, planes)
             plane = lax.rem(plane, planes)
             hs += [near_ref[plane, 0], far_ref[plane, 0] * even + far_ref[other, 0] * odd]
-        return total(hs, ordered(s_ref[...], planes))
+        return total(hs, ordered(s_ref[...]))
 
     @pl.when(g == 0)
     def _():
@@ -352,32 +352,28 @@
     def _():
         acc_ref[...] += main()
 
-    for core in range(2):
-
-        @pl.when((place_ref[0] > 0) & (place_ref[2] == core))
-        def _():
-            here, there = ordered(here_ref[...], planes // 2), ordered(there_ref[...], planes // 2)
-            s = jnp.concatenate([there, here] if core else [here, there], 0)
-            xs = (x0, x1, x2, x3)
-            hs = []
-            for d in range(planes):
-                other = xs[d - 1][1] * odd_z[0] + xs[(d + 1) % planes][1] * odd_z[1]
-                hs += [xs[d][0], xs[d][1] * even + other]
-            acc_ref[...] += total(hs, s)
+    @pl.when(place_ref[0] > 0)
+    def _():
+        xs = (x0, x1, x2, x3)
+        hs = []
+        for d in range(planes):
+            other = xs[d - 1][1] * odd_z[0] + xs[(d + 1) % planes][1] * odd_z[1]
+            hs += [xs[d][0], xs[d][1] * even + other]
+        acc_ref[...] += total(hs, ordered(sx_ref[...]))
 
     @pl.when(g == pl.num_programs(0) - 1)
     def _():
         out_ref[...] = acc_ref[...].astype(out_ref.dtype)
 
 
-def grad_of(place, hidden, extras, s, here, there):
+def grad_of(place, hidden, extras, s):
     planes, _, hid = hidden.shape
-    senders, span, part = here.shape
+    senders, span, part = s.shape
     n = GROUP * CAP
     hidden = hidden.reshape(planes, 2, -1, hid)
     h_specs = [pl.BlockSpec((planes, 1, n, hid), lambda g, s, i=i: (0, i, g, 0)) for i in range(2)]
     x_spec = pl.BlockSpec((2, n, hid), lambda g, s: (0, g, 0))
-    half = pl.BlockSpec((GROUP, span, part), lambda g, s: (g, 0, 0))
+    s_specs = [pl.BlockSpec((GROUP, span // 2, part), lambda g, s, i=i: (g, i, 0)) for i in range(2)]
     return pl.pallas_call(
         grad_kernel,
         grid_spec=pltpu.PrefetchScalarGridSpec(
@@ -385,14 +381,14 @@
             grid=(senders // GROUP,),
             in_specs=h_specs
             + [x_spec] * 4
-            + [pl.BlockSpec((GROUP, 2 * span, part), lambda g, s: (g, 0, 0)), half, half],
+            + s_specs,
             out_specs=pl.BlockSpec((hid, part), lambda g, s: (0, 0)),
             scratch_shapes=[pltpu.VMEM((hid, part), F32)],
         ),
         out_shape=jax.ShapeDtypeStruct((hid, part), BF16),
         compiler_params=pltpu.CompilerParams(vmem_limit_bytes=VMEM_LIMIT),
         name="grad_of",
-    )(place, hidden, hidden, *[x.reshape(2, -1, hid) for x in extras], s, here, there)
+    )(place, hidden, hidden, *[x.reshape(2, -1, hid) for x in extras], s, s)
 
 
 def join_kernel(in_ref, out_ref):
@@ -469,8 +465,7 @@
     scaled = pack_scaled(place, (blocks[0], moved, far_own, far_moved), experts)
     arrived, scaled = lax.optimization_barrier((arrived, scaled))
 
-    span = scaled.shape[-2] // 3
-    scaled = dispatch(scaled.reshape(experts // 2, 3 * span, scaled.shape[-1]))
+    scaled = dispatch(scaled)
 
     hidden = hidden_main(arrived, weight)
     arrived, _ = lax.optimization_barrier((arrived, hidden))
@@ -501,10 +496,8 @@
     extras = lax.switch(((hot_expert >> 3) & 1) * 2 + (hot_expert & 1), table, own_extra)
 
     scaled, own_extra, extras = lax.optimization_barrier((scaled, own_extra, extras))
-    near_scaled = scaled[:, 2 * span :]
-    far_scaled = lax.ppermute(near_scaled, "expert", other_core)
     extras = (own_extra, *extras)
-    grad = grad_of(place, hidden, extras, scaled, near_scaled, far_scaled)
+    grad = grad_of(place, hidden, extras, scaled)
     hid = grad.shape[0] // planes
     grad = lax.all_to_all(grad.reshape(planes, hid, -1), "dp", 0, 0, tiled=True)
     return join(grad)

time: 267 us -> 262 us (0.981)
  waiting for transfers between devices: 113 us -> 108 us
    all_gather x1, waiting for transfers between devices: 37.3 us -> 16.2 us  [local(): hidden = lax.all_gather(hidden, 'dp')]
    all_to_all x2, waiting for transfers between devices: 25 us -> 41.2 us  [dispatch(): lax.all_to_all(x, 'expert', 0, 0, tiled=True, axis_index_groups=same_z)]
  transfers between devices with their start and end apart: 16 -> 15, of which waited for: 9 -> 8; matrix products, arithmetic and copies ran while one was open for 3% -> 3% of each run, Pallas kernels for 9% -> 10%
where the time goes in v5:
time: 262 us; the launch traced here: 260 us
  waiting for transfers between devices  108 us (41%)
  blocking collectives  49.9 us (19%)
  Pallas kernels  45.8 us (17%)
  starting transfers between devices  31.5 us (12%)
  between operations  15.6 us (6%)
  local copies, waits for them, and re-layouts  6.45 us (2%)
  other arithmetic  3.03 us (1%)
    all_to_all x1, blocking collectives, local(): grad = lax.all_to_all(grad.reshape(planes, hid, -1), 'dp', 0, 0, tiled=True)  49.9 us
    all_to_all x2, waiting for transfers between devices, dispatch(): lax.all_to_all(x, 'expert', 0, 0, tiled=True, axis_index_groups=same_z)  41.2 us
    ppermute x3, waiting for transfers between devices, local(): lax.ppermute(blocks[d], 'dp', [(i, (i + d) % planes) for i in range(plane...  20.9 us
    ppermute x1, waiting for transfers between devices, local(): far_moved = lax.ppermute(moved, 'expert', other_z)  18.5 us
    all_gather x1, waiting for transfers between devices, local(): hidden = lax.all_gather(hidden, 'dp')  16.2 us
    all_to_all x2, starting transfers between devices, dispatch(): lax.all_to_all(x, 'expert', 0, 0, tiled=True, axis_index_groups=same_z)  14.9 us
    pallas_call x1, Pallas kernels, grad_of(): pl.pallas_call(grad_kernel, grid_spec=pltpu.PrefetchScalarGridSpec(num_sc...  11.3 us
    pallas_call x1, Pallas kernels, hidden_main(): pl.pallas_call(hidden_main_kernel, grid=(hid // block,), in_specs=[pl.Blo...  8.85 us
  transfers between devices with their start and end apart: 15, of which 8 were waited for; matrix products, arithmetic and copies ran while one was open for 3% of the time, Pallas kernels for 10%

profile of v5, /device:TPU:64, one launch (start us, length us, event | category | flops | bytes accessed | tf_op | source)
XLA Modules:
  0.0 260.1 jit_solution(10656310554802310036)
XLA Ops:
  6.5 1.9 collective-permute-start.16
  8.5 0.7 convert_bitcast_fusion
  9.1 0.8 reduce-precision_subtract_fusion
  9.9 0.2 collective-permute-start.17
  10.1 0.8 copy.7
  10.9 0.1 eq.20
  11.0 0.1 convert_reduce_fusion
  11.2 0.7 iota_reduce_fusion
  12.6 0.6 pad_add_fusion.place_ref
  13.2 3.1 %split_raw.1 = (bf16[144,896]{1,0:T(8,128)(2,1)}, bf16[144,896]{1,0:T(8,128)(2,1)}, bf16[144,896]{1,0:T(8,128)(2,1)}, bf16[144,896]{1,0:T(8,128)(2,1)}) custom-call(s32[4]{0:T(128)} %pad_add_fusion.place_ref, bf16[128,3584]{1,0:T(8,128)(2,1)} %q3_ref.1, bf16[128,3584]{1,0:T(8,128)(2,1)} %q3_ref.1, bf16[128,3584]{1,0:T(8,128)(2,1)} %q3_ref.1, ...), custom_call_target="tpu_custom_call" | custom-call | tf_op jit(solution)/shard_map/split_raw/pallas_call | solution.py:60
  16.3 3.9 %collective-permute-done.17.b_meta = f32[8,128]{1,0:T(8,128)S(1)} collective-permute-done((f32[8,128]{1,0:T(8,128)S(1)}, f32[8,128]{1,0:T(8,128)S(1)}, u32[]{:S(2)}, u32[]{:S(2)}) %collective-permute-start.17) | collective-permute-done | bytes 4128 | tf_op jit(solution)/shard_map/ppermute | solution.py:452
  20.2 0.6 copy-done.7
  20.8 0.3 copy-done.2
  21.1 5.2 %pack_tokens.1 = bf16[32,8,8960]{2,1,0:T(8,128)(2,1)} custom-call(s32[4]{0:T(128)} %pad_add_fusion.place_ref, f32[8,128]{1,0:T(8,128)} %copy-done.6, f32[8,128]{1,0:T(8,128)} %copy-done.7, bf16[128,3584]{1,0:T(8,128)(2,1)} %a_ref.1, bf16[128,3584]{1,0:T(8,128)(2,1)} %copy-done.2), custom_call_target="tpu_custom_call" | custom-call | tf_op jit(solution)/shard_map/pack_tokens/pallas_call | solution.py:118
  26.4 7.6 %all-to-all-start = ((bf16[32,8,8960]{2,1,0:T(8,128)(2,1)}), bf16[32,8,8960]{2,1,0:T(8,128)(2,1)}, u32[]{:S(2)}, u32[]{:S(2)}) async-start(bf16[32,8,8960]{2,1,0:T(8,128)(2,1)} %pack_tokens.1), calls=%async_computation | async-start | bytes 9175040 | tf_op jit(solution)/shard_map/all_to_all | solution.py:446
  34.0 2.0 collective-permute-start.18
  36.0 3.6 %collective-permute-start.19 = (bf16[144,896]{1,0:T(8,128)(2,1)S(1)}, bf16[144,896]{1,0:T(8,128)(2,1)S(1)}, u32[]{:S(2)}, u32[]{:S(2)}) collective-permute-start(bf16[144,896]{1,0:T(8,128)(2,1)S(1)} %copy-done.10), channel_id=1, source_target_pairs={{0,1},{1,2},{2,3},{3,0},{4,5},{5,6},{6,7},{7,4},{8,9},{9,10},{10,1... | collective-permute-start | bytes 774152 | tf_op jit(solution)/shard_map/ppermute | solution.py:460
  39.5 1.0 collective-permute-start.20
  40.5 2.8 %collective-permute-start.21 = (bf16[144,896]{1,0:T(8,128)(2,1)S(1)}, bf16[144,896]{1,0:T(8,128)(2,1)S(1)}, u32[]{:S(2)}, u32[]{:S(2)}) collective-permute-start(bf16[144,896]{1,0:T(8,128)(2,1)S(1)} %copy-done.8), channel_id=1, source_target_pairs={{0,3},{1,0},{2,1},{3,2},{4,7},{5,4},{6,5},{7,6},{8,11},{9,8},{10,9... | collective-permute-start | bytes 774152 | tf_op jit(solution)/shard_map/ppermute | solution.py:460
  43.4 4.7 %collective-permute-done.18.far_own_ref = bf16[144,896]{1,0:T(8,128)(2,1)S(1)} collective-permute-done((bf16[144,896]{1,0:T(8,128)(2,1)S(1)}, bf16[144,896]{1,0:T(8,128)(2,1)S(1)}, u32[]{:S(2)}, u32[]{:S(2)}) %collective-permute-start.18) | collective-permute-done | bytes 258080 | tf_op jit(solution)/shard_map/ppermute | solution.py:461
  48.1 9.2 %collective-permute-done.19 = bf16[144,896]{1,0:T(8,128)(2,1)S(1)} collective-permute-done((bf16[144,896]{1,0:T(8,128)(2,1)S(1)}, bf16[144,896]{1,0:T(8,128)(2,1)S(1)}, u32[]{:S(2)}, u32[]{:S(2)}) %collective-permute-start.19) | collective-permute-done | bytes 258080 | tf_op jit(solution)/shard_map/ppermute | solution.py:460
  57.3 11.7 %collective-permute-done.20 = bf16[144,896]{1,0:T(8,128)(2,1)S(1)} collective-permute-done((bf16[144,896]{1,0:T(8,128)(2,1)S(1)}, bf16[144,896]{1,0:T(8,128)(2,1)S(1)}, u32[]{:S(2)}, u32[]{:S(2)}) %collective-permute-start.20) | collective-permute-done | bytes 258080 | tf_op jit(solution)/shard_map/ppermute | solution.py:460
  69.0 0.1 pad_maximum_fusion.4.moved_ref
  69.1 0.1 collective-permute-start.22
  69.2 18.5 %collective-permute-done.22.far_moved_ref = bf16[3,144,896]{2,1,0:T(8,128)(2,1)S(1)} collective-permute-done((bf16[3,144,896]{2,1,0:T(8,128)(2,1)S(1)}, bf16[3,144,896]{2,1,0:T(8,128)(2,1)S(1)}, u32[]{:S(2)}, u32[]{:S(2)}) %collective-permute-start.22) | collective-permute-done | bytes 774176 | tf_op jit(solution)/shard_map/ppermute | solution.py:464
  87.7 0.9 copy-done.3
  88.5 7.4 %pack_scaled.1 = bf16[32,96,896]{2,1,0:T(8,128)(2,1)} custom-call(s32[4]{0:T(128)} %pad_add_fusion.place_ref, bf16[144,896]{1,0:T(8,128)(2,1)} %get-tuple-element.42.own_ref, bf16[3,144,896]{2,1,0:T(8,128)(2,1)} %copy-done.1, bf16[144,896]{1,0:T(8,128)(2,1)} %copy-done.5, bf16[3,144,896]{2,1,0:T(8,128)(2,1)} %copy-done.3), custom_call_target="tpu_custom_call" | custom-call | tf_op jit(solution)/shard_map/pack_scaled/pallas_call | solution.py:177
  96.0 7.3 %all-to-all-start.1 = ((bf16[32,96,896]{2,1,0:T(8,128)(2,1)}), bf16[32,96,896]{2,1,0:T(8,128)(2,1)}, u32[]{:S(2)}, u32[]{:S(2)}) async-start(bf16[32,96,896]{2,1,0:T(8,128)(2,1)} %pack_scaled.1), calls=%async_computation.1 | async-start | bytes 11010048 | tf_op jit(solution)/shard_map/all_to_all | solution.py:446
  103.3 0.0 all-gather.3.cloned.1.call-start
  103.3 8.8 %hidden_main.1 = bf16[384,1024]{1,0:T(8,128)(2,1)} custom-call(bf16[32,8,8960]{2,1,0:T(8,128)(2,1)} %all-to-all-done.x_ref, bf16[3584,1024]{1,0:T(8,128)(2,1)} %bitcast.17), custom_call_target="tpu_custom_call" | custom-call | tf_op jit(solution)/shard_map/hidden_main/pallas_call | solution.py:234
  112.2 0.0 all-gather.3.cloned.1.call-update
  112.2 1.6 slice.35.near_ref
  113.8 0.5 collective-permute-start.23
  115.7 2.3 collective-permute-done.23.far_ref
  118.0 5.9 %hidden_extra.1 = bf16[384,1024]{1,0:T(8,128)(2,1)S(1)} custom-call(s32[4]{0:T(128)} %pad_add_fusion.place_ref, bf16[32,8,3584]{2,1,0:T(8,128)(2,1)} %copy-done, bf16[32,8,3584]{2,1,0:T(8,128)(2,1)} %collective-permute-done.23.far_ref, bf16[3584,1024]{1,0:T(8,128)(2,1)} %bitcast.18), custom_call_target="tpu_custom_call" | custom-call | tf_op jit(solution)/shard_map/hidden_extra/pallas_call | solution.py:288
  123.9 6.7 %conditional.1 = (bf16[384,1024]{1,0:T(8,128)(2,1)}, bf16[384,1024]{1,0:T(8,128)(2,1)S(1)}, bf16[384,1024]{1,0:T(8,128)(2,1)}) conditional(s32[]{:T(128)} %clamp.3, bf16[384,1024]{1,0:T(8,128)(2,1)S(1)} %hidden_extra.1, bf16[384,1024]{1,0:T(8,128)(2,1)S(1)} %hidden_extra.1, ...), branch_computations={%region_2.3_spmd, %region_3.4_spmd, %region_4.5_spmd, %region_5.6_... | conditional | flops 1572864 | bytes 12583096 | solution.py:496
  123.9 1.6 collective-permute-start.12
  125.5 1.6 collective-permute-start.14
  127.0 1.0 slice.42
  128.1 0.7 collective-permute-start.13
  128.8 1.0 slice.43
  129.8 0.7 collective-permute-start.15
  130.5 0.1 pad_maximum_fusion.3
  130.6 41.2 %all-to-all-done.1.s_ref.sx_ref = bf16[32,96,896]{2,1,0:T(8,128)(2,1)} async-done(((bf16[32,96,896]{2,1,0:T(8,128)(2,1)}), bf16[32,96,896]{2,1,0:T(8,128)(2,1)}, u32[]{:S(2)}, u32[]{:S(2)}) %all-to-all-start.1) | async-done | bytes 5505056 | tf_op jit(solution)/shard_map/all_to_all | solution.py:446
  171.8 16.2 %all-gather.3.cloned.1.call-done = bf16[1536,1024]{1,0:T(8,128)(2,1)} async-done(((bf16[384,1024]{1,0:T(8,128)(2,1)}), bf16[1536,1024]{1,0:T(8,128)(2,1)}) %all-gather.3.cloned.1.call-update) | async-done | bytes 3145744 | tf_op jit(solution)/shard_map/all_gather | solution.py:472
  188.0 11.3 %grad_of.1 = bf16[1024,896]{1,0:T(8,128)(2,1)} custom-call(s32[4]{0:T(128)} %pad_add_fusion.place_ref, bf16[4,2,192,1024]{3,2,1,0:T(8,128)(2,1)} %bitcast.19, bf16[4,2,192,1024]{3,2,1,0:T(8,128)(2,1)} %bitcast.20, bf16[2,192,1024]{2,1,0:T(8,128)(2,1)S(1)} %bitcast.22, bf16[2,192,1024]{2,1,0:T(8,128)(2,1)} %bitcast.12.x1, bf16[2,192,1024]{2,1,0:T(8,128)(2,1)S(1)} %bitcast.23, ...), custom_call_target="tpu_custom_call" | custom-call | tf_op jit(solution)/shard_map/grad_of/pallas_call | solution.py:377
  199.3 49.9 %all_to_all.15.in_ref = bf16[4,256,896]{2,1,0:T(8,128)(2,1)} all-to-all(bf16[4,256,896]{2,1,0:T(8,128)(2,1)} %bitcast.21), channel_id=1, replica_groups=mesh['expert'=64,'dp'=4] {'dp'}, dimensions={0} | all-to-all | bytes 3670016 | tf_op jit(solution)/shard_map/all_to_all | solution.py:502
  249.2 4.0 %join.1 = f32[1,256,3584]{2,1,0:T(8,128)} custom-call(bf16[4,256,896]{2,1,0:T(8,128)(2,1)} %all_to_all.15.in_ref), custom_call_target="tpu_custom_call" | custom-call | tf_op jit(solution)/shard_map/join/pallas_call | solution.py:400
  (27 shorter events, 0.1 us)
Async XLA Ops:
  6.5 13.7 %collective-permute-start.16 = (bf16[128,3584]{1,0:T(8,128)(2,1)}, bf16[128,3584]{1,0:T(8,128)(2,1)S(1)}, u32[]{:S(2)}, u32[]{:S(2)}) collective-permute-start(bf16[128,3584]{1,0:T(8,128)(2,1)} %a_ref.1), channel_id=1, source_target_pairs={{0,32},{1,33},{2,34},{3,35},{4,39},{5,36},{6,37},{7,38},{8,40},{9,... | collective-permute-start | bytes 2752520 | tf_op jit(solution)/shard_map/ppermute | solution.py:451
  9.9 3.3 %copy-start.6 = (f32[8,128]{1,0:T(8,128)}, f32[8,128]{1,0:T(8,128)S(1)}, u32[]{:S(2)}) copy-start(f32[8,128]{1,0:T(8,128)S(1)} %concatenate.15.meta_ref.a_meta) | copy-start | bytes 12292
  9.9 10.3 %collective-permute-start.17 = (f32[8,128]{1,0:T(8,128)S(1)}, f32[8,128]{1,0:T(8,128)S(1)}, u32[]{:S(2)}, u32[]{:S(2)}) collective-permute-start(f32[8,128]{1,0:T(8,128)S(1)} %concatenate.15.meta_ref.a_meta), channel_id=1, source_target_pairs={{0,32},{1,33},{2,34},{3,35},{4,39},{5,36},{6,37},{7,38},{8,40},{9,... | collective-permute-start | bytes 12296 | tf_op jit(solution)/shard_map/ppermute | solution.py:452
  20.2 0.6 copy-start.7
  20.2 0.9 copy-start.2
  26.3 7.6 %copy-start.4 = (bf16[144,896]{1,0:T(8,128)(2,1)S(1)}, bf16[144,896]{1,0:T(8,128)(2,1)}, u32[]{:S(2)}) copy-start(bf16[144,896]{1,0:T(8,128)(2,1)} %get-tuple-element.42.own_ref) | copy-start | bytes 774148
  26.3 9.6 %copy-start.10 = (bf16[144,896]{1,0:T(8,128)(2,1)S(1)}, bf16[144,896]{1,0:T(8,128)(2,1)}, u32[]{:S(2)}) copy-start(bf16[144,896]{1,0:T(8,128)(2,1)} %get-tuple-element.43) | copy-start | bytes 774148
  26.3 13.2 %copy-start.9 = (bf16[144,896]{1,0:T(8,128)(2,1)S(1)}, bf16[144,896]{1,0:T(8,128)(2,1)}, u32[]{:S(2)}) copy-start(bf16[144,896]{1,0:T(8,128)(2,1)} %get-tuple-element.44) | copy-start | bytes 774148
  26.3 14.2 %copy-start.8 = (bf16[144,896]{1,0:T(8,128)(2,1)S(1)}, bf16[144,896]{1,0:T(8,128)(2,1)}, u32[]{:S(2)}) copy-start(bf16[144,896]{1,0:T(8,128)(2,1)} %get-tuple-element.45) | copy-start | bytes 774148
  26.4 69.6 %all-to-all-start = ((bf16[32,8,8960]{2,1,0:T(8,128)(2,1)}), bf16[32,8,8960]{2,1,0:T(8,128)(2,1)}, u32[]{:S(2)}, u32[]{:S(2)}) async-start(bf16[32,8,8960]{2,1,0:T(8,128)(2,1)} %pack_tokens.1), calls=%async_computation | async-start | bytes 9175040 | tf_op jit(solution)/shard_map/all_to_all | solution.py:446
  34.0 14.1 %collective-permute-start.18 = (bf16[144,896]{1,0:T(8,128)(2,1)S(1)}, bf16[144,896]{1,0:T(8,128)(2,1)S(1)}, u32[]{:S(2)}, u32[]{:S(2)}) collective-permute-start(bf16[144,896]{1,0:T(8,128)(2,1)S(1)} %copy-done.4), channel_id=1, source_target_pairs={{0,32},{4,36},{8,40},{12,44},{16,48},{20,52},{24,56},{28,60},{32,0... | collective-permute-start | bytes 774152 | tf_op jit(solution)/shard_map/ppermute | solution.py:461
  36.0 21.3 %collective-permute-start.19 = (bf16[144,896]{1,0:T(8,128)(2,1)S(1)}, bf16[144,896]{1,0:T(8,128)(2,1)S(1)}, u32[]{:S(2)}, u32[]{:S(2)}) collective-permute-start(bf16[144,896]{1,0:T(8,128)(2,1)S(1)} %copy-done.10), channel_id=1, source_target_pairs={{0,1},{1,2},{2,3},{3,0},{4,5},{5,6},{6,7},{7,4},{8,9},{9,10},{10,1... | collective-permute-start | bytes 774152 | tf_op jit(solution)/shard_map/ppermute | solution.py:460
  39.5 29.4 %collective-permute-start.20 = (bf16[144,896]{1,0:T(8,128)(2,1)S(1)}, bf16[144,896]{1,0:T(8,128)(2,1)S(1)}, u32[]{:S(2)}, u32[]{:S(2)}) collective-permute-start(bf16[144,896]{1,0:T(8,128)(2,1)S(1)} %copy-done.9), channel_id=1, source_target_pairs={{0,2},{1,3},{2,0},{3,1},{4,6},{5,7},{6,4},{7,5},{8,10},{9,11},{10,... | collective-permute-start | bytes 774152 | tf_op jit(solution)/shard_map/ppermute | solution.py:460
  40.5 28.4 %collective-permute-start.21 = (bf16[144,896]{1,0:T(8,128)(2,1)S(1)}, bf16[144,896]{1,0:T(8,128)(2,1)S(1)}, u32[]{:S(2)}, u32[]{:S(2)}) collective-permute-start(bf16[144,896]{1,0:T(8,128)(2,1)S(1)} %copy-done.8), channel_id=1, source_target_pairs={{0,3},{1,0},{2,1},{3,2},{4,7},{5,4},{6,5},{7,6},{8,11},{9,8},{10,9... | collective-permute-start | bytes 774152 | tf_op jit(solution)/shard_map/ppermute | solution.py:460
  48.1 39.6 %copy-start.5 = (bf16[144,896]{1,0:T(8,128)(2,1)}, bf16[144,896]{1,0:T(8,128)(2,1)S(1)}, u32[]{:S(2)}) copy-start(bf16[144,896]{1,0:T(8,128)(2,1)S(1)} %collective-permute-done.18.far_own_ref) | copy-start | bytes 774148
  69.1 18.6 %copy-start.1 = (bf16[3,144,896]{2,1,0:T(8,128)(2,1)}, bf16[3,144,896]{2,1,0:T(8,128)(2,1)S(1)}, u32[]{:S(2)}) copy-start(bf16[3,144,896]{2,1,0:T(8,128)(2,1)S(1)} %pad_maximum_fusion.4.moved_ref) | copy-start | bytes 2322436
  69.1 18.6 %collective-permute-start.22 = (bf16[3,144,896]{2,1,0:T(8,128)(2,1)S(1)}, bf16[3,144,896]{2,1,0:T(8,128)(2,1)S(1)}, u32[]{:S(2)}, u32[]{:S(2)}) collective-permute-start(bf16[3,144,896]{2,1,0:T(8,128)(2,1)S(1)} %pad_maximum_fusion.4.moved_ref), channel_id=1, source_target_pairs={{0,32},{4,36},{8,40},{12,44},{16,48},{20,52},{24,56},{28,60},{32,0... | collective-permute-start | bytes 2322440 | tf_op jit(solution)/shard_map/ppermute | solution.py:464
  87.7 0.9 copy-start.3
  96.0 75.8 %all-to-all-start.1 = ((bf16[32,96,896]{2,1,0:T(8,128)(2,1)}), bf16[32,96,896]{2,1,0:T(8,128)(2,1)}, u32[]{:S(2)}, u32[]{:S(2)}) async-start(bf16[32,96,896]{2,1,0:T(8,128)(2,1)} %pack_scaled.1), calls=%async_computation.1 | async-start | bytes 11010048 | tf_op jit(solution)/shard_map/all_to_all | solution.py:446
  103.3 84.7 %all-gather.3.cloned.1.call-start = ((), (), s32[]{:S(2)}) async-start(), calls=%async_computation.3 | async-start | bytes 3932160 | tf_op jit(solution)/shard_map/all_gather | solution.py:472
  113.8 4.2 %copy-start = (bf16[32,8,3584]{2,1,0:T(8,128)(2,1)}, bf16[32,8,3584]{2,1,0:T(8,128)(2,1)S(1)}, u32[]{:S(2)}) copy-start(bf16[32,8,3584]{2,1,0:T(8,128)(2,1)S(1)} %slice.35.near_ref) | copy-start | bytes 5505028
  113.8 4.2 %collective-permute-start.23 = (bf16[32,8,3584]{2,1,0:T(8,128)(2,1)S(1)}, bf16[32,8,3584]{2,1,0:T(8,128)(2,1)}, u32[]{:S(2)}, u32[]{:S(2)}) collective-permute-start(bf16[32,8,3584]{2,1,0:T(8,128)(2,1)S(1)} %slice.35.near_ref), channel_id=1, source_target_pairs={{0,4},{4,0},{8,12},{12,8},{16,20},{20,16},{24,28},{28,24},{32,36},... | collective-permute-start | bytes 5505032 | tf_op jit(solution)/shard_map/ppermute | solution.py:474
  123.9 3.1 %collective-permute-start.12 = (bf16[384,1024]{1,0:T(8,128)(2,1)S(1)}, bf16[384,1024]{1,0:T(8,128)(2,1)}, u32[]{:S(2)}, u32[]{:S(2)}) collective-permute-start(bf16[384,1024]{1,0:T(8,128)(2,1)S(1)} %param.3), channel_id=1, source_target_pairs={{36,37},{37,38},{38,39},{39,36},{44,45},{45,46},{46,47},{47,44},{5... | collective-permute-start | bytes 2359304 | tf_op jit(solution)/shard_map/cond/branch_3_fun/ppermute | solution.py:486
  125.5 3.3 %collective-permute-start.14 = (bf16[384,1024]{1,0:T(8,128)(2,1)S(1)}, bf16[384,1024]{1,0:T(8,128)(2,1)}, u32[]{:S(2)}, u32[]{:S(2)}) collective-permute-start(bf16[384,1024]{1,0:T(8,128)(2,1)S(1)} %param.3), channel_id=1, source_target_pairs={{36,39},{37,36},{38,37},{39,38},{44,47},{45,44},{46,45},{47,46},{5... | collective-permute-start | bytes 2359304 | tf_op jit(solution)/shard_map/cond/branch_3_fun/ppermute | solution.py:486
  128.1 2.4 collective-permute-start.13
  129.8 0.7 collective-permute-start.15
Sparse Core Ops, SparseCore 0:
  112.3 75.6 all-gather.2

commit v6 on v5

--- a/solution.py
+++ b/solution.py
@@ -79,10 +79,10 @@
     return (dest >> 3) * 16 + z * 8 + (dest & 7)
 
 
-def fold_rows(place_ref, meta_ref, tokens_ref, out_ref, experts, begin):
+def fold_rows(place_ref, keys, tokens_ref, out_ref, begin):
     dests = out_ref.shape[0]
     part = tokens_ref.shape[1] // 4
-    key0, key1 = slot_keys(meta_ref[...], experts)
+    key0, key1 = keys
     row = iota((dests * 8, 1), 0)
     jj = row & 7
     first = expert_of(row >> 3, place_ref[3]) * CAP
@@ -106,8 +106,8 @@
     slot = experts * CAP + iota((8, 1), 0)
     odd = (iota((dests, 1, 1), 0) & 1) == 1
     for source, (meta, in_ref) in enumerate(((a_meta, a_ref), (b_meta, b_ref))):
-        fold_rows(place_ref, meta, in_ref, out_ref, experts, source * head)
         key0, key1 = slot_keys(meta[...], experts)
+        fold_rows(place_ref, (key0, key1), in_ref, out_ref, source * head)
         left = pick((slot == key0) | (slot == key1))
         rows = jnp.dot(left, in_ref[...], preferred_element_type=F32)[None]
         first = 2 * head + source * half
@@ -399,9 +399,9 @@
     planes, rows, part = parts.shape
     return pl.pallas_call(
         join_kernel,
-        grid=(planes,),
-        in_specs=[pl.BlockSpec((1, rows, part), lambda n: (n, 0, 0))],
-        out_specs=pl.BlockSpec((1, rows, part), lambda n: (0, 0, n)),
+        grid=(planes, 2),
+        in_specs=[pl.BlockSpec((1, rows // 2, part), lambda n, h: (n, h, 0))],
+        out_specs=pl.BlockSpec((1, rows // 2, part), lambda n, h: (0, h, n)),
         out_shape=jax.ShapeDtypeStruct((1, rows, planes * part), F32),
         compiler_params=pltpu.CompilerParams(vmem_limit_bytes=VMEM_LIMIT),
         name="join",

time: 262 us -> 265 us (1.011)
  no operation moved by 1% of the time
where the time goes in v6:
time: 265 us; the launch traced here: 262 us
  waiting for transfers between devices  108 us (41%)
  blocking collectives  50.4 us (19%)
  Pallas kernels  47.7 us (18%)
  starting transfers between devices  31.5 us (12%)
  between operations  15.6 us (6%)
  local copies, waits for them, and re-layouts  6.45 us (2%)
  other arithmetic  3.03 us (1%)
    all_to_all x1, blocking collectives, local(): grad = lax.all_to_all(grad.reshape(planes, hid, -1), 'dp', 0, 0, tiled=True)  50.4 us
    all_to_all x2, waiting for transfers between devices, dispatch(): lax.all_to_all(x, 'expert', 0, 0, tiled=True, axis_index_groups=same_z)  41.2 us
    ppermute x3, waiting for transfers between devices, local(): lax.ppermute(blocks[d], 'dp', [(i, (i + d) % planes) for i in range(plane...  21 us
    ppermute x1, waiting for transfers between devices, local(): far_moved = lax.ppermute(moved, 'expert', other_z)  18.5 us
    all_gather x1, waiting for transfers between devices, local(): hidden = lax.all_gather(hidden, 'dp')  16.3 us
    all_to_all x2, starting transfers between devices, dispatch(): lax.all_to_all(x, 'expert', 0, 0, tiled=True, axis_index_groups=same_z)  14.9 us
    pallas_call x1, Pallas kernels, grad_of(): pl.pallas_call(grad_kernel, grid_spec=pltpu.PrefetchScalarGridSpec(num_sc...  11.3 us
    pallas_call x1, Pallas kernels, hidden_main(): pl.pallas_call(hidden_main_kernel, grid=(hid // block,), in_specs=[pl.Blo...  8.85 us
  transfers between devices with their start and end apart: 15, of which 8 were waited for; matrix products, arithmetic and copies ran while one was open for 3% of the time, Pallas kernels for 10%

profile of v6, /device:TPU:64, one launch (start us, length us, event | category | flops | bytes accessed | tf_op | source)
XLA Modules:
  0.0 262.5 jit_solution(1016453108842705965)
XLA Ops:
  6.5 1.9 collective-permute-start.16
  8.5 0.7 convert_bitcast_fusion
  9.1 0.8 reduce-precision_subtract_fusion
  9.9 0.2 collective-permute-start.17
  10.1 0.8 copy.7
  10.9 0.1 eq.20
  11.0 0.1 convert_reduce_fusion
  11.2 0.7 iota_reduce_fusion
  12.6 0.6 pad_add_fusion.place_ref
  13.2 3.1 %split_raw.1 = (bf16[144,896]{1,0:T(8,128)(2,1)}, bf16[144,896]{1,0:T(8,128)(2,1)}, bf16[144,896]{1,0:T(8,128)(2,1)}, bf16[144,896]{1,0:T(8,128)(2,1)}) custom-call(s32[4]{0:T(128)} %pad_add_fusion.place_ref, bf16[128,3584]{1,0:T(8,128)(2,1)} %q3_ref.1, bf16[128,3584]{1,0:T(8,128)(2,1)} %q3_ref.1, bf16[128,3584]{1,0:T(8,128)(2,1)} %q3_ref.1, ...), custom_call_target="tpu_custom_call" | custom-call | tf_op jit(solution)/shard_map/split_raw/pallas_call | solution.py:60
  16.3 3.9 %collective-permute-done.17.b_meta = f32[8,128]{1,0:T(8,128)S(1)} collective-permute-done((f32[8,128]{1,0:T(8,128)S(1)}, f32[8,128]{1,0:T(8,128)S(1)}, u32[]{:S(2)}, u32[]{:S(2)}) %collective-permute-start.17) | collective-permute-done | bytes 4128 | tf_op jit(solution)/shard_map/ppermute | solution.py:452
  20.2 0.6 copy-done.7
  20.8 0.3 copy-done.2
  21.1 5.2 %pack_tokens.1 = bf16[32,8,8960]{2,1,0:T(8,128)(2,1)} custom-call(s32[4]{0:T(128)} %pad_add_fusion.place_ref, f32[8,128]{1,0:T(8,128)} %copy-done.6, f32[8,128]{1,0:T(8,128)} %copy-done.7, bf16[128,3584]{1,0:T(8,128)(2,1)} %a_ref.1, bf16[128,3584]{1,0:T(8,128)(2,1)} %copy-done.2), custom_call_target="tpu_custom_call" | custom-call | tf_op jit(solution)/shard_map/pack_tokens/pallas_call | solution.py:118
  26.3 7.6 %all-to-all-start = ((bf16[32,8,8960]{2,1,0:T(8,128)(2,1)}), bf16[32,8,8960]{2,1,0:T(8,128)(2,1)}, u32[]{:S(2)}, u32[]{:S(2)}) async-start(bf16[32,8,8960]{2,1,0:T(8,128)(2,1)} %pack_tokens.1), calls=%async_computation | async-start | bytes 9175040 | tf_op jit(solution)/shard_map/all_to_all | solution.py:446
  33.9 2.0 collective-permute-start.18
  35.9 3.6 %collective-permute-start.19 = (bf16[144,896]{1,0:T(8,128)(2,1)S(1)}, bf16[144,896]{1,0:T(8,128)(2,1)S(1)}, u32[]{:S(2)}, u32[]{:S(2)}) collective-permute-start(bf16[144,896]{1,0:T(8,128)(2,1)S(1)} %copy-done.10), channel_id=1, source_target_pairs={{0,1},{1,2},{2,3},{3,0},{4,5},{5,6},{6,7},{7,4},{8,9},{9,10},{10,1... | collective-permute-start | bytes 774152 | tf_op jit(solution)/shard_map/ppermute | solution.py:460
  39.5 1.0 collective-permute-start.20
  40.5 2.8 %collective-permute-start.21 = (bf16[144,896]{1,0:T(8,128)(2,1)S(1)}, bf16[144,896]{1,0:T(8,128)(2,1)S(1)}, u32[]{:S(2)}, u32[]{:S(2)}) collective-permute-start(bf16[144,896]{1,0:T(8,128)(2,1)S(1)} %copy-done.8), channel_id=1, source_target_pairs={{0,3},{1,0},{2,1},{3,2},{4,7},{5,4},{6,5},{7,6},{8,11},{9,8},{10,9... | collective-permute-start | bytes 774152 | tf_op jit(solution)/shard_map/ppermute | solution.py:460
  43.4 4.6 %collective-permute-done.18.far_own_ref = bf16[144,896]{1,0:T(8,128)(2,1)S(1)} collective-permute-done((bf16[144,896]{1,0:T(8,128)(2,1)S(1)}, bf16[144,896]{1,0:T(8,128)(2,1)S(1)}, u32[]{:S(2)}, u32[]{:S(2)}) %collective-permute-start.18) | collective-permute-done | bytes 258080 | tf_op jit(solution)/shard_map/ppermute | solution.py:461
  48.0 9.2 %collective-permute-done.19 = bf16[144,896]{1,0:T(8,128)(2,1)S(1)} collective-permute-done((bf16[144,896]{1,0:T(8,128)(2,1)S(1)}, bf16[144,896]{1,0:T(8,128)(2,1)S(1)}, u32[]{:S(2)}, u32[]{:S(2)}) %collective-permute-start.19) | collective-permute-done | bytes 258080 | tf_op jit(solution)/shard_map/ppermute | solution.py:460
  57.2 11.8 %collective-permute-done.20 = bf16[144,896]{1,0:T(8,128)(2,1)S(1)} collective-permute-done((bf16[144,896]{1,0:T(8,128)(2,1)S(1)}, bf16[144,896]{1,0:T(8,128)(2,1)S(1)}, u32[]{:S(2)}, u32[]{:S(2)}) %collective-permute-start.20) | collective-permute-done | bytes 258080 | tf_op jit(solution)/shard_map/ppermute | solution.py:460
  69.0 0.1 pad_maximum_fusion.4.moved_ref
  69.1 0.1 collective-permute-start.22
  69.2 18.5 %collective-permute-done.22.far_moved_ref = bf16[3,144,896]{2,1,0:T(8,128)(2,1)S(1)} collective-permute-done((bf16[3,144,896]{2,1,0:T(8,128)(2,1)S(1)}, bf16[3,144,896]{2,1,0:T(8,128)(2,1)S(1)}, u32[]{:S(2)}, u32[]{:S(2)}) %collective-permute-start.22) | collective-permute-done | bytes 774176 | tf_op jit(solution)/shard_map/ppermute | solution.py:464
  87.6 0.9 copy-done.3
  88.5 7.4 %pack_scaled.1 = bf16[32,96,896]{2,1,0:T(8,128)(2,1)} custom-call(s32[4]{0:T(128)} %pad_add_fusion.place_ref, bf16[144,896]{1,0:T(8,128)(2,1)} %get-tuple-element.42.own_ref, bf16[3,144,896]{2,1,0:T(8,128)(2,1)} %copy-done.1, bf16[144,896]{1,0:T(8,128)(2,1)} %copy-done.5, bf16[3,144,896]{2,1,0:T(8,128)(2,1)} %copy-done.3), custom_call_target="tpu_custom_call" | custom-call | tf_op jit(solution)/shard_map/pack_scaled/pallas_call | solution.py:177
  96.0 7.3 %all-to-all-start.1 = ((bf16[32,96,896]{2,1,0:T(8,128)(2,1)}), bf16[32,96,896]{2,1,0:T(8,128)(2,1)}, u32[]{:S(2)}, u32[]{:S(2)}) async-start(bf16[32,96,896]{2,1,0:T(8,128)(2,1)} %pack_scaled.1), calls=%async_computation.1 | async-start | bytes 11010048 | tf_op jit(solution)/shard_map/all_to_all | solution.py:446
  103.3 0.0 all-gather.3.cloned.1.call-start
  103.3 8.8 %hidden_main.1 = bf16[384,1024]{1,0:T(8,128)(2,1)} custom-call(bf16[32,8,8960]{2,1,0:T(8,128)(2,1)} %all-to-all-done.x_ref, bf16[3584,1024]{1,0:T(8,128)(2,1)} %bitcast.17), custom_call_target="tpu_custom_call" | custom-call | tf_op jit(solution)/shard_map/hidden_main/pallas_call | solution.py:234
  112.2 0.0 all-gather.3.cloned.1.call-update
  112.2 1.6 slice.35.near_ref
  113.8 0.5 collective-permute-start.23
  115.7 2.3 collective-permute-done.23.far_ref
  118.0 5.9 %hidden_extra.1 = bf16[384,1024]{1,0:T(8,128)(2,1)S(1)} custom-call(s32[4]{0:T(128)} %pad_add_fusion.place_ref, bf16[32,8,3584]{2,1,0:T(8,128)(2,1)} %copy-done, bf16[32,8,3584]{2,1,0:T(8,128)(2,1)} %collective-permute-done.23.far_ref, bf16[3584,1024]{1,0:T(8,128)(2,1)} %bitcast.18), custom_call_target="tpu_custom_call" | custom-call | tf_op jit(solution)/shard_map/hidden_extra/pallas_call | solution.py:288
  123.9 6.7 %conditional.1 = (bf16[384,1024]{1,0:T(8,128)(2,1)}, bf16[384,1024]{1,0:T(8,128)(2,1)S(1)}, bf16[384,1024]{1,0:T(8,128)(2,1)}) conditional(s32[]{:T(128)} %clamp.3, bf16[384,1024]{1,0:T(8,128)(2,1)S(1)} %hidden_extra.1, bf16[384,1024]{1,0:T(8,128)(2,1)S(1)} %hidden_extra.1, ...), branch_computations={%region_2.3_spmd, %region_3.4_spmd, %region_4.5_spmd, %region_5.6_... | conditional | flops 1572864 | bytes 12583096 | solution.py:496
  123.9 1.6 collective-permute-start.12
  125.5 1.6 collective-permute-start.14
  127.0 1.0 slice.42
  128.1 0.7 collective-permute-start.13
  128.8 1.0 slice.43
  129.8 0.7 collective-permute-start.15
  130.5 0.1 pad_maximum_fusion.3
  130.6 41.2 %all-to-all-done.1.s_ref.sx_ref = bf16[32,96,896]{2,1,0:T(8,128)(2,1)} async-done(((bf16[32,96,896]{2,1,0:T(8,128)(2,1)}), bf16[32,96,896]{2,1,0:T(8,128)(2,1)}, u32[]{:S(2)}, u32[]{:S(2)}) %all-to-all-start.1) | async-done | bytes 5505056 | tf_op jit(solution)/shard_map/all_to_all | solution.py:446
  171.7 16.3 %all-gather.3.cloned.1.call-done = bf16[1536,1024]{1,0:T(8,128)(2,1)} async-done(((bf16[384,1024]{1,0:T(8,128)(2,1)}), bf16[1536,1024]{1,0:T(8,128)(2,1)}) %all-gather.3.cloned.1.call-update) | async-done | bytes 3145744 | tf_op jit(solution)/shard_map/all_gather | solution.py:472
  188.0 11.3 %grad_of.1 = bf16[1024,896]{1,0:T(8,128)(2,1)} custom-call(s32[4]{0:T(128)} %pad_add_fusion.place_ref, bf16[4,2,192,1024]{3,2,1,0:T(8,128)(2,1)} %bitcast.19, bf16[4,2,192,1024]{3,2,1,0:T(8,128)(2,1)} %bitcast.20, bf16[2,192,1024]{2,1,0:T(8,128)(2,1)S(1)} %bitcast.22, bf16[2,192,1024]{2,1,0:T(8,128)(2,1)} %bitcast.12.x1, bf16[2,192,1024]{2,1,0:T(8,128)(2,1)S(1)} %bitcast.23, ...), custom_call_target="tpu_custom_call" | custom-call | tf_op jit(solution)/shard_map/grad_of/pallas_call | solution.py:377
  199.3 50.4 %all_to_all.15.in_ref = bf16[4,256,896]{2,1,0:T(8,128)(2,1)} all-to-all(bf16[4,256,896]{2,1,0:T(8,128)(2,1)} %bitcast.21), channel_id=1, replica_groups=mesh['expert'=64,'dp'=4] {'dp'}, dimensions={0} | all-to-all | bytes 3670016 | tf_op jit(solution)/shard_map/all_to_all | solution.py:502
  249.7 5.9 %join.1 = f32[1,256,3584]{2,1,0:T(8,128)} custom-call(bf16[4,256,896]{2,1,0:T(8,128)(2,1)} %all_to_all.15.in_ref), custom_call_target="tpu_custom_call" | custom-call | tf_op jit(solution)/shard_map/join/pallas_call | solution.py:400
  (27 shorter events, 0.1 us)
Async XLA Ops:
  6.5 13.7 %collective-permute-start.16 = (bf16[128,3584]{1,0:T(8,128)(2,1)}, bf16[128,3584]{1,0:T(8,128)(2,1)S(1)}, u32[]{:S(2)}, u32[]{:S(2)}) collective-permute-start(bf16[128,3584]{1,0:T(8,128)(2,1)} %a_ref.1), channel_id=1, source_target_pairs={{0,32},{1,33},{2,34},{3,35},{4,39},{5,36},{6,37},{7,38},{8,40},{9,... | collective-permute-start | bytes 2752520 | tf_op jit(solution)/shard_map/ppermute | solution.py:451
  9.9 3.3 %copy-start.6 = (f32[8,128]{1,0:T(8,128)}, f32[8,128]{1,0:T(8,128)S(1)}, u32[]{:S(2)}) copy-start(f32[8,128]{1,0:T(8,128)S(1)} %concatenate.15.meta_ref.a_meta) | copy-start | bytes 12292
  9.9 10.3 %collective-permute-start.17 = (f32[8,128]{1,0:T(8,128)S(1)}, f32[8,128]{1,0:T(8,128)S(1)}, u32[]{:S(2)}, u32[]{:S(2)}) collective-permute-start(f32[8,128]{1,0:T(8,128)S(1)} %concatenate.15.meta_ref.a_meta), channel_id=1, source_target_pairs={{0,32},{1,33},{2,34},{3,35},{4,39},{5,36},{6,37},{7,38},{8,40},{9,... | collective-permute-start | bytes 12296 | tf_op jit(solution)/shard_map/ppermute | solution.py:452
  20.2 0.6 copy-start.7
  20.2 0.9 copy-start.2
  26.3 7.6 %copy-start.4 = (bf16[144,896]{1,0:T(8,128)(2,1)S(1)}, bf16[144,896]{1,0:T(8,128)(2,1)}, u32[]{:S(2)}) copy-start(bf16[144,896]{1,0:T(8,128)(2,1)} %get-tuple-element.42.own_ref) | copy-start | bytes 774148
  26.3 9.6 %copy-start.10 = (bf16[144,896]{1,0:T(8,128)(2,1)S(1)}, bf16[144,896]{1,0:T(8,128)(2,1)}, u32[]{:S(2)}) copy-start(bf16[144,896]{1,0:T(8,128)(2,1)} %get-tuple-element.43) | copy-start | bytes 774148
  26.3 13.2 %copy-start.9 = (bf16[144,896]{1,0:T(8,128)(2,1)S(1)}, bf16[144,896]{1,0:T(8,128)(2,1)}, u32[]{:S(2)}) copy-start(bf16[144,896]{1,0:T(8,128)(2,1)} %get-tuple-element.44) | copy-start | bytes 774148
  26.3 14.2 %copy-start.8 = (bf16[144,896]{1,0:T(8,128)(2,1)S(1)}, bf16[144,896]{1,0:T(8,128)(2,1)}, u32[]{:S(2)}) copy-start(bf16[144,896]{1,0:T(8,128)(2,1)} %get-tuple-element.45) | copy-start | bytes 774148
  26.3 69.6 %all-to-all-start = ((bf16[32,8,8960]{2,1,0:T(8,128)(2,1)}), bf16[32,8,8960]{2,1,0:T(8,128)(2,1)}, u32[]{:S(2)}, u32[]{:S(2)}) async-start(bf16[32,8,8960]{2,1,0:T(8,128)(2,1)} %pack_tokens.1), calls=%async_computation | async-start | bytes 9175040 | tf_op jit(solution)/shard_map/all_to_all | solution.py:446
  33.9 14.1 %collective-permute-start.18 = (bf16[144,896]{1,0:T(8,128)(2,1)S(1)}, bf16[144,896]{1,0:T(8,128)(2,1)S(1)}, u32[]{:S(2)}, u32[]{:S(2)}) collective-permute-start(bf16[144,896]{1,0:T(8,128)(2,1)S(1)} %copy-done.4), channel_id=1, source_target_pairs={{0,32},{4,36},{8,40},{12,44},{16,48},{20,52},{24,56},{28,60},{32,0... | collective-permute-start | bytes 774152 | tf_op jit(solution)/shard_map/ppermute | solution.py:461
  35.9 21.3 %collective-permute-start.19 = (bf16[144,896]{1,0:T(8,128)(2,1)S(1)}, bf16[144,896]{1,0:T(8,128)(2,1)S(1)}, u32[]{:S(2)}, u32[]{:S(2)}) collective-permute-start(bf16[144,896]{1,0:T(8,128)(2,1)S(1)} %copy-done.10), channel_id=1, source_target_pairs={{0,1},{1,2},{2,3},{3,0},{4,5},{5,6},{6,7},{7,4},{8,9},{9,10},{10,1... | collective-permute-start | bytes 774152 | tf_op jit(solution)/shard_map/ppermute | solution.py:460
  39.5 29.5 %collective-permute-start.20 = (bf16[144,896]{1,0:T(8,128)(2,1)S(1)}, bf16[144,896]{1,0:T(8,128)(2,1)S(1)}, u32[]{:S(2)}, u32[]{:S(2)}) collective-permute-start(bf16[144,896]{1,0:T(8,128)(2,1)S(1)} %copy-done.9), channel_id=1, source_target_pairs={{0,2},{1,3},{2,0},{3,1},{4,6},{5,7},{6,4},{7,5},{8,10},{9,11},{10,... | collective-permute-start | bytes 774152 | tf_op jit(solution)/shard_map/ppermute | solution.py:460
  40.5 28.4 %collective-permute-start.21 = (bf16[144,896]{1,0:T(8,128)(2,1)S(1)}, bf16[144,896]{1,0:T(8,128)(2,1)S(1)}, u32[]{:S(2)}, u32[]{:S(2)}) collective-permute-start(bf16[144,896]{1,0:T(8,128)(2,1)S(1)} %copy-done.8), channel_id=1, source_target_pairs={{0,3},{1,0},{2,1},{3,2},{4,7},{5,4},{6,5},{7,6},{8,11},{9,8},{10,9... | collective-permute-start | bytes 774152 | tf_op jit(solution)/shard_map/ppermute | solution.py:460
  48.0 39.6 %copy-start.5 = (bf16[144,896]{1,0:T(8,128)(2,1)}, bf16[144,896]{1,0:T(8,128)(2,1)S(1)}, u32[]{:S(2)}) copy-start(bf16[144,896]{1,0:T(8,128)(2,1)S(1)} %collective-permute-done.18.far_own_ref) | copy-start | bytes 774148
  69.1 18.6 %copy-start.1 = (bf16[3,144,896]{2,1,0:T(8,128)(2,1)}, bf16[3,144,896]{2,1,0:T(8,128)(2,1)S(1)}, u32[]{:S(2)}) copy-start(bf16[3,144,896]{2,1,0:T(8,128)(2,1)S(1)} %pad_maximum_fusion.4.moved_ref) | copy-start | bytes 2322436
  69.1 18.6 %collective-permute-start.22 = (bf16[3,144,896]{2,1,0:T(8,128)(2,1)S(1)}, bf16[3,144,896]{2,1,0:T(8,128)(2,1)S(1)}, u32[]{:S(2)}, u32[]{:S(2)}) collective-permute-start(bf16[3,144,896]{2,1,0:T(8,128)(2,1)S(1)} %pad_maximum_fusion.4.moved_ref), channel_id=1, source_target_pairs={{0,32},{4,36},{8,40},{12,44},{16,48},{20,52},{24,56},{28,60},{32,0... | collective-permute-start | bytes 2322440 | tf_op jit(solution)/shard_map/ppermute | solution.py:464
  87.6 0.9 copy-start.3
  96.0 75.8 %all-to-all-start.1 = ((bf16[32,96,896]{2,1,0:T(8,128)(2,1)}), bf16[32,96,896]{2,1,0:T(8,128)(2,1)}, u32[]{:S(2)}, u32[]{:S(2)}) async-start(bf16[32,96,896]{2,1,0:T(8,128)(2,1)} %pack_scaled.1), calls=%async_computation.1 | async-start | bytes 11010048 | tf_op jit(solution)/shard_map/all_to_all | solution.py:446
  103.3 84.7 %all-gather.3.cloned.1.call-start = ((), (), s32[]{:S(2)}) async-start(), calls=%async_computation.3 | async-start | bytes 3932160 | tf_op jit(solution)/shard_map/all_gather | solution.py:472
  113.8 4.2 %copy-start = (bf16[32,8,3584]{2,1,0:T(8,128)(2,1)}, bf16[32,8,3584]{2,1,0:T(8,128)(2,1)S(1)}, u32[]{:S(2)}) copy-start(bf16[32,8,3584]{2,1,0:T(8,128)(2,1)S(1)} %slice.35.near_ref) | copy-start | bytes 5505028
  113.8 4.2 %collective-permute-start.23 = (bf16[32,8,3584]{2,1,0:T(8,128)(2,1)S(1)}, bf16[32,8,3584]{2,1,0:T(8,128)(2,1)}, u32[]{:S(2)}, u32[]{:S(2)}) collective-permute-start(bf16[32,8,3584]{2,1,0:T(8,128)(2,1)S(1)} %slice.35.near_ref), channel_id=1, source_target_pairs={{0,4},{4,0},{8,12},{12,8},{16,20},{20,16},{24,28},{28,24},{32,36},... | collective-permute-start | bytes 5505032 | tf_op jit(solution)/shard_map/ppermute | solution.py:474
  123.9 3.1 %collective-permute-start.12 = (bf16[384,1024]{1,0:T(8,128)(2,1)S(1)}, bf16[384,1024]{1,0:T(8,128)(2,1)}, u32[]{:S(2)}, u32[]{:S(2)}) collective-permute-start(bf16[384,1024]{1,0:T(8,128)(2,1)S(1)} %param.3), channel_id=1, source_target_pairs={{36,37},{37,38},{38,39},{39,36},{44,45},{45,46},{46,47},{47,44},{5... | collective-permute-start | bytes 2359304 | tf_op jit(solution)/shard_map/cond/branch_3_fun/ppermute | solution.py:486
  125.5 3.3 %collective-permute-start.14 = (bf16[384,1024]{1,0:T(8,128)(2,1)S(1)}, bf16[384,1024]{1,0:T(8,128)(2,1)}, u32[]{:S(2)}, u32[]{:S(2)}) collective-permute-start(bf16[384,1024]{1,0:T(8,128)(2,1)S(1)} %param.3), channel_id=1, source_target_pairs={{36,39},{37,36},{38,37},{39,38},{44,47},{45,44},{46,45},{47,46},{5... | collective-permute-start | bytes 2359304 | tf_op jit(solution)/shard_map/cond/branch_3_fun/ppermute | solution.py:486
  128.1 2.4 collective-permute-start.13
  129.8 0.7 collective-permute-start.15
Sparse Core Ops, SparseCore 0:
  112.3 75.6 all-gather.2
